TPU v7x, 128 devices: a whole 4x4x4 slice. The times are simulated.
128 devices in a mesh: col: 16 (over x, z_hi, core), row: 8 (over z_lo, y).
Axes of the slice: x: 4, y: 4, z: 4 (z_hi: 2, z_lo: 2; z = z_hi * 2 + z_lo), core: 2. Of those that a mesh axis runs over, the one named last changes fastest.
Arguments:
- noise_bits: int32 [2, 8192, 8192], P(None, 'col', 'row'), may hold values from 0 to 4095
- eigenvalues: float32 [8192, 8192], P('col', 'row'), may hold values from 0.05 to 5
Outputs:
- field: float32 [2, 8192, 8192], P(None, ('col', 'row'))
All inputs are finite; a program needn't handle non-finite values.
Results may differ from a plain program's by a relative error of at most 0.000098.
Values sent between devices are 32-bit elements; how exact they have to be, the bound alone decides.
No kernel may reach another device: no remote copies, remote signals or barrier semaphores. Data moves between devices by JAX's collectives and lax.ppermute only.
A program may use at most 128 MiB of HBM per device.

v0:
```python
import functools
import math

import jax
import jax.numpy as jnp
import ml_dtypes
import numpy as np
from jax import lax
from jax.experimental import pallas as pl
from jax.experimental.pallas import tpu as pltpu
from jax.sharding import Mesh, PartitionSpec as P

N = 8192
M = 8192
LOCAL = 512
WIDTH = 1024
BLOCK = 256

AXES = ("x", "zh", "core", "zl", "y")
SIZES = (4, 2, 2, 2, 4)

F32 = jnp.float32
BF16 = jnp.bfloat16


def halves(table):
    high = table.astype(np.float32).astype(ml_dtypes.bfloat16)
    low = (table - high.astype(np.float64)).astype(np.float32).astype(ml_dtypes.bfloat16)
    return high, low


def split(value):
    high = value.astype(BF16)
    low = (value - high.astype(F32)).astype(BF16)
    return high, low


def complex_table(product, length):
    angle = 2.0 * np.pi * (product % length) / length
    cosine, sine = np.cos(angle), np.sin(angle)
    return np.concatenate(
        [np.concatenate([cosine, sine], 1), np.concatenate([-sine, cosine], 1)], 0
    )


def column_table():
    steps = np.arange(LOCAL)
    return halves(complex_table(np.outer(steps, steps), LOCAL))


def row_tables():
    place = 8 * (4 * np.arange(2)[None, None, :] + np.arange(4)[None, :, None]) + np.arange(8)[:, None, None]
    angle = 2.0 * np.pi * (np.arange(64)[:, None] * place.reshape(1, 64) % 64) / 64
    cosine, sine = np.cos(angle), np.sin(angle)
    real_part = np.stack([cosine, sine], -1).reshape(64, 128)
    imag_part = np.stack([-sine, cosine], -1).reshape(64, 128)
    first = halves(np.concatenate([real_part, imag_part], 0))
    angle = 2.0 * np.pi * (np.outer(np.arange(128), np.arange(128)) % M) / M
    twist = (np.cos(angle).astype(np.float32), (-np.sin(angle)).astype(np.float32))
    second = halves(complex_table(np.outer(np.arange(64), np.arange(128)), 64))
    return first, twist, second


def sine_polynomials():
    nodes = 0.25 * np.cos(np.pi * (np.arange(400) + 0.5) / 800)
    square = np.polynomial.chebyshev.Chebyshev.fit(
        nodes**2, np.sin(2 * np.pi * nodes) / nodes, 4, domain=[0, 1 / 16]
    ).convert(kind=np.polynomial.Polynomial, domain=[-1, 1], window=[-1, 1])
    cosine = np.polynomial.chebyshev.Chebyshev.fit(
        nodes**2, np.cos(2 * np.pi * nodes), 5, domain=[0, 1 / 16]
    ).convert(kind=np.polynomial.Polynomial, domain=[-1, 1], window=[-1, 1])
    return [float(c) for c in square.coef], [float(c) for c in cosine.coef]


SINE, COSINE = sine_polynomials()


def horner(coefficients, value):
    total = jnp.full_like(value, coefficients[-1])
    for coefficient in coefficients[-2::-1]:
        total = total * value + coefficient
    return total


def dot(a, b):
    return jnp.dot(a, b, preferred_element_type=F32)


def dot_nt(a, b):
    return lax.dot_general(a, b, (((1,), (1,)), ((), ())), preferred_element_type=F32)


def draw(bits_0, bits_1, eigen):
    uniform = (bits_0.astype(F32) + 0.5) * 2.0**-12
    radius = jnp.sqrt(jnp.log(uniform) * eigen * (-2.0 / (N * M)))
    past = (bits_1.astype(F32) - 2047.5) * 2.0**-12
    h = jnp.abs(past) - 0.25
    square = h * h
    value_re = radius * (h * horner(SINE, square))
    value_im = jnp.where(past > 0, -radius, radius) * horner(COSINE, square)
    return value_re, value_im


def column_kernel(noise, eigen, high, low, twist, out, data_high, data_low):
    value_re, value_im = draw(noise[0], noise[1], eigen[...])
    for part, value in enumerate((value_re, value_im)):
        data_high[LOCAL * part : LOCAL * (part + 1), :], data_low[LOCAL * part : LOCAL * (part + 1), :] = split(value)

    def rows(place, carry):
        zl, y = place // 4, place % 4
        parts = []
        for part in range(2):
            at = pl.ds(pl.multiple_of(LOCAL * part + 64 * place, 64), 64)
            table = high[at, :]
            parts.append(dot(table, data_high[...]) + dot(low[at, :], data_high[...]) + dot(table, data_low[...]))
        at = pl.ds(pl.multiple_of(64 * place, 64), 64)
        turn_re, turn_im = twist[0, at, :], twist[1, at, :]
        for a in range(BLOCK // 128):
            real, imag = (p[:, 128 * a : 128 * (a + 1)] for p in parts)
            out[a, zl, y, 0] = real * turn_re - imag * turn_im
            out[a, zl, y, 1] = real * turn_im + imag * turn_re
        return carry

    lax.fori_loop(0, 8, rows, 0)


def column_transform(noise, eigen, twist):
    high, low = column_table()
    whole = lambda shape: pl.BlockSpec(shape, lambda i: (0,) * len(shape))
    return pl.pallas_call(
        column_kernel,
        grid=(WIDTH // BLOCK,),
        in_specs=[
            pl.BlockSpec((2, LOCAL, BLOCK), lambda i: (0, 0, i)),
            pl.BlockSpec((LOCAL, BLOCK), lambda i: (0, i)),
            whole((2 * LOCAL, 2 * LOCAL)),
            whole((2 * LOCAL, 2 * LOCAL)),
            whole((2, LOCAL, 128)),
        ],
        out_specs=pl.BlockSpec((BLOCK // 128, 2, 4, 2, 64, 128), lambda i: (i, 0, 0, 0, 0, 0)),
        out_shape=jax.ShapeDtypeStruct((8, 2, 4, 2, 64, 128), F32),
        scratch_shapes=[pltpu.VMEM((2 * LOCAL, BLOCK), BF16), pltpu.VMEM((2 * LOCAL, BLOCK), BF16)],
        compiler_params=pltpu.CompilerParams(vmem_limit_bytes=40 * 2**20),
        cost_estimate=pl.CostEstimate(flops=7 * 10**9, bytes_accessed=14 * 2**20, transcendentals=0),
    )(noise, eigen, jnp.asarray(high), jnp.asarray(low), twist)


def add(a, b):
    return a[0] + b[0], a[1] + b[1]


def sub(a, b):
    return a[0] - b[0], a[1] - b[1]


def turn_back(a):
    return a[1], -a[0]


ROOT = math.sqrt(0.5)


def dft_4(a, b, c, d):
    even, odd = add(a, c), add(b, d)
    less, turned = sub(a, c), turn_back(sub(b, d))
    return add(even, odd), add(less, turned), sub(even, odd), sub(less, turned)


def dft_8(v):
    even = dft_4(v[0], v[2], v[4], v[6])
    odd = dft_4(v[1], v[3], v[5], v[7])
    spun = [
        odd[0],
        ((odd[1][0] + odd[1][1]) * ROOT, (odd[1][1] - odd[1][0]) * ROOT),
        turn_back(odd[2]),
        ((odd[3][1] - odd[3][0]) * ROOT, (odd[3][0] + odd[3][1]) * -ROOT),
    ]
    return [add(e, o) for e, o in zip(even, spun)] + [sub(e, o) for e, o in zip(even, spun)]


def middle_kernel(scalars, mine, other, out):
    sign = scalars[16]
    for row in range(0, 64, 8):
        at = pl.ds(row, 8)
        values = []
        for e in range(8):
            zh, xl, xh = e >> 2, e >> 1 & 1, e & 1
            x = 2 * xh + xl
            re = mine[x, zh, 0, 0, 0, at, :] * sign + other[x, zh, 0, 0, 0, at, :]
            im = mine[x, zh, 0, 0, 1, at, :] * sign + other[x, zh, 0, 0, 1, at, :]
            c, s = scalars[2 * e], scalars[2 * e + 1]
            values.append((re * c - im * s, re * s + im * c))
        for k, (re, im) in enumerate(dft_8(values)):
            zh, xl, xh = k & 1, k >> 1 & 1, k >> 2
            x = 2 * xh + xl
            out[x, zh, 0, 0, 0, at, :] = re
            out[x, zh, 0, 0, 1, at, :] = im


def middle(scalars, mine, other):
    block = (4, 2, 1, 1, 2, 64, 128)
    return pl.pallas_call(
        middle_kernel,
        grid=(2, 4),
        in_specs=[
            pl.BlockSpec(memory_space=pltpu.SMEM),
            pl.BlockSpec(block, lambda i, j: (0, 0, i, j, 0, 0, 0)),
            pl.BlockSpec(block, lambda i, j: (0, 0, i, j, 0, 0, 0)),
        ],
        out_specs=pl.BlockSpec(block, lambda i, j: (0, 0, j, i, 0, 0, 0)),
        out_shape=jax.ShapeDtypeStruct((4, 2, 4, 2, 2, 64, 128), F32),
        cost_estimate=pl.CostEstimate(flops=10**7, bytes_accessed=12 * 2**20, transcendentals=0),
    )(scalars, mine, other)


def row_kernel(x, first_high, first_low, twist, second_high, second_low, out, turned):
    for t in range(8):
        high, low = split(x[:, t, :])
        table = first_high[...]
        step = dot(table, high) + dot(first_low[...], high) + dot(table, low)
        both = []
        for v in range(2):
            re, im = twist[0, 64 * v : 64 * (v + 1), :], twist[1, 64 * v : 64 * (v + 1), :]
            both.append(jnp.concatenate([step[:64] * re - step[64:] * im, step[:64] * im + step[64:] * re], 1))
        high, low = split(jnp.concatenate(both, 0))
        table = second_high[...]
        last = dot_nt(table, high) + dot_nt(second_low[...], high) + dot_nt(table, low)
        turned[pl.ds(t, 128, stride=8), :] = last
    for part in range(2):
        for u in range(64):
            out[part, :, 128 * u : 128 * (u + 1)] = turned[8 * (64 * part + u) : 8 * (64 * part + u) + 8, :]


def row_transform(x):
    first, twist, second = row_tables()
    whole = lambda shape: pl.BlockSpec(shape, lambda i: (0,) * len(shape))
    return pl.pallas_call(
        row_kernel,
        grid=(8,),
        in_specs=[
            pl.BlockSpec((128, 8, 128), lambda i: (0, i, 0)),
            whole((128, 128)),
            whole((128, 128)),
            whole((2, 128, 128)),
            whole((128, 256)),
            whole((128, 256)),
        ],
        out_specs=pl.BlockSpec((2, 8, M), lambda i: (0, i, 0)),
        out_shape=jax.ShapeDtypeStruct((2, 64, M), F32),
        scratch_shapes=[pltpu.VMEM((1024, 128), F32)],
        compiler_params=pltpu.CompilerParams(vmem_limit_bytes=32 * 2**20),
        cost_estimate=pl.CostEstimate(flops=3 * 10**9, bytes_accessed=9 * 2**20, transcendentals=0),
    )(x, *(jnp.asarray(t) for t in first), jnp.stack([jnp.asarray(t) for t in twist]), *(jnp.asarray(t) for t in second))


def on_device(noise, eigen):
    xh, xl = lax.axis_index("x") // 2, lax.axis_index("x") % 2
    zh, core = lax.axis_index("zh"), lax.axis_index("core")
    anchor = 8 * core + 4 * zh + 2 * xl + xh
    angle = (anchor * jnp.arange(LOCAL, dtype=jnp.int32) % N).astype(F32) * (-2.0 * math.pi / N)
    twist = jnp.broadcast_to(jnp.stack([jnp.cos(angle), jnp.sin(angle)])[:, :, None], (2, LOCAL, 128))
    angle = (core * jnp.arange(8, dtype=jnp.int32)).astype(F32) * (-2.0 * math.pi / 16)
    scalars = jnp.concatenate(
        [jnp.stack([jnp.cos(angle), jnp.sin(angle)], 1).reshape(16), (1 - 2 * core).astype(F32)[None]]
    )
    with jax.named_scope("columns"):
        current = column_transform(noise, eigen, twist)
    with jax.named_scope("first_exchange"):
        current = lax.all_to_all(current.reshape(16, 4, 2, 64, 128), ("x", "zh", "zl"), 0, 0, tiled=True)
        current = current.reshape(4, 2, 2, 4, 2, 64, 128)
    with jax.named_scope("core_exchange"):
        other = lax.ppermute(current, "core", [(0, 1), (1, 0)])
    with jax.named_scope("middle"):
        current = middle(scalars, current, other)
    with jax.named_scope("second_exchange"):
        current = lax.all_to_all(current.reshape(32, 2, 2, 64, 128), ("x", "zh", "y"), 0, 0, tiled=True)
        current = current.reshape(128, 64, 128)
    with jax.named_scope("rows"):
        return row_transform(current)


def solution(mesh):
    fine = Mesh(mesh.devices.reshape(SIZES), AXES)
    col, row = AXES[:3], AXES[3:]
    return jax.shard_map(
        on_device,
        mesh=fine,
        in_specs=(P(None, col, row), P(col, row)),
        out_specs=P(None, AXES, None),
        check_vma=False,
    )
```

profile of v0, /device:TPU:0, one launch (start us, length us, event | category | flops | bytes accessed | tf_op | source)
XLA Modules:
  0.0 184.4 jit_solution(11801944762679169840)
XLA Ops:
  0.0 0.1 fusion.3
  0.1 0.2 broadcast_in_dim.10.twist
  0.3 0.0 copy-start
  0.3 1.6 copy-done
  1.9 0.0 copy-start.1
  1.9 1.6 copy-done.1
  3.5 0.0 copy-start.2
  3.5 1.6 copy-done.2
  5.1 26.3 %columns.1 = f32[8,2,4,2,64,128]{5,4,3,2,1,0:T(8,128)S(1)} custom-call(s32[2,512,1024]{2,1,0:T(8,128)} %noise.1, f32[512,1024]{1,0:T(8,128)S(1)} %copy-done, bf16[1024,1024]{1,0:T(8,128)(2,1)S(1)} %copy-done.2, bf16[1024,1024]{1,0:T(8,128)(2,1)S(1)} %copy-done.1, f32[2,512,128]{2,1,0:T(8,128)S(1)} %broadcast_in_dim.10.twist), custom_call_target="tpu_custom_call" | custom-call | flops 7000000000 | bytes 14680064 | tf_op jit(solution)/shard_map/columns/pallas_call | solution.py:130
  31.3 58.6 %all_to_all.10 = f32[16,4,2,64,128]{4,3,2,1,0:T(8,128)} all-to-all(f32[16,4,2,64,128]{4,3,2,1,0:T(8,128)S(1)} %bitcast.6), channel_id=1, replica_groups=mesh['x'=4,'zh'=2,'core'=2,'zl'=2,'y'=4] {'x','zh','zl'}, dimensions={0} | all-to-all | bytes 8388608 | tf_op jit(solution)/shard_map/first_exchange/all_to_all | solution.py:269
  89.9 0.0 collective-permute-start
  90.0 0.1 copy.11
  90.1 0.1 reshape.89
  90.2 0.6 pad_maximum_fusion.2.scalars
  90.8 6.6 %collective-permute-done.other = f32[4,2,2,4,2,64,128]{6,5,4,3,2,1,0:T(8,128)} collective-permute-done((f32[4,2,2,4,2,64,128]{6,5,4,3,2,1,0:T(8,128)}, f32[4,2,2,4,2,64,128]{6,5,4,3,2,1,0:T(8,128)}, u32[]{:S(2)}, u32[]{:S(2)}) %collective-permute-start) | collective-permute-done | bytes 4194336 | tf_op jit(solution)/shard_map/core_exchange/ppermute | solution.py:272
  97.4 8.1 %middle.1 = f32[4,2,4,2,2,64,128]{6,5,4,3,2,1,0:T(8,128)} custom-call(f32[17]{0:T(128)} %pad_maximum_fusion.2.scalars, f32[4,2,2,4,2,64,128]{6,5,4,3,2,1,0:T(8,128)} %bitcast.2.mine, f32[4,2,2,4,2,64,128]{6,5,4,3,2,1,0:T(8,128)} %collective-permute-done.other), custom_call_target="tpu_custom_call" | custom-call | flops 10000000 | bytes 12582912 | tf_op jit(solution)/shard_map/middle/pallas_call | solution.py:202
  105.5 0.0 copy-start.3
  105.5 0.0 copy-start.4
  105.5 0.0 copy-start.5
  105.5 0.0 copy-start.6
  105.5 0.0 copy-start.7
  105.5 58.9 %all_to_all.11 = f32[32,2,2,64,128]{4,3,2,1,0:T(8,128)S(1)} all-to-all(f32[32,2,2,64,128]{4,3,2,1,0:T(8,128)} %bitcast.7), channel_id=1, replica_groups=mesh['x'=4,'zh'=2,'core'=2,'zl'=2,'y'=4] {'x','zh','y'}, dimensions={0} | all-to-all | bytes 8388608 | tf_op jit(solution)/shard_map/second_exchange/all_to_all | solution.py:276
  164.5 0.0 copy-done.3
  164.5 0.0 copy-done.4
  164.5 0.0 copy-done.5
  164.5 0.0 copy-done.6
  164.5 0.0 copy-done.7
  164.5 19.9 %rows.1 = f32[2,64,8192]{2,1,0:T(8,128)} custom-call(f32[128,64,128]{2,1,0:T(8,128)S(1)} %bitcast.5, bf16[128,128]{1,0:T(8,128)(2,1)S(1)} %copy-done.7, bf16[128,128]{1,0:T(8,128)(2,1)S(1)} %copy-done.6, f32[2,128,128]{2,1,0:T(8,128)S(1)} %copy-done.3, bf16[128,256]{1,0:T(8,128)(2,1)S(1)} %copy-done.5, bf16[128,256]{1,0:T(8,128)(2,1)S(1)} %copy-done.4), custom_call_target="tpu_custom_call" | custom-call | flops 3000000000 | bytes 9437184 | tf_op jit(solution)/shard_map/rows/pallas_call | solution.py:237
  (3 shorter events, 0.1 us)
Async XLA Ops:
  0.3 1.6 copy-start
  1.9 1.6 copy-start.1
  3.5 1.6 copy-start.2
  89.9 7.5 %collective-permute-start = (f32[4,2,2,4,2,64,128]{6,5,4,3,2,1,0:T(8,128)}, f32[4,2,2,4,2,64,128]{6,5,4,3,2,1,0:T(8,128)}, u32[]{:S(2)}, u32[]{:S(2)}) collective-permute-start(f32[4,2,2,4,2,64,128]{6,5,4,3,2,1,0:T(8,128)} %bitcast.2.mine), channel_id=1, source_target_pairs={{0,8},{8,0},{1,9},{9,1},{2,10},{10,2},{3,11},{11,3},{4,12},{12,4},... | collective-permute-start | bytes 12582920 | tf_op jit(solution)/shard_map/core_exchange/ppermute | solution.py:272
  105.5 59.0 %copy-start.3 = (f32[2,128,128]{2,1,0:T(8,128)S(1)}, f32[2,128,128]{2,1,0:T(8,128)}, u32[]{:S(2)}) copy-start(f32[2,128,128]{2,1,0:T(8,128)} %constant.88.twist) | copy-start | bytes 393220
  105.5 59.0 %copy-start.4 = (bf16[128,256]{1,0:T(8,128)(2,1)S(1)}, bf16[128,256]{1,0:T(8,128)(2,1)}, u32[]{:S(2)}) copy-start(bf16[128,256]{1,0:T(8,128)(2,1)} %constant.85.clone.second_low) | copy-start | bytes 196612
  105.5 59.0 %copy-start.5 = (bf16[128,256]{1,0:T(8,128)(2,1)S(1)}, bf16[128,256]{1,0:T(8,128)(2,1)}, u32[]{:S(2)}) copy-start(bf16[128,256]{1,0:T(8,128)(2,1)} %constant.84.clone.second_high) | copy-start | bytes 196612
  105.5 58.9 %copy-start.6 = (bf16[128,128]{1,0:T(8,128)(2,1)S(1)}, bf16[128,128]{1,0:T(8,128)(2,1)}, u32[]{:S(2)}) copy-start(bf16[128,128]{1,0:T(8,128)(2,1)} %constant.81.clone.first_low) | copy-start | bytes 98308
  105.5 58.9 %copy-start.7 = (bf16[128,128]{1,0:T(8,128)(2,1)S(1)}, bf16[128,128]{1,0:T(8,128)(2,1)}, u32[]{:S(2)}) copy-start(bf16[128,128]{1,0:T(8,128)(2,1)} %constant.80.clone.first_high) | copy-start | bytes 98308
where the time goes:
time: 185 us; the launch traced here: 184 us
  blocking collectives  118 us (64%)
  Pallas kernels  54.3 us (29%)
  waiting for transfers between devices  6.62 us (4%)
  local copies, waits for them, and re-layouts  5.15 us (3%)
    all_to_all x1, blocking collectives, on_device(): lax.all_to_all(current.reshape(32, 2, 2, 64, 128), ('x', 'zh', 'y'), 0, 0...  58.9 us
    all_to_all x1, blocking collectives, on_device(): lax.all_to_all(current.reshape(16, 4, 2, 64, 128), ('x', 'zh', 'zl'), 0,...  58.6 us
    pallas_call x1, Pallas kernels, column_transform(): pl.pallas_call(column_kernel, grid=(WIDTH // BLOCK,), in_specs=[pl.BlockS...  26.3 us
    pallas_call x1, Pallas kernels, row_transform(): pl.pallas_call(row_kernel, grid=(8,), in_specs=[pl.BlockSpec((128, 8, 128...  19.9 us
    pallas_call x1, Pallas kernels, middle(): pl.pallas_call(middle_kernel, grid=(2, 4), in_specs=[pl.BlockSpec(memory_...  8.06 us
    ppermute x1, waiting for transfers between devices, on_device(): other = lax.ppermute(current, 'core', [(0, 1), (1, 0)])  6.62 us
    unnamed x16, local copies, waits for them, and re-layouts  4.8 us
  transfers between devices with their start and end apart: 1, of which 1 were waited for; matrix products, arithmetic and copies ran while one was open for 0% of the time, Pallas kernels for 0%

commit v1 on v0

v1 whole, which is shorter than its diff:
```python
import functools
import math

import jax
import jax.numpy as jnp
import ml_dtypes
import numpy as np
from jax import lax
from jax.experimental import pallas as pl
from jax.experimental.pallas import tpu as pltpu
from jax.sharding import Mesh, PartitionSpec as P

N = 8192
M = 8192
LOCAL = 512
WIDTH = 1024
KINDS = ("x", "z", "x", "z")
CHUNKS = len(KINDS)
ROWS = 64 // CHUNKS

AXES = ("x", "zh", "core", "zl", "y")
SIZES = (4, 2, 2, 2, 4)

F32 = jnp.float32
BF16 = jnp.bfloat16


def halves(table):
    high = table.astype(np.float32).astype(ml_dtypes.bfloat16)
    low = (table - high.astype(np.float64)).astype(np.float32).astype(ml_dtypes.bfloat16)
    return high, low


def split(value):
    high = value.astype(BF16)
    low = (value - high.astype(F32)).astype(BF16)
    return high, low


def complex_table(product, length):
    angle = 2.0 * np.pi * (product % length) / length
    cosine, sine = np.cos(angle), np.sin(angle)
    return np.concatenate(
        [np.concatenate([cosine, sine], 1), np.concatenate([-sine, cosine], 1)], 0
    )


def column_tables():
    steps = np.arange(LOCAL)
    table = complex_table(np.outer(steps, steps), LOCAL)
    table = table.reshape(2, 2, 4, CHUNKS, ROWS, 2 * LOCAL).transpose(3, 1, 0, 2, 4, 5)
    return np.stack(halves(table.reshape(CHUNKS, 16 * ROWS, 2 * LOCAL)))


def row_tables(kind):
    x, zh, y, first_of = np.arange(4), np.arange(2), np.arange(4), []
    zl = np.arange(2)
    for at_x in range(4):
        for at_zh in range(2):
            for at_y in range(4):
                a_x, a_zh, a_y = x ^ at_x, zh ^ at_zh, y ^ at_y
                if kind == "x":
                    a = 2 * a_x[None, :] + a_zh[:, None]
                else:
                    a = 2 * a_x[:, None] + a_zh[None, :]
                r = 4 * zl[:, None] + a_y[None, :]
                place = (8 * r[None, None] + a[:, :, None, None]).reshape(64)
                angle = 2.0 * np.pi * (np.outer(np.arange(64), place) % 64) / 64
                cosine, sine = np.cos(angle), np.sin(angle)
                real_part = np.stack([cosine, sine], -1).reshape(64, 128)
                imag_part = np.stack([-sine, cosine], -1).reshape(64, 128)
                first_of.append(np.stack(halves(np.concatenate([real_part, imag_part], 0))))
    angle = 2.0 * np.pi * (np.outer(np.arange(128), np.arange(128)) % M) / M
    twist = np.stack([np.cos(angle), -np.sin(angle)]).astype(np.float32)
    second = np.stack(halves(complex_table(np.outer(np.arange(64), np.arange(128)), 64)))
    return np.stack(first_of), twist, second


def sine_polynomials():
    nodes = 0.25 * np.cos(np.pi * (np.arange(400) + 0.5) / 800)
    square = np.polynomial.chebyshev.Chebyshev.fit(
        nodes**2, np.sin(2 * np.pi * nodes) / nodes, 4, domain=[0, 1 / 16]
    ).convert(kind=np.polynomial.Polynomial, domain=[-1, 1], window=[-1, 1])
    cosine = np.polynomial.chebyshev.Chebyshev.fit(
        nodes**2, np.cos(2 * np.pi * nodes), 5, domain=[0, 1 / 16]
    ).convert(kind=np.polynomial.Polynomial, domain=[-1, 1], window=[-1, 1])
    return [float(c) for c in square.coef], [float(c) for c in cosine.coef]


SINE, COSINE = sine_polynomials()


def horner(coefficients, value):
    total = jnp.full_like(value, coefficients[-1])
    for coefficient in coefficients[-2::-1]:
        total = total * value + coefficient
    return total


def dot(a, b):
    return jnp.dot(a, b, preferred_element_type=F32)


def dot_nt(a, b):
    return lax.dot_general(a, b, (((1,), (1,)), ((), ())), preferred_element_type=F32)


def draw(bits_0, bits_1, eigen):
    uniform = (bits_0.astype(F32) + 0.5) * 2.0**-12
    radius = jnp.sqrt(jnp.log(uniform) * eigen * (-2.0 / (N * M)))
    past = (bits_1.astype(F32) - 2047.5) * 2.0**-12
    h = jnp.abs(past) - 0.25
    square = h * h
    value_re = radius * (h * horner(SINE, square))
    value_im = jnp.where(past > 0, -radius, radius) * horner(COSINE, square)
    return value_re, value_im


def draw_kernel(noise, eigen, high, low):
    for part, value in enumerate(draw(noise[0], noise[1], eigen[...])):
        at = slice(LOCAL * part, LOCAL * (part + 1))
        high[at, :], low[at, :] = split(value)


def draw_field(noise, eigen):
    block = 128
    shape = jax.ShapeDtypeStruct((2 * LOCAL, WIDTH), BF16)
    return pl.pallas_call(
        draw_kernel,
        grid=(WIDTH // block,),
        in_specs=[
            pl.BlockSpec((2, LOCAL, block), lambda i: (0, 0, i)),
            pl.BlockSpec((LOCAL, block), lambda i: (0, i)),
        ],
        out_specs=[pl.BlockSpec((2 * LOCAL, block), lambda i: (0, i))] * 2,
        out_shape=[shape, shape],
        compiler_params=pltpu.CompilerParams(vmem_limit_bytes=32 * 2**20),
        cost_estimate=pl.CostEstimate(flops=10**7, bytes_accessed=10 * 2**20, transcendentals=0),
    )(noise, eigen)


def column_kernel(kind, place, high, low, table, twist, *outs):
    x, zh, zl = place[0], place[1], place[3]
    half = 4 * ROWS
    for d in range(4):
        columns = pl.ds(pl.multiple_of(256 * (d ^ x), 256), 256)
        data_high, data_low = high[:, columns], low[:, columns]
        for d_zl in range(2):
            zl_out = d_zl ^ zl
            at = pl.ds(pl.multiple_of(2 * half * zl_out, 2 * half), 2 * half)
            table_high = table[0, at, :]
            both = dot(table_high, data_high) + dot(table[1, at, :], data_high) + dot(table_high, data_low)
            at = pl.ds(pl.multiple_of(half * zl_out, half), half)
            turn_re, turn_im = twist[0, at, :], twist[1, at, :]
            turned = []
            for a in range(2):
                re, im = both[:half, 128 * a : 128 * a + 128], both[half:, 128 * a : 128 * a + 128]
                turned.append((re * turn_re - im * turn_im, re * turn_im + im * turn_re))
            for part in range(2):
                first, second = turned[0][part], turned[1][part]
                for d_zh in range(2):
                    value = jnp.where(zh == d_zh, first, second)
                    value = value.reshape(4, ROWS, 128)
                    for y in range(4):
                        d_y = y ^ place[4]
                        if kind == "x":
                            outs[d][2 * d_zh + d_zl, d_y, part] = value[y]
                        else:
                            outs[2 * d_zh + d_zl][d, d_y, part] = value[y]


IN_VMEM = pl.BlockSpec(memory_space=pltpu.VMEM)
IN_SMEM = pl.BlockSpec(memory_space=pltpu.SMEM)


def column_transform(kind, place, high, low, table, twist):
    shape = jax.ShapeDtypeStruct((4, 4, 2, ROWS, 128), F32)
    return pl.pallas_call(
        functools.partial(column_kernel, kind),
        in_specs=[IN_SMEM] + [IN_VMEM] * 4,
        out_specs=[IN_VMEM] * 4,
        out_shape=[shape] * 4,
        compiler_params=pltpu.CompilerParams(vmem_limit_bytes=40 * 2**20),
        cost_estimate=pl.CostEstimate(flops=7 * 10**9 // CHUNKS, bytes_accessed=6 * 2**20, transcendentals=0),
    )(place, high, low, table, twist)


def add(a, b):
    return a[0] + b[0], a[1] + b[1]


def sub(a, b):
    return a[0] - b[0], a[1] - b[1]


def turn_back(a):
    return a[1], -a[0]


ROOT = math.sqrt(0.5)


def dft_4(a, b, c, d):
    even, odd = add(a, c), add(b, d)
    less, turned = sub(a, c), turn_back(sub(b, d))
    return add(even, odd), add(less, turned), sub(even, odd), sub(less, turned)


def dft_8(v):
    even = dft_4(v[0], v[2], v[4], v[6])
    odd = dft_4(v[1], v[3], v[5], v[7])
    spun = [
        odd[0],
        ((odd[1][0] + odd[1][1]) * ROOT, (odd[1][1] - odd[1][0]) * ROOT),
        turn_back(odd[2]),
        ((odd[3][1] - odd[3][0]) * ROOT, (odd[3][0] + odd[3][1]) * -ROOT),
    ]
    return [add(e, o) for e, o in zip(even, spun)] + [sub(e, o) for e, o in zip(even, spun)]


def middle_kernel(kind, place, scalars, mine, other, *outs):
    sign = scalars[16]
    at_x, at_zh, at_zl = place[0], place[1], place[3]

    def run(here):
        def step(d_y, carry):
            for zl in range(2):
                for row in range(0, ROWS, 8):
                    at = pl.ds(row, 8)
                    values = []
                    for e in range(8):
                        zh, xl, xh = e >> 2, e >> 1 & 1, e & 1
                        d_x, d_z = (2 * xh + xl) ^ at_x, 2 * (zh ^ at_zh) + (zl ^ at_zl)
                        index = (d_z, d_y, d_x) if kind == "x" else (d_y, d_x, d_z)
                        re = mine[*index, 0, at, :] * sign + other[*index, 0, at, :]
                        im = mine[*index, 1, at, :] * sign + other[*index, 1, at, :]
                        c, s = scalars[2 * e], scalars[2 * e + 1]
                        values.append((re * c - im * s, re * s + im * c))
                    for k, value in enumerate(dft_8(values)):
                        zh, x = k & 1, 2 * (k >> 2) + (k >> 1 & 1)
                        for part in range(2):
                            if kind == "x":
                                outs[x ^ here][zh ^ at_zh, zl, d_y, part, at, :] = value[part]
                            else:
                                outs[zh ^ here][x ^ at_x, zl, d_y, part, at, :] = value[part]
            return carry

        lax.fori_loop(0, 4, step, 0)

    for here in range(4 if kind == "x" else 2):
        pl.when((at_x if kind == "x" else at_zh) == here)(functools.partial(run, here))


def middle(kind, place, scalars, mine, other):
    count = 4 if kind == "x" else 2
    shape = jax.ShapeDtypeStruct((8 // count, 2, 4, 2, ROWS, 128), F32)
    return pl.pallas_call(
        functools.partial(middle_kernel, kind),
        in_specs=[IN_SMEM] * 2 + [IN_VMEM] * 2,
        out_specs=[IN_VMEM] * count,
        out_shape=[shape] * count,
        compiler_params=pltpu.CompilerParams(vmem_limit_bytes=32 * 2**20),
        cost_estimate=pl.CostEstimate(flops=10**7, bytes_accessed=3 * 2**20, transcendentals=0),
    )(place, scalars, mine, other)


def row_kernel(count, *refs):
    pieces, (first, twist, second) = refs[:count], refs[count : count + 3]
    out, turned = refs[-2:]
    for t in range(8):
        high, low = split(jnp.concatenate([piece[:, t, :] for piece in pieces], 0))
        table = first[0]
        step = dot(table, high) + dot(first[1], high) + dot(table, low)
        both = []
        for v in range(2):
            re, im = twist[0, 64 * v : 64 * (v + 1), :], twist[1, 64 * v : 64 * (v + 1), :]
            both.append(jnp.concatenate([step[:64] * re - step[64:] * im, step[:64] * im + step[64:] * re], 1))
        high, low = split(jnp.concatenate(both, 0))
        table = second[0]
        last = dot_nt(table, high) + dot_nt(second[1], high) + dot_nt(table, low)
        turned[pl.ds(t, 128, stride=8), :] = last
    for part in range(2):
        for u in range(64):
            out[part, :, 128 * u : 128 * (u + 1)] = turned[8 * (64 * part + u) : 8 * (64 * part + u) + 8, :]


def row_transform(chunk, result, pieces, first, twist, second):
    count = len(pieces)
    pieces = [piece.reshape(128 // count, ROWS, 128) for piece in pieces]
    whole = lambda shape: pl.BlockSpec(shape, lambda i: (0,) * len(shape))
    kernel = functools.partial(row_kernel, count)
    operands = pieces + [first, twist, second]
    specs = [pl.BlockSpec((128 // count, 8, 128), lambda i: (0, i, 0))] * count
    specs += [whole(first.shape), whole(twist.shape), whole(second.shape)]
    aliases = {}
    if result is not None:
        aliases = {len(operands): 0}
        operands.append(result)
        specs.append(pl.BlockSpec(memory_space=pl.ANY))
    steps = ROWS // 8
    return pl.pallas_call(
        kernel,
        grid=(steps,),
        in_specs=specs,
        out_specs=pl.BlockSpec((2, 8, M), lambda i: (0, chunk * steps + i, 0)),
        out_shape=jax.ShapeDtypeStruct((2, 64, M), F32),
        input_output_aliases=aliases,
        scratch_shapes=[pltpu.VMEM((1024, 128), F32)],
        compiler_params=pltpu.CompilerParams(vmem_limit_bytes=32 * 2**20),
        cost_estimate=pl.CostEstimate(flops=3 * 10**9 // CHUNKS, bytes_accessed=2 * 2**20, transcendentals=0),
    )(*operands)


def swap(value, axis, apart):
    if apart == 0:
        return value
    count = math.prod(SIZES[AXES.index(name)] for name in (axis if isinstance(axis, tuple) else (axis,)))
    return lax.ppermute(value, axis, [(i, i ^ apart) for i in range(count)])


def exchange(pieces, axis):
    return [swap(piece, axis, d) for d, piece in enumerate(pieces)]


def regroup(pieces, count):
    return [jnp.stack([piece[j] for piece in pieces]) for j in range(count)]


Z = ("zh", "zl")


def on_device(noise, eigen):
    place = jnp.stack([lax.axis_index(name) for name in AXES]).astype(jnp.int32)
    x, zh, core = place[0], place[1], place[2]
    xh, xl = x // 2, x % 2
    anchor = 8 * core + 4 * zh + 2 * xl + xh
    rows = jnp.arange(LOCAL, dtype=jnp.int32).reshape(8, CHUNKS, ROWS).transpose(1, 0, 2).reshape(CHUNKS, 8 * ROWS)
    angle = (anchor * rows % N).astype(F32) * (-2.0 * math.pi / N)
    twist = jnp.stack([jnp.cos(angle), jnp.sin(angle)], 1)
    twist = jnp.broadcast_to(twist[..., None], (CHUNKS, 2, 8 * ROWS, 128))
    angle = (core * jnp.arange(8, dtype=jnp.int32)).astype(F32) * (-2.0 * math.pi / 16)
    scalars = jnp.concatenate(
        [jnp.stack([jnp.cos(angle), jnp.sin(angle)], 1).reshape(16), (1 - 2 * core).astype(F32)[None]]
    )
    tables = {kind: row_tables(kind) for kind in sorted(set(KINDS))}
    own = (x * 2 + zh) * 4 + place[4]
    firsts = {
        kind: lax.dynamic_index_in_dim(jnp.asarray(table[0]), own, 0, keepdims=False) for kind, table in tables.items()
    }
    row_twist, second = (jnp.asarray(t) for t in tables[KINDS[0]][1:])
    column_table = column_tables()

    with jax.named_scope("draw"):
        high, low = draw_field(noise, eigen)
    current = []
    for chunk, kind in enumerate(KINDS):
        with jax.named_scope(f"columns_{chunk}"):
            current.append(
                column_transform(kind, place, high, low, jnp.asarray(column_table[:, chunk]), twist[chunk])
            )
    result = None
    for chunk, kind in enumerate(KINDS):
        pieces = current[chunk]
        with jax.named_scope(f"out_{chunk}"):
            if kind == "x":
                pieces = exchange(pieces, "x")
                pieces = [jnp.stack([piece[:, j] for piece in pieces], 1) for j in range(4)]
                pieces = exchange(pieces, "y")
                pieces = exchange(regroup(pieces, 4), Z)
            else:
                pieces = exchange(pieces, Z)
                pieces = exchange(regroup(pieces, 4), "x")
                pieces = [jnp.stack([piece[:, j] for piece in pieces]) for j in range(4)]
                pieces = exchange(pieces, "y")
            mine = jnp.stack(pieces)
            other = swap(mine, "core", 1)
        with jax.named_scope(f"middle_{chunk}"):
            pieces = middle(kind, place, scalars, mine, other)
        with jax.named_scope(f"back_{chunk}"):
            if kind == "x":
                pieces = exchange(pieces, "x")
                pieces = exchange(regroup(pieces, 2), "zh")
            else:
                pieces = exchange(pieces, "zh")
                pieces = exchange(regroup(pieces, 4), "x")
        with jax.named_scope(f"rows_{chunk}"):
            result = row_transform(chunk, result, pieces, firsts[kind], row_twist, second)
    return result


def solution(mesh):
    fine = Mesh(mesh.devices.reshape(SIZES), AXES)
    col, row = AXES[:3], AXES[3:]
    return jax.shard_map(
        on_device,
        mesh=fine,
        in_specs=(P(None, col, row), P(col, row)),
        out_specs=P(None, AXES, None),
        check_vma=False,
    )
```

time: 185 us -> 232 us (1.25)
  blocking collectives: 118 us -> 0 us
  waiting for transfers between devices: 6.62 us -> 96.5 us
  starting transfers between devices: 0.01 us -> 78.5 us
  Pallas kernels: 54.3 us -> 37.3 us
  local copies, waits for them, and re-layouts: 5.15 us -> 13.3 us
  other arithmetic: 0.8 us -> 4.23 us
    all_to_all x2 -> x0, blocking collectives: 118 us -> none  [the longest x1 58.9 us: on_device(): lax.all_to_all(current.reshape(32, 2, 2, 64, 128), ('x', 'zh', 'y'), 0, 0...]
    ppermute x1 -> x56, waiting for transfers between devices: 6.62 us -> 96.5 us  [swap(): return lax.ppermute(value, axis, [(i, i ^ apart) for i in range(count)])]
    ppermute x1 -> x56, starting transfers between devices: 0.01 us -> 78.5 us  [swap(): return lax.ppermute(value, axis, [(i, i ^ apart) for i in range(count)])]
    pallas_call x3 -> x13, Pallas kernels: 54.3 us -> 37.3 us  [the longest x4 15.7 us: row_transform(): pl.pallas_call(kernel, grid=(steps,), in_specs=specs, out_specs=pl.BlockS...]
    another operation x1 -> x49, other arithmetic: 0.01 us -> 4.04 us  [the longest x8 2.47 us: on_device(): mine = jnp.stack(pieces)]
    unnamed x16 -> x22, local copies, waits for them, and re-layouts: 4.8 us -> 8.64 us
  transfers between devices with their start and end apart: 1 -> 56, of which waited for: 1 -> 25; matrix products, arithmetic and copies ran while one was open for 0% -> 4% of each run, Pallas kernels for 0% -> 11%
where the time goes in v1:
time: 232 us; the launch traced here: 231 us
  waiting for transfers between devices  96.5 us (42%)
  starting transfers between devices  78.5 us (34%)
  Pallas kernels  37.3 us (16%)
  local copies, waits for them, and re-layouts  13.3 us (6%)
  other arithmetic  4.23 us (2%)
    ppermute x56, waiting for transfers between devices, swap(): return lax.ppermute(value, axis, [(i, i ^ apart) for i in range(count)])  96.5 us
    ppermute x56, starting transfers between devices, swap(): return lax.ppermute(value, axis, [(i, i ^ apart) for i in range(count)])  78.5 us
    pallas_call x4, Pallas kernels, row_transform(): pl.pallas_call(kernel, grid=(steps,), in_specs=specs, out_specs=pl.BlockS...  15.7 us
    pallas_call x4, Pallas kernels, column_transform(): pl.pallas_call(functools.partial(column_kernel, kind), in_specs=[IN_SMEM]...  9.87 us
    unnamed x22, local copies, waits for them, and re-layouts  8.64 us
    pallas_call x4, Pallas kernels, middle(): pl.pallas_call(functools.partial(middle_kernel, kind), in_specs=[IN_SMEM]...  5.87 us
    pallas_call x1, Pallas kernels, draw_field(): pl.pallas_call(draw_kernel, grid=(WIDTH // block,), in_specs=[pl.BlockSpe...  5.83 us
  transfers between devices with their start and end apart: 56, of which 25 were waited for; matrix products, arithmetic and copies ran while one was open for 4% of the time, Pallas kernels for 11%

profile of v1, /device:TPU:0, one launch (start us, length us, event | category | flops | bytes accessed | tf_op | source)
XLA Modules:
  0.0 231.0 jit_solution(3933216722517676123)
XLA Ops:
  0.3 2.2 copy-done
  4.0 5.8 %draw.1 = (bf16[1024,1024]{1,0:T(8,128)(2,1)S(1)}, bf16[1024,1024]{1,0:T(8,128)(2,1)S(1)}) custom-call(s32[2,512,1024]{2,1,0:T(8,128)S(1)} %copy-done, f32[512,1024]{1,0:T(8,128)S(1)} %copy-done.3), custom_call_target="tpu_custom_call" | custom-call | flops 10000000 | bytes 10485760 | tf_op jit(solution)/shard_map/draw/pallas_call | solution.py:128
  14.2 2.4 %columns_0.1 = (f32[4,4,2,16,128]{4,3,2,1,0:T(8,128)S(1)}, f32[4,4,2,16,128]{4,3,2,1,0:T(8,128)S(1)}, f32[4,4,2,16,128]{4,3,2,1,0:T(8,128)S(1)}, f32[4,4,2,16,128]{4,3,2,1,0:T(8,128)S(1)}) custom-call(s32[5]{0:T(128)S(1)} %stack.225.place, bf16[1024,1024]{1,0:T(8,128)(2,1)S(1)} %get-tuple-element.35.high, bf16[1024,1024]{1,0:T(8,128)(2,1)S(1)} %copy-done.5, ...), custom_call_target="tpu_custom_call" | custom-call | flops 1750000000 | bytes 6291456 | tf_op jit(solution)/shard_map/columns_0/pallas_call | solution.py:178
  18.3 2.7 %collective-permute-start.43 = (f32[4,4,2,16,128]{4,3,2,1,0:T(8,128)S(1)}, f32[4,4,2,16,128]{4,3,2,1,0:T(8,128)S(1)}, u32[]{:S(2)}, u32[]{:S(2)}) collective-permute-start(f32[4,4,2,16,128]{4,3,2,1,0:T(8,128)S(1)} %get-tuple-element.59), channel_id=1, source_target_pairs={{0,64},{32,96},{64,0},{96,32},{1,65},{33,97},{65,1},{97,33},{2,66}... | collective-permute-start | bytes 786440 | tf_op jit(solution)/shard_map/out_0/ppermute | solution.py:318
  21.5 2.5 %columns_1.1 = (f32[4,4,2,16,128]{4,3,2,1,0:T(8,128)S(1)}, f32[4,4,2,16,128]{4,3,2,1,0:T(8,128)S(1)}, f32[4,4,2,16,128]{4,3,2,1,0:T(8,128)S(1)}, f32[4,4,2,16,128]{4,3,2,1,0:T(8,128)S(1)}) custom-call(s32[5]{0:T(128)S(1)} %stack.225.place, bf16[1024,1024]{1,0:T(8,128)(2,1)S(1)} %get-tuple-element.35.high, bf16[1024,1024]{1,0:T(8,128)(2,1)S(1)} %copy-done.5, ...), custom_call_target="tpu_custom_call" | custom-call | flops 1750000000 | bytes 6291456 | tf_op jit(solution)/shard_map/columns_1/pallas_call | solution.py:178
  24.1 4.2 %collective-permute-start.30 = (f32[4,4,2,16,128]{4,3,2,0,1:T(8,128)S(1)}, f32[4,4,2,16,128]{4,3,2,0,1:T(8,128)S(1)}, u32[]{:S(2)}, u32[]{:S(2)}) collective-permute-start(f32[4,4,2,16,128]{4,3,2,0,1:T(8,128)S(1)} %copy.68), channel_id=1, source_target_pairs={{0,20},{4,16},{16,4},{20,0},{1,21},{5,17},{17,5},{21,1},{2,22},{6,... | collective-permute-start | bytes 786440 | tf_op jit(solution)/shard_map/out_1/ppermute | solution.py:318
  28.5 2.5 %columns_3.1 = (f32[4,4,2,16,128]{4,3,2,1,0:T(8,128)S(1)}, f32[4,4,2,16,128]{4,3,2,1,0:T(8,128)S(1)}, f32[4,4,2,16,128]{4,3,2,1,0:T(8,128)S(1)}, f32[4,4,2,16,128]{4,3,2,1,0:T(8,128)S(1)}) custom-call(s32[5]{0:T(128)S(1)} %stack.225.place, bf16[1024,1024]{1,0:T(8,128)(2,1)S(1)} %get-tuple-element.35.high, bf16[1024,1024]{1,0:T(8,128)(2,1)S(1)} %copy-done.5, ...), custom_call_target="tpu_custom_call" | custom-call | flops 1750000000 | bytes 6291456 | tf_op jit(solution)/shard_map/columns_3/pallas_call | solution.py:178
  31.2 2.5 %columns_2.1 = (f32[4,4,2,16,128]{4,3,2,1,0:T(8,128)S(1)}, f32[4,4,2,16,128]{4,3,2,1,0:T(8,128)S(1)}, f32[4,4,2,16,128]{4,3,2,1,0:T(8,128)S(1)}, f32[4,4,2,16,128]{4,3,2,1,0:T(8,128)S(1)}) custom-call(s32[5]{0:T(128)S(1)} %stack.225.place, bf16[1024,1024]{1,0:T(8,128)(2,1)S(1)} %get-tuple-element.35.high, bf16[1024,1024]{1,0:T(8,128)(2,1)S(1)} %copy-done.5, ...), custom_call_target="tpu_custom_call" | custom-call | flops 1750000000 | bytes 6291456 | tf_op jit(solution)/shard_map/columns_2/pallas_call | solution.py:178
  34.7 3.3 %collective-permute-start.2 = (f32[4,4,2,16,128]{4,3,2,0,1:T(8,128)S(1)}, f32[4,4,2,16,128]{4,3,2,0,1:T(8,128)S(1)}, u32[]{:S(2)}, u32[]{:S(2)}) collective-permute-start(f32[4,4,2,16,128]{4,3,2,0,1:T(8,128)S(1)} %copy.61), channel_id=1, source_target_pairs={{0,20},{4,16},{16,4},{20,0},{1,21},{5,17},{17,5},{21,1},{2,22},{6,... | collective-permute-start | bytes 786440 | tf_op jit(solution)/shard_map/out_3/ppermute | solution.py:318
  39.3 2.8 %collective-permute-done.30 = f32[4,4,2,16,128]{4,3,2,0,1:T(8,128)S(1)} collective-permute-done((f32[4,4,2,16,128]{4,3,2,0,1:T(8,128)S(1)}, f32[4,4,2,16,128]{4,3,2,0,1:T(8,128)S(1)}, u32[]{:S(2)}, u32[]{:S(2)}) %collective-permute-start.30) | collective-permute-done | bytes 262176 | tf_op jit(solution)/shard_map/out_1/ppermute | solution.py:318
  42.5 4.0 %collective-permute-start.15 = (f32[4,4,2,16,128]{4,3,2,1,0:T(8,128)S(1)}, f32[4,4,2,16,128]{4,3,2,1,0:T(8,128)S(1)}, u32[]{:S(2)}, u32[]{:S(2)}) collective-permute-start(f32[4,4,2,16,128]{4,3,2,1,0:T(8,128)S(1)} %get-tuple-element.45), channel_id=1, source_target_pairs={{0,64},{32,96},{64,0},{96,32},{1,65},{33,97},{65,1},{97,33},{2,66}... | collective-permute-start | bytes 786440 | tf_op jit(solution)/shard_map/out_2/ppermute | solution.py:318
  46.6 4.0 %collective-permute-done.2 = f32[4,4,2,16,128]{4,3,2,0,1:T(8,128)S(1)} collective-permute-done((f32[4,4,2,16,128]{4,3,2,0,1:T(8,128)S(1)}, f32[4,4,2,16,128]{4,3,2,0,1:T(8,128)S(1)}, u32[]{:S(2)}, u32[]{:S(2)}) %collective-permute-start.2) | collective-permute-done | bytes 262176 | tf_op jit(solution)/shard_map/out_3/ppermute | solution.py:318
  50.6 2.8 %collective-permute-start.16 = (f32[4,4,2,16,128]{4,3,2,1,0:T(8,128)S(1)}, f32[4,4,2,16,128]{4,3,2,1,0:T(8,128)S(1)}, u32[]{:S(2)}, u32[]{:S(2)}) collective-permute-start(f32[4,4,2,16,128]{4,3,2,1,0:T(8,128)S(1)} %get-tuple-element.46), channel_id=1, source_target_pairs={{0,96},{32,64},{64,32},{96,0},{1,97},{33,65},{65,33},{97,1},{2,98}... | collective-permute-start | bytes 786440 | tf_op jit(solution)/shard_map/out_2/ppermute | solution.py:318
  55.4 3.0 %collective-permute-start.46 = (f32[4,4,2,16,128]{4,3,2,1,0:T(8,128)S(1)}, f32[4,4,2,16,128]{4,3,2,1,0:T(8,128)S(1)}, u32[]{:S(2)}, u32[]{:S(2)}) collective-permute-start(f32[4,4,2,16,128]{4,3,2,1,0:T(8,128)S(1)} %pad_maximum_fusion.39), channel_id=1, source_target_pairs={{0,2},{1,3},{2,0},{3,1},{4,6},{5,7},{6,4},{7,5},{8,10},{9,11},{10,... | collective-permute-start | bytes 786440 | tf_op jit(solution)/shard_map/out_0/ppermute | solution.py:318
  63.0 5.6 %collective-permute-done.46 = f32[4,4,2,16,128]{4,3,2,1,0:T(8,128)S(1)} collective-permute-done((f32[4,4,2,16,128]{4,3,2,1,0:T(8,128)S(1)}, f32[4,4,2,16,128]{4,3,2,1,0:T(8,128)S(1)}, u32[]{:S(2)}, u32[]{:S(2)}) %collective-permute-start.46) | collective-permute-done | bytes 262176 | tf_op jit(solution)/shard_map/out_0/ppermute | solution.py:318
  69.3 9.6 %collective-permute-done.3 = f32[4,4,2,16,128]{4,3,2,0,1:T(8,128)S(1)} collective-permute-done((f32[4,4,2,16,128]{4,3,2,0,1:T(8,128)S(1)}, f32[4,4,2,16,128]{4,3,2,0,1:T(8,128)S(1)}, u32[]{:S(2)}, u32[]{:S(2)}) %collective-permute-start.3) | collective-permute-done | bytes 262176 | tf_op jit(solution)/shard_map/out_3/ppermute | solution.py:318
  79.3 3.0 %collective-permute-done.4 = f32[4,4,2,16,128]{4,3,2,0,1:T(8,128)S(1)} collective-permute-done((f32[4,4,2,16,128]{4,3,2,0,1:T(8,128)S(1)}, f32[4,4,2,16,128]{4,3,2,0,1:T(8,128)S(1)}, u32[]{:S(2)}, u32[]{:S(2)}) %collective-permute-start.4) | collective-permute-done | bytes 262176 | tf_op jit(solution)/shard_map/out_3/ppermute | solution.py:318
  82.5 4.2 %collective-permute-done.5 = f32[4,4,2,16,128]{4,3,2,0,1:T(8,128)S(1)} collective-permute-done((f32[4,4,2,16,128]{4,3,2,0,1:T(8,128)S(1)}, f32[4,4,2,16,128]{4,3,2,0,1:T(8,128)S(1)}, u32[]{:S(2)}, u32[]{:S(2)}) %collective-permute-start.5) | collective-permute-done | bytes 262176 | tf_op jit(solution)/shard_map/out_3/ppermute | solution.py:318
  86.7 2.4 %collective-permute-start.18 = (f32[4,4,2,16,128]{4,3,2,1,0:T(8,128)S(1)}, f32[4,4,2,16,128]{4,3,2,1,0:T(8,128)S(1)}, u32[]{:S(2)}, u32[]{:S(2)}) collective-permute-start(f32[4,4,2,16,128]{4,3,2,1,0:T(8,128)S(1)} %pad_maximum_fusion.21), channel_id=1, source_target_pairs={{0,2},{1,3},{2,0},{3,1},{4,6},{5,7},{6,4},{7,5},{8,10},{9,11},{10,... | collective-permute-start | bytes 786440 | tf_op jit(solution)/shard_map/out_2/ppermute | solution.py:318
  89.2 4.9 %collective-permute-start.19 = (f32[4,4,2,16,128]{4,3,2,1,0:T(8,128)S(1)}, f32[4,4,2,16,128]{4,3,2,1,0:T(8,128)S(1)}, u32[]{:S(2)}, u32[]{:S(2)}) collective-permute-start(f32[4,4,2,16,128]{4,3,2,1,0:T(8,128)S(1)} %pad_maximum_fusion.22), channel_id=1, source_target_pairs={{0,3},{1,2},{2,1},{3,0},{4,7},{5,6},{6,5},{7,4},{8,11},{9,10},{10,... | collective-permute-start | bytes 786440 | tf_op jit(solution)/shard_map/out_2/ppermute | solution.py:318
  94.2 2.5 %collective-permute-done.18 = f32[4,4,2,16,128]{4,3,2,1,0:T(8,128)S(1)} collective-permute-done((f32[4,4,2,16,128]{4,3,2,1,0:T(8,128)S(1)}, f32[4,4,2,16,128]{4,3,2,1,0:T(8,128)S(1)}, u32[]{:S(2)}, u32[]{:S(2)}) %collective-permute-start.18) | collective-permute-done | bytes 262176 | tf_op jit(solution)/shard_map/out_2/ppermute | solution.py:318
  96.7 2.3 collective-permute-start.33
  101.5 2.8 %collective-permute-start.7 = (f32[4,4,2,16,128]{4,3,2,1,0:T(8,128)S(1)}, f32[4,4,2,16,128]{4,3,2,1,0:T(8,128)S(1)}, u32[]{:S(2)}, u32[]{:S(2)}) collective-permute-start(f32[4,4,2,16,128]{4,3,2,1,0:T(8,128)S(1)} %pad_maximum_fusion.13), channel_id=1, source_target_pairs={{0,2},{1,3},{2,0},{3,1},{4,6},{5,7},{6,4},{7,5},{8,10},{9,11},{10,... | collective-permute-start | bytes 786440 | tf_op jit(solution)/shard_map/out_3/ppermute | solution.py:318
  105.0 6.3 %collective-permute-start.21 = (f32[4,4,2,16,128]{4,3,2,1,0:T(8,128)S(1)}, f32[4,4,2,16,128]{4,3,2,1,0:T(8,128)S(1)}, u32[]{:S(2)}, u32[]{:S(2)}) collective-permute-start(f32[4,4,2,16,128]{4,3,2,1,0:T(8,128)S(1)} %pad_maximum_fusion.24), channel_id=1, source_target_pairs={{0,16},{4,20},{16,0},{20,4},{1,17},{5,21},{17,1},{21,5},{2,18},{6,... | collective-permute-start | bytes 786440 | tf_op jit(solution)/shard_map/out_2/ppermute | solution.py:318
  111.6 2.3 %collective-permute-start.8 = (f32[4,4,2,16,128]{4,3,2,1,0:T(8,128)S(1)}, f32[4,4,2,16,128]{4,3,2,1,0:T(8,128)S(1)}, u32[]{:S(2)}, u32[]{:S(2)}) collective-permute-start(f32[4,4,2,16,128]{4,3,2,1,0:T(8,128)S(1)} %pad_maximum_fusion.14), channel_id=1, source_target_pairs={{0,3},{1,2},{2,1},{3,0},{4,7},{5,6},{6,5},{7,4},{8,11},{9,10},{10,... | collective-permute-start | bytes 786440 | tf_op jit(solution)/shard_map/out_3/ppermute | solution.py:318
  114.1 8.4 %collective-permute-done.21 = f32[4,4,2,16,128]{4,3,2,1,0:T(8,128)S(1)} collective-permute-done((f32[4,4,2,16,128]{4,3,2,1,0:T(8,128)S(1)}, f32[4,4,2,16,128]{4,3,2,1,0:T(8,128)S(1)}, u32[]{:S(2)}, u32[]{:S(2)}) %collective-permute-start.21) | collective-permute-done | bytes 262176 | tf_op jit(solution)/shard_map/out_2/ppermute | solution.py:318
  125.3 2.3 collective-permute-start.36
  128.6 2.2 collective-permute-done.35
  130.8 5.5 %collective-permute-done.36 = f32[4,4,2,16,128]{4,3,2,1,0:T(8,128)S(1)} collective-permute-done((f32[4,4,2,16,128]{4,3,2,1,0:T(8,128)S(1)}, f32[4,4,2,16,128]{4,3,2,1,0:T(8,128)S(1)}, u32[]{:S(2)}, u32[]{:S(2)}) %collective-permute-start.36) | collective-permute-done | bytes 262176 | tf_op jit(solution)/shard_map/out_1/ppermute | solution.py:318
  136.5 1.9 collective-permute-start.49
  142.3 4.7 %collective-permute-done.49 = f32[4,4,2,16,128]{4,3,2,1,0:T(8,128)} collective-permute-done((f32[4,4,2,16,128]{4,3,2,1,0:T(8,128)S(1)}, f32[4,4,2,16,128]{4,3,2,1,0:T(8,128)}, u32[]{:S(2)}, u32[]{:S(2)}) %collective-permute-start.49) | collective-permute-done | bytes 262176 | tf_op jit(solution)/shard_map/out_0/ppermute | solution.py:318
  147.0 5.5 %collective-permute-done.50 = f32[4,4,2,16,128]{4,3,2,1,0:T(8,128)} collective-permute-done((f32[4,4,2,16,128]{4,3,2,1,0:T(8,128)}, f32[4,4,2,16,128]{4,3,2,1,0:T(8,128)}, u32[]{:S(2)}, u32[]{:S(2)}) %collective-permute-start.50) | collective-permute-done | bytes 262176 | tf_op jit(solution)/shard_map/out_0/ppermute | solution.py:318
  158.4 3.2 %collective-permute-start.25 = (f32[2,2,4,2,16,128]{5,4,3,2,1,0:T(8,128)S(1)}, f32[2,2,4,2,16,128]{5,4,3,2,1,0:T(8,128)S(1)}, u32[]{:S(2)}, u32[]{:S(2)}) collective-permute-start(f32[2,2,4,2,16,128]{5,4,3,2,1,0:T(8,128)S(1)} %get-tuple-element.49), channel_id=1, source_target_pairs={{0,64},{32,96},{64,0},{96,32},{1,65},{33,97},{65,1},{97,33},{2,66}... | collective-permute-start | bytes 786440 | tf_op jit(solution)/shard_map/back_2/ppermute | solution.py:318
  163.7 1.9 collective-permute-start.10
  170.5 3.4 %collective-permute-done.25 = f32[2,2,4,2,16,128]{5,4,3,2,1,0:T(8,128)S(1)} collective-permute-done((f32[2,2,4,2,16,128]{5,4,3,2,1,0:T(8,128)S(1)}, f32[2,2,4,2,16,128]{5,4,3,2,1,0:T(8,128)S(1)}, u32[]{:S(2)}, u32[]{:S(2)}) %collective-permute-start.25) | collective-permute-done | bytes 262176 | tf_op jit(solution)/shard_map/back_2/ppermute | solution.py:318
  177.1 2.7 %collective-permute-done.52 = f32[2,2,4,2,16,128]{5,4,3,2,1,0:T(8,128)S(1)} collective-permute-done((f32[2,2,4,2,16,128]{5,4,3,2,1,0:T(8,128)S(1)}, f32[2,2,4,2,16,128]{5,4,3,2,1,0:T(8,128)S(1)}, u32[]{:S(2)}, u32[]{:S(2)}) %collective-permute-start.52) | collective-permute-done | bytes 262176 | tf_op jit(solution)/shard_map/back_0/ppermute | solution.py:318
  179.7 1.8 collective-permute-start.27
  181.6 4.1 %collective-permute-done.53 = f32[2,2,4,2,16,128]{5,4,3,2,1,0:T(8,128)S(1)} collective-permute-done((f32[2,2,4,2,16,128]{5,4,3,2,1,0:T(8,128)S(1)}, f32[2,2,4,2,16,128]{5,4,3,2,1,0:T(8,128)S(1)}, u32[]{:S(2)}, u32[]{:S(2)}) %collective-permute-start.53) | collective-permute-done | bytes 262176 | tf_op jit(solution)/shard_map/back_0/ppermute | solution.py:318
  185.7 4.2 %collective-permute-done.54 = f32[2,2,4,2,16,128]{5,4,3,2,1,0:T(8,128)S(1)} collective-permute-done((f32[2,2,4,2,16,128]{5,4,3,2,1,0:T(8,128)S(1)}, f32[2,2,4,2,16,128]{5,4,3,2,1,0:T(8,128)S(1)}, u32[]{:S(2)}, u32[]{:S(2)}) %collective-permute-start.54) | collective-permute-done | bytes 262176 | tf_op jit(solution)/shard_map/back_0/ppermute | solution.py:318
  191.6 4.3 %collective-permute-start.40 = (f32[2,2,4,2,16,128]{5,4,3,2,1,0:T(8,128)S(1)}, f32[2,2,4,2,16,128]{5,4,3,2,1,0:T(8,128)S(1)}, u32[]{:S(2)}, u32[]{:S(2)}) collective-permute-start(f32[2,2,4,2,16,128]{5,4,3,2,1,0:T(8,128)S(1)} %pad_maximum_fusion.35), channel_id=1, source_target_pairs={{0,64},{32,96},{64,0},{96,32},{1,65},{33,97},{65,1},{97,33},{2,66}... | collective-permute-start | bytes 786440 | tf_op jit(solution)/shard_map/back_1/ppermute | solution.py:318
  196.6 4.2 %collective-permute-done.39 = f32[2,2,4,2,16,128]{5,4,3,2,1,0:T(8,128)S(1)} collective-permute-done((f32[2,2,4,2,16,128]{5,4,3,2,1,0:T(8,128)S(1)}, f32[2,2,4,2,16,128]{5,4,3,2,1,0:T(8,128)S(1)}, u32[]{:S(2)}, u32[]{:S(2)}) %collective-permute-start.39) | collective-permute-done | bytes 262176 | tf_op jit(solution)/shard_map/back_1/ppermute | solution.py:318
  200.8 7.8 %collective-permute-done.40 = f32[2,2,4,2,16,128]{5,4,3,2,1,0:T(8,128)S(1)} collective-permute-done((f32[2,2,4,2,16,128]{5,4,3,2,1,0:T(8,128)S(1)}, f32[2,2,4,2,16,128]{5,4,3,2,1,0:T(8,128)S(1)}, u32[]{:S(2)}, u32[]{:S(2)}) %collective-permute-start.40) | collective-permute-done | bytes 262176 | tf_op jit(solution)/shard_map/back_1/ppermute | solution.py:318
  208.6 3.9 %collective-permute-done.55 = f32[4,2,4,2,16,128]{5,4,3,2,1,0:T(8,128)S(1)} collective-permute-done((f32[4,2,4,2,16,128]{5,4,3,2,1,0:T(8,128)S(1)}, f32[4,2,4,2,16,128]{5,4,3,2,1,0:T(8,128)S(1)}, u32[]{:S(2)}, u32[]{:S(2)}) %collective-permute-start.55) | collective-permute-done | bytes 524320 | tf_op jit(solution)/shard_map/back_0/ppermute | solution.py:318
  212.5 2.8 %collective-permute-start.13 = (f32[2,2,4,2,16,128]{5,4,3,2,1,0:T(8,128)S(1)}, f32[2,2,4,2,16,128]{5,4,3,2,1,0:T(8,128)S(1)}, u32[]{:S(2)}, u32[]{:S(2)}) collective-permute-start(f32[2,2,4,2,16,128]{5,4,3,2,1,0:T(8,128)S(1)} %pad_maximum_fusion.18), channel_id=1, source_target_pairs={{0,96},{32,64},{64,32},{96,0},{1,97},{33,65},{65,33},{97,1},{2,98}... | collective-permute-start | bytes 786440 | tf_op jit(solution)/shard_map/back_3/ppermute | solution.py:318
  215.3 3.9 %rows_0.1.refs_7_ = f32[2,64,8192]{2,1,0:T(8,128)} custom-call(f32[64,16,128]{2,1,0:T(8,128)S(1)} %bitcast.111, f32[64,16,128]{2,1,0:T(8,128)S(1)} %bitcast.115, bf16[2,128,128]{2,1,0:T(8,128)(2,1)S(1)} %dynamic-slice_bitcast_fusion.refs_2_, f32[2,128,128]{2,1,0:T(8,128)S(1)} %copy-done.2, bf16[2,128,256]{2,1,0:T(8,128)(2,1)S(1)} %copy-done.1), custom_call_target="tpu_custom_call" | custom-call | flops 750000000 | bytes 2097152 | tf_op jit(solution)/shard_map/rows_0/pallas_call | solution.py:301
  219.2 3.9 %rows_1.1.refs_5_ = f32[2,64,8192]{2,1,0:T(8,128)} custom-call(f32[32,16,128]{2,1,0:T(8,128)S(1)} %bitcast.113, f32[32,16,128]{2,1,0:T(8,128)S(1)} %bitcast.116, f32[32,16,128]{2,1,0:T(8,128)S(1)} %bitcast.117, f32[32,16,128]{2,1,0:T(8,128)S(1)} %bitcast.119, ...), custom_call_target="tpu_custom_call", output_to_operand_aliasing={{}: (7, {})} | custom-call | flops 750000000 | bytes 2097152 | tf_op jit(solution)/shard_map/rows_1/pallas_call | solution.py:301
  223.1 3.9 %rows_2.1.refs_7_ = f32[2,64,8192]{2,1,0:T(8,128)} custom-call(f32[64,16,128]{2,1,0:T(8,128)S(1)} %bitcast.110, f32[64,16,128]{2,1,0:T(8,128)S(1)} %bitcast.114, bf16[2,128,128]{2,1,0:T(8,128)(2,1)S(1)} %dynamic-slice_bitcast_fusion.refs_2_, f32[2,128,128]{2,1,0:T(8,128)S(1)} %copy-done.2, ...), custom_call_target="tpu_custom_call", output_to_operand_aliasing={{}: (5, {})} | custom-call | flops 750000000 | bytes 2097152 | tf_op jit(solution)/shard_map/rows_2/pallas_call | solution.py:301
  227.1 3.9 %rows_3.1 = f32[2,64,8192]{2,1,0:T(8,128)} custom-call(f32[32,16,128]{2,1,0:T(8,128)S(1)} %bitcast.112, f32[32,16,128]{2,1,0:T(8,128)S(1)} %bitcast.118, f32[32,16,128]{2,1,0:T(8,128)S(1)} %bitcast.120, f32[32,16,128]{2,1,0:T(8,128)S(1)} %bitcast.121, bf16[2,128,128]{2,1,0:T(8,128)(2,1)S(1)} %dynamic-slice_bitcast_fusion.1.refs_4_, ...), custom_call_target="tpu_custom_call", output_to_operand_aliasing={{}: (7, {})} | custom-call | flops 750000000 | bytes 2097152 | tf_op jit(solution)/shard_map/rows_3/pallas_call | solution.py:301
  (215 shorter events, 49.0 us)
Async XLA Ops:
  16.7 17.1 %collective-permute-start.42 = (f32[4,4,2,16,128]{4,3,2,1,0:T(8,128)S(1)}, f32[4,4,2,16,128]{4,3,2,1,0:T(8,128)S(1)}, u32[]{:S(2)}, u32[]{:S(2)}) collective-permute-start(f32[4,4,2,16,128]{4,3,2,1,0:T(8,128)S(1)} %get-tuple-element.58), channel_id=1, source_target_pairs={{0,32},{32,0},{64,96},{96,64},{1,33},{33,1},{65,97},{97,65},{2,34}... | collective-permute-start | bytes 786440 | tf_op jit(solution)/shard_map/out_0/ppermute | solution.py:318
  18.3 16.4 %collective-permute-start.43 = (f32[4,4,2,16,128]{4,3,2,1,0:T(8,128)S(1)}, f32[4,4,2,16,128]{4,3,2,1,0:T(8,128)S(1)}, u32[]{:S(2)}, u32[]{:S(2)}) collective-permute-start(f32[4,4,2,16,128]{4,3,2,1,0:T(8,128)S(1)} %get-tuple-element.59), channel_id=1, source_target_pairs={{0,64},{32,96},{64,0},{96,32},{1,65},{33,97},{65,1},{97,33},{2,66}... | collective-permute-start | bytes 786440 | tf_op jit(solution)/shard_map/out_0/ppermute | solution.py:318
  21.1 17.0 %collective-permute-start.44 = (f32[4,4,2,16,128]{4,3,2,1,0:T(8,128)S(1)}, f32[4,4,2,16,128]{4,3,2,1,0:T(8,128)S(1)}, u32[]{:S(2)}, u32[]{:S(2)}) collective-permute-start(f32[4,4,2,16,128]{4,3,2,1,0:T(8,128)S(1)} %get-tuple-element.60), channel_id=1, source_target_pairs={{0,96},{32,64},{64,32},{96,0},{1,97},{33,65},{65,33},{97,1},{2,98}... | collective-permute-start | bytes 786440 | tf_op jit(solution)/shard_map/out_0/ppermute | solution.py:318
  24.1 18.0 %collective-permute-start.30 = (f32[4,4,2,16,128]{4,3,2,0,1:T(8,128)S(1)}, f32[4,4,2,16,128]{4,3,2,0,1:T(8,128)S(1)}, u32[]{:S(2)}, u32[]{:S(2)}) collective-permute-start(f32[4,4,2,16,128]{4,3,2,0,1:T(8,128)S(1)} %copy.68), channel_id=1, source_target_pairs={{0,20},{4,16},{16,4},{20,0},{1,21},{5,17},{17,5},{21,1},{2,22},{6,... | collective-permute-start | bytes 786440 | tf_op jit(solution)/shard_map/out_1/ppermute | solution.py:318
  28.3 13.8 %collective-permute-start.29 = (f32[4,4,2,16,128]{4,3,2,0,1:T(8,128)S(1)}, f32[4,4,2,16,128]{4,3,2,0,1:T(8,128)S(1)}, u32[]{:S(2)}, u32[]{:S(2)}) collective-permute-start(f32[4,4,2,16,128]{4,3,2,0,1:T(8,128)S(1)} %copy.67), channel_id=1, source_target_pairs={{0,16},{4,20},{16,0},{20,4},{1,17},{5,21},{17,1},{21,5},{2,18},{6,... | collective-permute-start | bytes 786440 | tf_op jit(solution)/shard_map/out_1/ppermute | solution.py:318
  34.7 15.8 %collective-permute-start.2 = (f32[4,4,2,16,128]{4,3,2,0,1:T(8,128)S(1)}, f32[4,4,2,16,128]{4,3,2,0,1:T(8,128)S(1)}, u32[]{:S(2)}, u32[]{:S(2)}) collective-permute-start(f32[4,4,2,16,128]{4,3,2,0,1:T(8,128)S(1)} %copy.61), channel_id=1, source_target_pairs={{0,20},{4,16},{16,4},{20,0},{1,21},{5,17},{17,5},{21,1},{2,22},{6,... | collective-permute-start | bytes 786440 | tf_op jit(solution)/shard_map/out_3/ppermute | solution.py:318
  38.1 15.4 %collective-permute-start.1 = (f32[4,4,2,16,128]{4,3,2,0,1:T(8,128)S(1)}, f32[4,4,2,16,128]{4,3,2,0,1:T(8,128)S(1)}, u32[]{:S(2)}, u32[]{:S(2)}) collective-permute-start(f32[4,4,2,16,128]{4,3,2,0,1:T(8,128)S(1)} %copy.60), channel_id=1, source_target_pairs={{0,16},{4,20},{16,0},{20,4},{1,17},{5,21},{17,1},{21,5},{2,18},{6,... | collective-permute-start | bytes 786440 | tf_op jit(solution)/shard_map/out_3/ppermute | solution.py:318
  42.1 13.3 %collective-permute-start = (f32[4,4,2,16,128]{4,3,2,0,1:T(8,128)S(1)}, f32[4,4,2,16,128]{4,3,2,0,1:T(8,128)S(1)}, u32[]{:S(2)}, u32[]{:S(2)}) collective-permute-start(f32[4,4,2,16,128]{4,3,2,0,1:T(8,128)S(1)} %copy.59), channel_id=1, source_target_pairs={{0,4},{4,0},{16,20},{20,16},{1,5},{5,1},{17,21},{21,17},{2,6},{6,2... | collective-permute-start | bytes 786440 | tf_op jit(solution)/shard_map/out_3/ppermute | solution.py:318
  42.1 16.3 %collective-permute-start.14 = (f32[4,4,2,16,128]{4,3,2,1,0:T(8,128)S(1)}, f32[4,4,2,16,128]{4,3,2,1,0:T(8,128)S(1)}, u32[]{:S(2)}, u32[]{:S(2)}) collective-permute-start(f32[4,4,2,16,128]{4,3,2,1,0:T(8,128)S(1)} %get-tuple-element.44), channel_id=1, source_target_pairs={{0,32},{32,0},{64,96},{96,64},{1,33},{33,1},{65,97},{97,65},{2,34}... | collective-permute-start | bytes 786440 | tf_op jit(solution)/shard_map/out_2/ppermute | solution.py:318
  42.5 16.3 %collective-permute-start.15 = (f32[4,4,2,16,128]{4,3,2,1,0:T(8,128)S(1)}, f32[4,4,2,16,128]{4,3,2,1,0:T(8,128)S(1)}, u32[]{:S(2)}, u32[]{:S(2)}) collective-permute-start(f32[4,4,2,16,128]{4,3,2,1,0:T(8,128)S(1)} %get-tuple-element.45), channel_id=1, source_target_pairs={{0,64},{32,96},{64,0},{96,32},{1,65},{33,97},{65,1},{97,33},{2,66}... | collective-permute-start | bytes 786440 | tf_op jit(solution)/shard_map/out_2/ppermute | solution.py:318
  55.4 13.3 %collective-permute-start.46 = (f32[4,4,2,16,128]{4,3,2,1,0:T(8,128)S(1)}, f32[4,4,2,16,128]{4,3,2,1,0:T(8,128)S(1)}, u32[]{:S(2)}, u32[]{:S(2)}) collective-permute-start(f32[4,4,2,16,128]{4,3,2,1,0:T(8,128)S(1)} %pad_maximum_fusion.39), channel_id=1, source_target_pairs={{0,2},{1,3},{2,0},{3,1},{4,6},{5,7},{6,4},{7,5},{8,10},{9,11},{10,... | collective-permute-start | bytes 786440 | tf_op jit(solution)/shard_map/out_0/ppermute | solution.py:318
  58.4 43.0 %collective-permute-start.47 = (f32[4,4,2,16,128]{4,3,2,1,0:T(8,128)S(1)}, f32[4,4,2,16,128]{4,3,2,1,0:T(8,128)S(1)}, u32[]{:S(2)}, u32[]{:S(2)}) collective-permute-start(f32[4,4,2,16,128]{4,3,2,1,0:T(8,128)S(1)} %pad_maximum_fusion.40), channel_id=1, source_target_pairs={{0,3},{1,2},{2,1},{3,0},{4,7},{5,6},{6,5},{7,4},{8,11},{9,10},{10,... | collective-permute-start | bytes 786440 | tf_op jit(solution)/shard_map/out_0/ppermute | solution.py:318
  58.8 46.1 %collective-permute-start.31 = (f32[4,4,2,16,128]{4,3,2,0,1:T(8,128)S(1)}, f32[4,4,2,16,128]{4,3,2,0,1:T(8,128)S(1)}, u32[]{:S(2)}, u32[]{:S(2)}) collective-permute-start(f32[4,4,2,16,128]{4,3,2,0,1:T(8,128)S(1)} %pad_maximum_fusion.27), channel_id=1, source_target_pairs={{0,32},{32,0},{64,96},{96,64},{1,33},{33,1},{65,97},{97,65},{2,34}... | collective-permute-start | bytes 786440 | tf_op jit(solution)/shard_map/out_1/ppermute | solution.py:318
  60.0 45.0 %collective-permute-start.32 = (f32[4,4,2,16,128]{4,3,2,0,1:T(8,128)S(1)}, f32[4,4,2,16,128]{4,3,2,0,1:T(8,128)S(1)}, u32[]{:S(2)}, u32[]{:S(2)}) collective-permute-start(f32[4,4,2,16,128]{4,3,2,0,1:T(8,128)S(1)} %pad_maximum_fusion.28), channel_id=1, source_target_pairs={{0,64},{32,96},{64,0},{96,32},{1,65},{33,97},{65,1},{97,33},{2,66}... | collective-permute-start | bytes 786440 | tf_op jit(solution)/shard_map/out_1/ppermute | solution.py:318
  63.0 15.9 %collective-permute-start.3 = (f32[4,4,2,16,128]{4,3,2,0,1:T(8,128)S(1)}, f32[4,4,2,16,128]{4,3,2,0,1:T(8,128)S(1)}, u32[]{:S(2)}, u32[]{:S(2)}) collective-permute-start(f32[4,4,2,16,128]{4,3,2,0,1:T(8,128)S(1)} %pad_maximum_fusion.9), channel_id=1, source_target_pairs={{0,32},{32,0},{64,96},{96,64},{1,33},{33,1},{65,97},{97,65},{2,34}... | collective-permute-start | bytes 786440 | tf_op jit(solution)/shard_map/out_3/ppermute | solution.py:318
  68.6 13.6 %collective-permute-start.4 = (f32[4,4,2,16,128]{4,3,2,0,1:T(8,128)S(1)}, f32[4,4,2,16,128]{4,3,2,0,1:T(8,128)S(1)}, u32[]{:S(2)}, u32[]{:S(2)}) collective-permute-start(f32[4,4,2,16,128]{4,3,2,0,1:T(8,128)S(1)} %pad_maximum_fusion.10), channel_id=1, source_target_pairs={{0,64},{32,96},{64,0},{96,32},{1,65},{33,97},{65,1},{97,33},{2,66}... | collective-permute-start | bytes 786440 | tf_op jit(solution)/shard_map/out_3/ppermute | solution.py:318
  86.7 9.9 %collective-permute-start.18 = (f32[4,4,2,16,128]{4,3,2,1,0:T(8,128)S(1)}, f32[4,4,2,16,128]{4,3,2,1,0:T(8,128)S(1)}, u32[]{:S(2)}, u32[]{:S(2)}) collective-permute-start(f32[4,4,2,16,128]{4,3,2,1,0:T(8,128)S(1)} %pad_maximum_fusion.21), channel_id=1, source_target_pairs={{0,2},{1,3},{2,0},{3,1},{4,6},{5,7},{6,4},{7,5},{8,10},{9,11},{10,... | collective-permute-start | bytes 786440 | tf_op jit(solution)/shard_map/out_2/ppermute | solution.py:318
  89.2 11.6 %collective-permute-start.19 = (f32[4,4,2,16,128]{4,3,2,1,0:T(8,128)S(1)}, f32[4,4,2,16,128]{4,3,2,1,0:T(8,128)S(1)}, u32[]{:S(2)}, u32[]{:S(2)}) collective-permute-start(f32[4,4,2,16,128]{4,3,2,1,0:T(8,128)S(1)} %pad_maximum_fusion.22), channel_id=1, source_target_pairs={{0,3},{1,2},{2,1},{3,0},{4,7},{5,6},{6,5},{7,4},{8,11},{9,10},{10,... | collective-permute-start | bytes 786440 | tf_op jit(solution)/shard_map/out_2/ppermute | solution.py:318
  96.7 14.7 %collective-permute-start.33 = (f32[4,4,2,16,128]{4,3,2,0,1:T(8,128)S(1)}, f32[4,4,2,16,128]{4,3,2,0,1:T(8,128)S(1)}, u32[]{:S(2)}, u32[]{:S(2)}) collective-permute-start(f32[4,4,2,16,128]{4,3,2,0,1:T(8,128)S(1)} %pad_maximum_fusion.29), channel_id=1, source_target_pairs={{0,96},{32,64},{64,32},{96,0},{1,97},{33,65},{65,33},{97,1},{2,98}... | collective-permute-start | bytes 786440 | tf_op jit(solution)/shard_map/out_1/ppermute | solution.py:318
  100.8 10.8 %collective-permute-start.6 = (f32[4,4,2,16,128]{4,3,2,1,0:T(8,128)S(1)}, f32[4,4,2,16,128]{4,3,2,1,0:T(8,128)S(1)}, u32[]{:S(2)}, u32[]{:S(2)}) collective-permute-start(f32[4,4,2,16,128]{4,3,2,1,0:T(8,128)S(1)} %pad_maximum_fusion.12), channel_id=1, source_target_pairs={{0,1},{1,0},{2,3},{3,2},{4,5},{5,4},{6,7},{7,6},{8,9},{9,8},{10,11... | collective-permute-start | bytes 786440 | tf_op jit(solution)/shard_map/out_3/ppermute | solution.py:318
  101.5 26.2 %collective-permute-start.7 = (f32[4,4,2,16,128]{4,3,2,1,0:T(8,128)S(1)}, f32[4,4,2,16,128]{4,3,2,1,0:T(8,128)S(1)}, u32[]{:S(2)}, u32[]{:S(2)}) collective-permute-start(f32[4,4,2,16,128]{4,3,2,1,0:T(8,128)S(1)} %pad_maximum_fusion.13), channel_id=1, source_target_pairs={{0,2},{1,3},{2,0},{3,1},{4,6},{5,7},{6,4},{7,5},{8,10},{9,11},{10,... | collective-permute-start | bytes 786440 | tf_op jit(solution)/shard_map/out_3/ppermute | solution.py:318
  105.0 17.5 %collective-permute-start.21 = (f32[4,4,2,16,128]{4,3,2,1,0:T(8,128)S(1)}, f32[4,4,2,16,128]{4,3,2,1,0:T(8,128)S(1)}, u32[]{:S(2)}, u32[]{:S(2)}) collective-permute-start(f32[4,4,2,16,128]{4,3,2,1,0:T(8,128)S(1)} %pad_maximum_fusion.24), channel_id=1, source_target_pairs={{0,16},{4,20},{16,0},{20,4},{1,17},{5,21},{17,1},{21,5},{2,18},{6,... | collective-permute-start | bytes 786440 | tf_op jit(solution)/shard_map/out_2/ppermute | solution.py:318
  111.3 14.0 %collective-permute-start.22 = (f32[4,4,2,16,128]{4,3,2,1,0:T(8,128)S(1)}, f32[4,4,2,16,128]{4,3,2,1,0:T(8,128)S(1)}, u32[]{:S(2)}, u32[]{:S(2)}) collective-permute-start(f32[4,4,2,16,128]{4,3,2,1,0:T(8,128)S(1)} %pad_maximum_fusion.25), channel_id=1, source_target_pairs={{0,20},{4,16},{16,4},{20,0},{1,21},{5,17},{17,5},{21,1},{2,22},{6,... | collective-permute-start | bytes 786440 | tf_op jit(solution)/shard_map/out_2/ppermute | solution.py:318
  111.6 16.2 %collective-permute-start.8 = (f32[4,4,2,16,128]{4,3,2,1,0:T(8,128)S(1)}, f32[4,4,2,16,128]{4,3,2,1,0:T(8,128)S(1)}, u32[]{:S(2)}, u32[]{:S(2)}) collective-permute-start(f32[4,4,2,16,128]{4,3,2,1,0:T(8,128)S(1)} %pad_maximum_fusion.14), channel_id=1, source_target_pairs={{0,3},{1,2},{2,1},{3,0},{4,7},{5,6},{6,5},{7,4},{8,11},{9,10},{10,... | collective-permute-start | bytes 786440 | tf_op jit(solution)/shard_map/out_3/ppermute | solution.py:318
  114.0 14.0 %collective-permute-start.34 = (f32[4,4,2,16,128]{4,3,2,1,0:T(8,128)S(1)}, f32[4,4,2,16,128]{4,3,2,1,0:T(8,128)S(1)}, u32[]{:S(2)}, u32[]{:S(2)}) collective-permute-start(f32[4,4,2,16,128]{4,3,2,1,0:T(8,128)S(1)} %pad_maximum_fusion.30), channel_id=1, source_target_pairs={{0,1},{1,0},{2,3},{3,2},{4,5},{5,4},{6,7},{7,6},{8,9},{9,8},{10,11... | collective-permute-start | bytes 786440 | tf_op jit(solution)/shard_map/out_1/ppermute | solution.py:318
  125.3 10.9 %collective-permute-start.36 = (f32[4,4,2,16,128]{4,3,2,1,0:T(8,128)S(1)}, f32[4,4,2,16,128]{4,3,2,1,0:T(8,128)S(1)}, u32[]{:S(2)}, u32[]{:S(2)}) collective-permute-start(f32[4,4,2,16,128]{4,3,2,1,0:T(8,128)S(1)} %pad_maximum_fusion.32), channel_id=1, source_target_pairs={{0,3},{1,2},{2,1},{3,0},{4,7},{5,6},{6,5},{7,4},{8,11},{9,10},{10,... | collective-permute-start | bytes 786440 | tf_op jit(solution)/shard_map/out_1/ppermute | solution.py:318
  127.7 11.4 %collective-permute-start.48 = (f32[4,4,2,16,128]{4,3,2,1,0:T(8,128)S(1)}, f32[4,4,2,16,128]{4,3,2,1,0:T(8,128)S(1)}, u32[]{:S(2)}, u32[]{:S(2)}) collective-permute-start(f32[4,4,2,16,128]{4,3,2,1,0:T(8,128)S(1)} %pad_maximum_fusion.41), channel_id=1, source_target_pairs={{0,4},{4,0},{16,20},{20,16},{1,5},{5,1},{17,21},{21,17},{2,6},{6,2... | collective-permute-start | bytes 786440 | tf_op jit(solution)/shard_map/out_0/ppermute | solution.py:318
  127.8 27.8 %collective-permute-start.23 = (f32[4,4,4,2,16,128]{5,4,3,2,1,0:T(8,128)S(1)}, f32[4,4,4,2,16,128]{5,4,3,2,1,0:T(8,128)}, u32[]{:S(2)}, u32[]{:S(2)}) collective-permute-start(f32[4,4,4,2,16,128]{5,4,3,2,1,0:T(8,128)S(1)} %pad_maximum_fusion.1.mine), channel_id=1, source_target_pairs={{0,8},{8,0},{1,9},{9,1},{2,10},{10,2},{3,11},{11,3},{4,12},{12,4},... | collective-permute-start | bytes 3145736 | tf_op jit(solution)/shard_map/out_2/ppermute | solution.py:318
  128.0 33.5 %collective-permute-start.9 = (f32[4,4,4,2,16,128]{5,4,3,2,1,0:T(8,128)S(1)}, f32[4,4,4,2,16,128]{5,4,3,2,1,0:T(8,128)}, u32[]{:S(2)}, u32[]{:S(2)}) collective-permute-start(f32[4,4,4,2,16,128]{5,4,3,2,1,0:T(8,128)S(1)} %pad_maximum_fusion.mine), channel_id=1, source_target_pairs={{0,8},{8,0},{1,9},{9,1},{2,10},{10,2},{3,11},{11,3},{4,12},{12,4},... | collective-permute-start | bytes 3145736 | tf_op jit(solution)/shard_map/out_3/ppermute | solution.py:318
  136.4 27.3 %collective-permute-start.37 = (f32[4,4,4,2,16,128]{5,4,3,2,1,0:T(8,128)S(1)}, f32[4,4,4,2,16,128]{5,4,3,2,1,0:T(8,128)}, u32[]{:S(2)}, u32[]{:S(2)}) collective-permute-start(f32[4,4,4,2,16,128]{5,4,3,2,1,0:T(8,128)S(1)} %pad_maximum_fusion.2.mine), channel_id=1, source_target_pairs={{0,8},{8,0},{1,9},{9,1},{2,10},{10,2},{3,11},{11,3},{4,12},{12,4},... | collective-permute-start | bytes 3145736 | tf_op jit(solution)/shard_map/out_1/ppermute | solution.py:318
  136.5 10.5 %collective-permute-start.49 = (f32[4,4,2,16,128]{4,3,2,1,0:T(8,128)S(1)}, f32[4,4,2,16,128]{4,3,2,1,0:T(8,128)}, u32[]{:S(2)}, u32[]{:S(2)}) collective-permute-start(f32[4,4,2,16,128]{4,3,2,1,0:T(8,128)S(1)} %pad_maximum_fusion.42), channel_id=1, source_target_pairs={{0,16},{4,20},{16,0},{20,4},{1,17},{5,21},{17,1},{21,5},{2,18},{6,... | collective-permute-start | bytes 786440 | tf_op jit(solution)/shard_map/out_0/ppermute | solution.py:318
  139.9 12.6 %collective-permute-start.50 = (f32[4,4,2,16,128]{4,3,2,1,0:T(8,128)}, f32[4,4,2,16,128]{4,3,2,1,0:T(8,128)}, u32[]{:S(2)}, u32[]{:S(2)}) collective-permute-start(f32[4,4,2,16,128]{4,3,2,1,0:T(8,128)} %pad_maximum_fusion.43), channel_id=1, source_target_pairs={{0,20},{4,16},{16,4},{20,0},{1,21},{5,17},{17,5},{21,1},{2,22},{6,... | collective-permute-start | bytes 786440 | tf_op jit(solution)/shard_map/out_0/ppermute | solution.py:318
  153.8 13.7 %collective-permute-start.51 = (f32[4,4,4,2,16,128]{5,4,3,2,1,0:T(8,128)S(1)}, f32[4,4,4,2,16,128]{5,4,3,2,1,0:T(8,128)S(1)}, u32[]{:S(2)}, u32[]{:S(2)}) collective-permute-start(f32[4,4,4,2,16,128]{5,4,3,2,1,0:T(8,128)S(1)} %pad_maximum_fusion.3.mine), channel_id=1, source_target_pairs={{0,8},{8,0},{1,9},{9,1},{2,10},{10,2},{3,11},{11,3},{4,12},{12,4},... | collective-permute-start | bytes 3145736 | tf_op jit(solution)/shard_map/out_0/ppermute | solution.py:318
  157.3 12.9 %collective-permute-start.24 = (f32[2,2,4,2,16,128]{5,4,3,2,1,0:T(8,128)S(1)}, f32[2,2,4,2,16,128]{5,4,3,2,1,0:T(8,128)S(1)}, u32[]{:S(2)}, u32[]{:S(2)}) collective-permute-start(f32[2,2,4,2,16,128]{5,4,3,2,1,0:T(8,128)S(1)} %get-tuple-element.48), channel_id=1, source_target_pairs={{0,32},{32,0},{64,96},{96,64},{1,33},{33,1},{65,97},{97,65},{2,34}... | collective-permute-start | bytes 786440 | tf_op jit(solution)/shard_map/back_2/ppermute | solution.py:318
  158.4 15.5 %collective-permute-start.25 = (f32[2,2,4,2,16,128]{5,4,3,2,1,0:T(8,128)S(1)}, f32[2,2,4,2,16,128]{5,4,3,2,1,0:T(8,128)S(1)}, u32[]{:S(2)}, u32[]{:S(2)}) collective-permute-start(f32[2,2,4,2,16,128]{5,4,3,2,1,0:T(8,128)S(1)} %get-tuple-element.49), channel_id=1, source_target_pairs={{0,64},{32,96},{64,0},{96,32},{1,65},{33,97},{65,1},{97,33},{2,66}... | collective-permute-start | bytes 786440 | tf_op jit(solution)/shard_map/back_2/ppermute | solution.py:318
  161.6 14.9 %collective-permute-start.26 = (f32[2,2,4,2,16,128]{5,4,3,2,1,0:T(8,128)S(1)}, f32[2,2,4,2,16,128]{5,4,3,2,1,0:T(8,128)S(1)}, u32[]{:S(2)}, u32[]{:S(2)}) collective-permute-start(f32[2,2,4,2,16,128]{5,4,3,2,1,0:T(8,128)S(1)} %get-tuple-element.50), channel_id=1, source_target_pairs={{0,96},{32,64},{64,32},{96,0},{1,97},{33,65},{65,33},{97,1},{2,98}... | collective-permute-start | bytes 786440 | tf_op jit(solution)/shard_map/back_2/ppermute | solution.py:318
  163.7 32.1 %collective-permute-start.10 = (f32[4,2,4,2,16,128]{5,4,3,2,1,0:T(8,128)S(1)}, f32[4,2,4,2,16,128]{5,4,3,2,1,0:T(8,128)S(1)}, u32[]{:S(2)}, u32[]{:S(2)}) collective-permute-start(f32[4,2,4,2,16,128]{5,4,3,2,1,0:T(8,128)S(1)} %get-tuple-element.42), channel_id=1, source_target_pairs={{0,16},{16,0},{1,17},{17,1},{2,18},{18,2},{3,19},{19,3},{4,20},{20... | collective-permute-start | bytes 1572872 | tf_op jit(solution)/shard_map/back_3/ppermute | solution.py:318
  167.4 24.0 %collective-permute-start.38 = (f32[4,2,4,2,16,128]{5,4,3,2,1,0:T(8,128)S(1)}, f32[4,2,4,2,16,128]{5,4,3,2,1,0:T(8,128)S(1)}, u32[]{:S(2)}, u32[]{:S(2)}) collective-permute-start(f32[4,2,4,2,16,128]{5,4,3,2,1,0:T(8,128)S(1)} %get-tuple-element.56), channel_id=1, source_target_pairs={{0,16},{16,0},{1,17},{17,1},{2,18},{18,2},{3,19},{19,3},{4,20},{20... | collective-permute-start | bytes 1572872 | tf_op jit(solution)/shard_map/back_1/ppermute | solution.py:318
  170.2 9.5 %collective-permute-start.52 = (f32[2,2,4,2,16,128]{5,4,3,2,1,0:T(8,128)S(1)}, f32[2,2,4,2,16,128]{5,4,3,2,1,0:T(8,128)S(1)}, u32[]{:S(2)}, u32[]{:S(2)}) collective-permute-start(f32[2,2,4,2,16,128]{5,4,3,2,1,0:T(8,128)S(1)} %get-tuple-element.62), channel_id=1, source_target_pairs={{0,32},{32,0},{64,96},{96,64},{1,33},{33,1},{65,97},{97,65},{2,34}... | collective-permute-start | bytes 786440 | tf_op jit(solution)/shard_map/back_0/ppermute | solution.py:318
  173.9 11.7 %collective-permute-start.53 = (f32[2,2,4,2,16,128]{5,4,3,2,1,0:T(8,128)S(1)}, f32[2,2,4,2,16,128]{5,4,3,2,1,0:T(8,128)S(1)}, u32[]{:S(2)}, u32[]{:S(2)}) collective-permute-start(f32[2,2,4,2,16,128]{5,4,3,2,1,0:T(8,128)S(1)} %get-tuple-element.63), channel_id=1, source_target_pairs={{0,64},{32,96},{64,0},{96,32},{1,65},{33,97},{65,1},{97,33},{2,66}... | collective-permute-start | bytes 786440 | tf_op jit(solution)/shard_map/back_0/ppermute | solution.py:318
  176.5 13.4 %collective-permute-start.54 = (f32[2,2,4,2,16,128]{5,4,3,2,1,0:T(8,128)S(1)}, f32[2,2,4,2,16,128]{5,4,3,2,1,0:T(8,128)S(1)}, u32[]{:S(2)}, u32[]{:S(2)}) collective-permute-start(f32[2,2,4,2,16,128]{5,4,3,2,1,0:T(8,128)S(1)} %get-tuple-element.64), channel_id=1, source_target_pairs={{0,96},{32,64},{64,32},{96,0},{1,97},{33,65},{65,33},{97,1},{2,98}... | collective-permute-start | bytes 786440 | tf_op jit(solution)/shard_map/back_0/ppermute | solution.py:318
  179.7 43.4 %collective-permute-start.27 = (f32[4,2,4,2,16,128]{5,4,3,2,1,0:T(8,128)S(1)}, f32[4,2,4,2,16,128]{5,4,3,2,1,0:T(8,128)S(1)}, u32[]{:S(2)}, u32[]{:S(2)}) collective-permute-start(f32[4,2,4,2,16,128]{5,4,3,2,1,0:T(8,128)S(1)} %pad_maximum_fusion.5), channel_id=1, source_target_pairs={{0,16},{16,0},{1,17},{17,1},{2,18},{18,2},{3,19},{19,3},{4,20},{20... | collective-permute-start | bytes 1572872 | tf_op jit(solution)/shard_map/back_2/ppermute | solution.py:318
  190.0 22.5 %collective-permute-start.55 = (f32[4,2,4,2,16,128]{5,4,3,2,1,0:T(8,128)S(1)}, f32[4,2,4,2,16,128]{5,4,3,2,1,0:T(8,128)S(1)}, u32[]{:S(2)}, u32[]{:S(2)}) collective-permute-start(f32[4,2,4,2,16,128]{5,4,3,2,1,0:T(8,128)S(1)} %pad_maximum_fusion.7), channel_id=1, source_target_pairs={{0,16},{16,0},{1,17},{17,1},{2,18},{18,2},{3,19},{19,3},{4,20},{20... | collective-permute-start | bytes 1572872 | tf_op jit(solution)/shard_map/back_0/ppermute | solution.py:318
  191.6 17.0 %collective-permute-start.40 = (f32[2,2,4,2,16,128]{5,4,3,2,1,0:T(8,128)S(1)}, f32[2,2,4,2,16,128]{5,4,3,2,1,0:T(8,128)S(1)}, u32[]{:S(2)}, u32[]{:S(2)}) collective-permute-start(f32[2,2,4,2,16,128]{5,4,3,2,1,0:T(8,128)S(1)} %pad_maximum_fusion.35), channel_id=1, source_target_pairs={{0,64},{32,96},{64,0},{96,32},{1,65},{33,97},{65,1},{97,33},{2,66}... | collective-permute-start | bytes 786440 | tf_op jit(solution)/shard_map/back_1/ppermute | solution.py:318
  195.9 23.3 %collective-permute-start.41 = (f32[2,2,4,2,16,128]{5,4,3,2,1,0:T(8,128)S(1)}, f32[2,2,4,2,16,128]{5,4,3,2,1,0:T(8,128)S(1)}, u32[]{:S(2)}, u32[]{:S(2)}) collective-permute-start(f32[2,2,4,2,16,128]{5,4,3,2,1,0:T(8,128)S(1)} %pad_maximum_fusion.36), channel_id=1, source_target_pairs={{0,96},{32,64},{64,32},{96,0},{1,97},{33,65},{65,33},{97,1},{2,98}... | collective-permute-start | bytes 786440 | tf_op jit(solution)/shard_map/back_1/ppermute | solution.py:318
  200.8 26.3 %collective-permute-start.11 = (f32[2,2,4,2,16,128]{5,4,3,2,1,0:T(8,128)S(1)}, f32[2,2,4,2,16,128]{5,4,3,2,1,0:T(8,128)S(1)}, u32[]{:S(2)}, u32[]{:S(2)}) collective-permute-start(f32[2,2,4,2,16,128]{5,4,3,2,1,0:T(8,128)S(1)} %pad_maximum_fusion.16), channel_id=1, source_target_pairs={{0,32},{32,0},{64,96},{96,64},{1,33},{33,1},{65,97},{97,65},{2,34}... | collective-permute-start | bytes 786440 | tf_op jit(solution)/shard_map/back_3/ppermute | solution.py:318
  208.6 18.5 %collective-permute-start.12 = (f32[2,2,4,2,16,128]{5,4,3,2,1,0:T(8,128)S(1)}, f32[2,2,4,2,16,128]{5,4,3,2,1,0:T(8,128)S(1)}, u32[]{:S(2)}, u32[]{:S(2)}) collective-permute-start(f32[2,2,4,2,16,128]{5,4,3,2,1,0:T(8,128)S(1)} %pad_maximum_fusion.17), channel_id=1, source_target_pairs={{0,64},{32,96},{64,0},{96,32},{1,65},{33,97},{65,1},{97,33},{2,66}... | collective-permute-start | bytes 786440 | tf_op jit(solution)/shard_map/back_3/ppermute | solution.py:318
  212.5 14.6 %collective-permute-start.13 = (f32[2,2,4,2,16,128]{5,4,3,2,1,0:T(8,128)S(1)}, f32[2,2,4,2,16,128]{5,4,3,2,1,0:T(8,128)S(1)}, u32[]{:S(2)}, u32[]{:S(2)}) collective-permute-start(f32[2,2,4,2,16,128]{5,4,3,2,1,0:T(8,128)S(1)} %pad_maximum_fusion.18), channel_id=1, source_target_pairs={{0,96},{32,64},{64,32},{96,0},{1,97},{33,65},{65,33},{97,1},{2,98}... | collective-permute-start | bytes 786440 | tf_op jit(solution)/shard_map/back_3/ppermute | solution.py:318
  (19 other events, 131.1 us)

commit v2 on v0

v2 whole, which is shorter than its diff:
```python
import functools
import math

import jax
import jax.numpy as jnp
import ml_dtypes
import numpy as np
from jax import lax
from jax.experimental import pallas as pl
from jax.experimental.pallas import tpu as pltpu
from jax.sharding import Mesh, PartitionSpec as P

N = 8192
M = 8192
LOCAL = 512
WIDTH = 1024
BLOCK = 256
STEPS = WIDTH // BLOCK

AXES = ("x", "zh", "core", "zl", "y")
SIZES = (4, 2, 2, 2, 4)

F32 = jnp.float32
BF16 = jnp.bfloat16


def halves(table):
    high = table.astype(np.float32).astype(ml_dtypes.bfloat16)
    low = (table - high.astype(np.float64)).astype(np.float32).astype(ml_dtypes.bfloat16)
    return high, low


def split(value):
    high = value.astype(BF16)
    low = (value - high.astype(F32)).astype(BF16)
    return high, low


def column_table():
    row = 4 * np.arange(128)[None, :, None] + np.arange(4)[:, None, None]
    angle = 2.0 * np.pi * (row * np.arange(128) % LOCAL) / LOCAL
    return np.stack([np.cos(angle), np.sin(angle)]).astype(np.float32)


def row_tables():
    place = 8 * (4 * np.arange(2)[None, None, :] + np.arange(4)[None, :, None]) + np.arange(8)[:, None, None]
    angle = 2.0 * np.pi * (np.arange(64)[:, None] * place.reshape(1, 64) % 64) / 64
    cosine, sine = np.cos(angle), np.sin(angle)
    real_part = np.stack([cosine, sine], -1).reshape(64, 128)
    imag_part = np.stack([-sine, cosine], -1).reshape(64, 128)
    high, low = halves(np.concatenate([real_part, imag_part], 0))
    first = np.concatenate([np.concatenate([high, high], 1), np.concatenate([low, np.zeros_like(low)], 1)], 0)
    angle = 2.0 * np.pi * (np.outer(np.arange(128), np.arange(128)) % M) / M
    twist = np.stack([np.cos(angle), -np.sin(angle)]).astype(np.float32)
    angle = 2.0 * np.pi * (np.outer(np.arange(128), np.arange(64)) % 64) / 64
    cosine, sine = np.cos(angle), np.sin(angle)
    last = np.concatenate([np.concatenate([cosine, -sine], 1), np.concatenate([sine, cosine], 1)], 0)
    return first, twist, np.concatenate(halves(last), 1)


def sine_polynomials():
    nodes = 0.25 * np.cos(np.pi * (np.arange(400) + 0.5) / 800)
    square = np.polynomial.chebyshev.Chebyshev.fit(
        nodes**2, np.sin(2 * np.pi * nodes) / nodes, 4, domain=[0, 1 / 16]
    ).convert(kind=np.polynomial.Polynomial, domain=[-1, 1], window=[-1, 1])
    cosine = np.polynomial.chebyshev.Chebyshev.fit(
        nodes**2, np.cos(2 * np.pi * nodes), 5, domain=[0, 1 / 16]
    ).convert(kind=np.polynomial.Polynomial, domain=[-1, 1], window=[-1, 1])
    return [float(c) for c in square.coef], [float(c) for c in cosine.coef]


SINE, COSINE = sine_polynomials()


def horner(coefficients, value):
    total = jnp.full_like(value, coefficients[-1])
    for coefficient in coefficients[-2::-1]:
        total = total * value + coefficient
    return total


def dot(a, b):
    return jnp.dot(a, b, preferred_element_type=F32)


def draw(bits_0, bits_1, eigen):
    uniform = (bits_0.astype(F32) + 0.5) * 2.0**-12
    radius = jnp.sqrt(jnp.log(uniform) * eigen * (-2.0 / (N * M)))
    past = (bits_1.astype(F32) - 2047.5) * 2.0**-12
    h = jnp.abs(past) - 0.25
    square = h * h
    value_re = radius * (h * horner(SINE, square))
    value_im = jnp.where(past > 0, -radius, radius) * horner(COSINE, square)
    return value_re, value_im


def add(a, b):
    return a[0] + b[0], a[1] + b[1]


def sub(a, b):
    return a[0] - b[0], a[1] - b[1]


def turn_back(a):
    return a[1], -a[0]


def dft_4(a, b, c, d):
    even, odd = add(a, c), add(b, d)
    less, turned = sub(a, c), turn_back(sub(b, d))
    return add(even, odd), add(less, turned), sub(even, odd), sub(less, turned)


def spin(a, step):
    if step == 0:
        return a
    if step == 4:
        return turn_back(a)
    if step % 4 == 2:
        root = math.sqrt(0.5)
        a = ((a[0] + a[1]) * root, (a[1] - a[0]) * root)
        return a if step == 2 else turn_back(a)
    c, s = math.cos(math.pi * step / 8), math.sin(math.pi * step / 8)
    return a[0] * c + a[1] * s, a[1] * c - a[0] * s


def dft_16(v):
    first = [dft_4(v[e], v[4 + e], v[8 + e], v[12 + e]) for e in range(4)]
    second = [dft_4(*(spin(first[e][s], e * s) for e in range(4))) for s in range(4)]
    return [second[k % 4][k // 4] for k in range(16)]


def front_kernel(noise, eigen, base, turn, out, bits, eig, base_in, turn_in, tables, high, low, arrived):
    step = pl.program_id(0)

    def copies():
        for i in range(STEPS):
            columns = slice(BLOCK * i, BLOCK * (i + 1))
            yield pltpu.make_async_copy(noise.at[:, :, columns], bits.at[i], arrived.at[i])
            yield pltpu.make_async_copy(eigen.at[:, columns], eig.at[i], arrived.at[STEPS + i])
        yield pltpu.make_async_copy(base, base_in, arrived.at[2 * STEPS])
        yield pltpu.make_async_copy(turn, turn_in, arrived.at[2 * STEPS + 1])

    moves = list(copies())

    def start():
        for move in moves:
            move.start()

    def prepare():
        moves[-2].wait()
        moves[-1].wait()
        for r in range(4):
            cosine = base_in[0, r] * turn_in[0, r] - base_in[1, r] * turn_in[1, r]
            sine = base_in[1, r] * turn_in[0, r] + base_in[0, r] * turn_in[1, r]
            (cosine, cosine_low), (sine, sine_low) = split(cosine), split(sine)
            for at, c, s in ((0, cosine, sine), (256, cosine_low, sine_low)):
                tables[r, at : at + 128, :128] = c
                tables[r, at : at + 128, 128:] = s
                tables[r, at + 128 : at + 256, :128] = -s
                tables[r, at + 128 : at + 256, 128:] = c

    def wait(i):
        moves[2 * i].wait()
        moves[2 * i + 1].wait()

    def draws():
        parts = [
            draw(bits[step, 0, at, :], bits[step, 1, at, :], eig[step, at, :])
            for at in (slice(128 * j, 128 * (j + 1)) for j in range(4))
        ]
        for r, value in enumerate(dft_4(*parts)):
            for part in range(2):
                at = slice(128 * part, 128 * (part + 1))
                high[r, at, :], low[r, at, :] = split(value[part])

    def multiply():
        for r in range(4):
            both = dot(tables[r], high[r])
            both = both[:256] + both[256:] + dot(tables[r, :256, :], low[r])
            for a in range(BLOCK // 128):
                for row in range(0, 256, 8):
                    part, zl, y, b = row // 128, row // 64 % 2, row // 16 % 4, row // 8 % 2
                    out[a, b, zl, y, part, r] = both[row : row + 8, 128 * a : 128 * (a + 1)]

    @pl.when(step == 0)
    def _():
        start()
        wait(0)
        draws()
        prepare()

    for i in range(1, STEPS):
        pl.when(step == i)(functools.partial(wait, i))

    @pl.when(jnp.logical_and(step > 0, step < STEPS))
    def _():
        multiply()
        draws()

    pl.when(step == STEPS)(multiply)


def front(noise, eigen, turn):
    base = jnp.asarray(column_table())
    in_hbm = pl.BlockSpec(memory_space=pltpu.HBM)
    return pl.pallas_call(
        front_kernel,
        grid=(STEPS + 1,),
        in_specs=[in_hbm] * 4,
        out_specs=pl.BlockSpec(
            (BLOCK // 128, 2, 2, 4, 2, 4, 8, 128), lambda i: (jnp.maximum(i - 1, 0), 0, 0, 0, 0, 0, 0, 0)
        ),
        out_shape=jax.ShapeDtypeStruct((8, 2, 2, 4, 2, 4, 8, 128), F32),
        scratch_shapes=[
            pltpu.VMEM((STEPS, 2, LOCAL, BLOCK), jnp.int32),
            pltpu.VMEM((STEPS, LOCAL, BLOCK), F32),
            pltpu.VMEM((2, 4, 128, 128), F32),
            pltpu.VMEM((2, 4, 128, 128), F32),
            pltpu.VMEM((4, 512, 256), BF16),
            pltpu.VMEM((4, 256, BLOCK), BF16),
            pltpu.VMEM((4, 256, BLOCK), BF16),
            pltpu.SemaphoreType.DMA((2 * STEPS + 2,)),
        ],
        compiler_params=pltpu.CompilerParams(vmem_limit_bytes=40 * 2**20),
        cost_estimate=pl.CostEstimate(flops=2 * 10**9, bytes_accessed=12 * 2**20, transcendentals=0),
    )(noise, eigen, base, turn)


IN_VMEM = pl.BlockSpec(memory_space=pltpu.VMEM)


def middle_kernel(data, out):
    def step(at, carry):
        y, part = at // 4, at % 4
        row = pl.ds(pl.multiple_of(8 * part, 8), 8)
        for zl in range(2):
            values = []
            for e in range(16):
                core, zh, xl, xh = e >> 3, e >> 2 & 1, e >> 1 & 1, e & 1
                index = (2 * xh + xl, zh, core, zl, y)
                values.append((data[*index, 0, row, :], data[*index, 1, row, :]))
            for k, value in enumerate(dft_16(values)):
                core, zh, xl, xh = k & 1, k >> 1 & 1, k >> 2 & 1, k >> 3
                index = (2 * xh + xl, zh, core, y, zl)
                out[*index, 0, row, :], out[*index, 1, row, :] = value
        return carry

    lax.fori_loop(0, 16, step, 0)


def middle(data):
    return pl.pallas_call(
        middle_kernel,
        in_specs=[IN_VMEM],
        out_specs=IN_VMEM,
        out_shape=jax.ShapeDtypeStruct((4, 2, 2, 4, 2, 2, 32, 128), F32),
        compiler_params=pltpu.CompilerParams(vmem_limit_bytes=32 * 2**20),
        cost_estimate=pl.CostEstimate(flops=10**7, bytes_accessed=8 * 2**20, transcendentals=0),
    )(data)


def row_kernel(data, first, twist, last, out):
    step = pl.program_id(0)
    start = 512 * (step // 2) + 4 * (step % 2)

    def piece(t):
        row = start + 8 * (t % 4) + t // 4
        return jnp.concatenate([data[pl.ds(1024 * a + row, 16, stride=32), :] for a in range(8)], 0)

    high, low = split(jnp.concatenate([piece(t) for t in range(16)], 1))
    sums = dot(first[...], jnp.concatenate([high, low], 0))
    sums = sums[:128] + sums[128:]
    for t in range(16):
        re, im = sums[:64, 128 * t : 128 * (t + 1)], sums[64:, 128 * t : 128 * (t + 1)]
        both = []
        for v in range(2):
            c, s = twist[0, 64 * v : 64 * (v + 1), :], twist[1, 64 * v : 64 * (v + 1), :]
            both.append(jnp.concatenate([re * c - im * s, re * s + im * c], 1))
        high, low = split(jnp.concatenate(both, 0))
        whole = dot(high, last[...])
        whole = (whole[:, :128] + whole[:, 128:] + dot(low, last[:, :128])).T
        for part in range(2):
            out[part, t // 8, :, t % 8, :] = whole[64 * part : 64 * (part + 1)]


def row_transform(data):
    tables = [jnp.asarray(table) for table in row_tables()]
    result = pl.pallas_call(
        row_kernel,
        grid=(4,),
        in_specs=[IN_VMEM] * 4,
        out_specs=pl.BlockSpec((2, 2, 64, 8, 128), lambda i: (0, i, 0, 0, 0)),
        out_shape=jax.ShapeDtypeStruct((2, 8, 64, 8, 128), F32),
        compiler_params=pltpu.CompilerParams(vmem_limit_bytes=48 * 2**20),
        cost_estimate=pl.CostEstimate(flops=3 * 10**9, bytes_accessed=9 * 2**20, transcendentals=0),
    )(data.reshape(8192, 128), *tables)
    return result.transpose(0, 1, 3, 2, 4).reshape(2, 64, M)


def on_device(noise, eigen):
    x, zh, core = (lax.axis_index(name) for name in AXES[:3])
    anchor = 8 * core + 4 * zh + 2 * (x % 2) + x // 2
    row = 4 * jnp.arange(128, dtype=jnp.int32)[None, :] + jnp.arange(4, dtype=jnp.int32)[:, None]
    angle = (anchor * row).astype(F32) * (2.0 * math.pi / N)
    turn = jnp.broadcast_to(jnp.stack([jnp.cos(angle), jnp.sin(angle)])[..., None], (2, 4, 128, 128))
    with jax.named_scope("columns"):
        data = front(noise, eigen, turn)
    with jax.named_scope("first_exchange"):
        data = lax.all_to_all(data.reshape(32, 4, 2, 32, 128), ("x", "zh", "core", "zl"), 0, 0, tiled=True)
    with jax.named_scope("middle"):
        data = middle(data.reshape(4, 2, 2, 2, 4, 2, 32, 128))
    with jax.named_scope("second_exchange"):
        data = lax.all_to_all(data.reshape(64, 2, 2, 32, 128), ("x", "zh", "core", "y"), 0, 0, tiled=True)
    with jax.named_scope("rows"):
        return row_transform(data)


def solution(mesh):
    fine = Mesh(mesh.devices.reshape(SIZES), AXES)
    col, row = AXES[:3], AXES[3:]
    return jax.shard_map(
        on_device,
        mesh=fine,
        in_specs=(P(None, col, row), P(col, row)),
        out_specs=P(None, AXES, None),
        check_vma=False,
    )
```

time: 185 us -> 144 us (0.78)
  Pallas kernels: 54.3 us -> 17.2 us
  waiting for transfers between devices: 6.62 us -> 0 us
  blocking collectives: 118 us -> 120 us
    pallas_call x3, Pallas kernels: 54.3 us -> 17.2 us  [the longest x1 8.65 us: row_transform(): pl.pallas_call(row_kernel, grid=(4,), in_specs=[IN_VMEM] * 4, out_specs=p...]
    ppermute x1 -> x0, waiting for transfers between devices: 6.62 us -> none  [on_device(): other = lax.ppermute(current, 'core', [(0, 1), (1, 0)])]
    all_to_all x2, blocking collectives: 118 us -> 120 us  [the longest x1 61.3 us: on_device(): lax.all_to_all(data.reshape(32, 4, 2, 32, 128), ('x', 'zh', 'core', 'zl')...]
    unnamed x16 -> x12, local copies, waits for them, and re-layouts: 4.8 us -> 4.84 us
  transfers between devices with their start and end apart: 1 -> 0, of which waited for: 1 -> 0; matrix products, arithmetic and copies ran while one was open for 0% -> 0% of each run, Pallas kernels for 0% -> 0%
where the time goes in v2:
time: 144 us; the launch traced here: 143 us
  blocking collectives  120 us (83%)
  Pallas kernels  17.2 us (12%)
  local copies, waits for them, and re-layouts  5.03 us (3%)
    all_to_all x1, blocking collectives, on_device(): lax.all_to_all(data.reshape(32, 4, 2, 32, 128), ('x', 'zh', 'core', 'zl')...  61.3 us
    all_to_all x1, blocking collectives, on_device(): lax.all_to_all(data.reshape(64, 2, 2, 32, 128), ('x', 'zh', 'core', 'y'),...  59.1 us
    pallas_call x1, Pallas kernels, row_transform(): pl.pallas_call(row_kernel, grid=(4,), in_specs=[IN_VMEM] * 4, out_specs=p...  8.65 us
    pallas_call x1, Pallas kernels, front(): pl.pallas_call(front_kernel, grid=(STEPS + 1,), in_specs=[in_hbm] * 4, ou...  7.34 us
    unnamed x12, local copies, waits for them, and re-layouts  4.84 us

profile of v2, /device:TPU:0, one launch (start us, length us, event | category | flops | bytes accessed | tf_op | source)
XLA Modules:
  0.0 142.8 jit_solution(325245365001219130)
XLA Ops:
  0.1 0.2 broadcast_in_dim.2.turn
  0.3 0.0 copy-start
  0.3 2.2 %copy-done = s32[2,512,1024]{2,1,0:T(8,128)S(1)} copy-done((s32[2,512,1024]{2,1,0:T(8,128)S(1)}, s32[2,512,1024]{2,1,0:T(8,128)}, u32[]{:S(2)}) %copy-start) | copy-done | bytes 4194328
  2.5 0.0 copy-start.1
  2.5 1.6 %copy-done.1 = f32[512,1024]{1,0:T(8,128)S(1)} copy-done((f32[512,1024]{1,0:T(8,128)S(1)}, f32[512,1024]{1,0:T(8,128)}, u32[]{:S(2)}) %copy-start.1) | copy-done | bytes 2097176
  4.1 0.0 copy-start.2
  4.1 1.0 copy-done.2
  5.1 7.3 %columns.1 = f32[8,2,2,4,2,4,8,128]{7,6,5,4,3,2,1,0:T(8,128)S(1)} custom-call(s32[2,512,1024]{2,1,0:T(8,128)S(1)} %copy-done, f32[512,1024]{1,0:T(8,128)S(1)} %copy-done.1, f32[2,4,128,128]{3,2,1,0:T(8,128)S(1)} %copy-done.2, f32[2,4,128,128]{3,2,1,0:T(8,128)S(1)} %broadcast_in_dim.2.turn), custom_call_target="tpu_custom_call" | custom-call | flops 2000000000 | bytes 12582912 | tf_op jit(solution)/shard_map/columns/pallas_call | solution.py:208
  12.4 61.3 %all_to_all.10 = f32[32,4,2,32,128]{4,3,2,1,0:T(8,128)S(1)} all-to-all(f32[32,4,2,32,128]{4,3,2,1,0:T(8,128)S(1)} %bitcast.9), channel_id=1, replica_groups=mesh['x'=4,'zh'=2,'core'=2,'zl'=2,'y'=4] {'x','zh','core','zl'}, dimensions={0} | all-to-all | bytes 8388608 | tf_op jit(solution)/shard_map/first_exchange/all_to_all | solution.py:311
  73.7 1.2 middle.1
  75.0 0.0 copy-start.3
  75.0 0.0 copy-start.4
  75.0 0.0 copy-start.5
  75.0 59.1 %all_to_all.11 = f32[64,2,2,32,128]{4,3,2,1,0:T(8,128)S(1)} all-to-all(f32[64,2,2,32,128]{4,3,2,1,0:T(8,128)S(1)} %bitcast.8), channel_id=1, replica_groups=mesh['x'=4,'zh'=2,'core'=2,'zl'=2,'y'=4] {'x','zh','core','y'}, dimensions={0} | all-to-all | bytes 8388608 | tf_op jit(solution)/shard_map/second_exchange/all_to_all | solution.py:315
  134.1 0.0 copy-done.3
  134.1 0.0 copy-done.4
  134.1 0.0 copy-done.5
  134.1 8.6 %rows.1 = f32[2,8,64,8,128]{4,3,2,1,0:T(8,128)} custom-call(f32[8192,128]{1,0:T(8,128)S(1)} %bitcast.10, bf16[256,256]{1,0:T(8,128)(2,1)S(1)} %copy-done.5, f32[2,128,128]{2,1,0:T(8,128)S(1)} %copy-done.4, bf16[256,256]{1,0:T(8,128)(2,1)S(1)} %copy-done.3), custom_call_target="tpu_custom_call" | custom-call | flops 3000000000 | bytes 9437184 | tf_op jit(solution)/shard_map/rows/pallas_call | solution.py:290
  (3 shorter events, 0.1 us)
Async XLA Ops:
  0.3 2.2 %copy-start = (s32[2,512,1024]{2,1,0:T(8,128)S(1)}, s32[2,512,1024]{2,1,0:T(8,128)}, u32[]{:S(2)}) copy-start(s32[2,512,1024]{2,1,0:T(8,128)} %noise.1) | copy-start | bytes 12582916
  2.5 1.6 %copy-start.1 = (f32[512,1024]{1,0:T(8,128)S(1)}, f32[512,1024]{1,0:T(8,128)}, u32[]{:S(2)}) copy-start(f32[512,1024]{1,0:T(8,128)} %eigen.1) | copy-start | bytes 6291460
  4.1 1.0 copy-start.2
  75.0 59.2 %copy-start.3 = (bf16[256,256]{1,0:T(8,128)(2,1)S(1)}, bf16[256,256]{1,0:T(8,128)(2,1)}, u32[]{:S(2)}) copy-start(bf16[256,256]{1,0:T(8,128)(2,1)} %constant.57.clone.last) | copy-start | bytes 393220
  75.0 59.2 %copy-start.4 = (f32[2,128,128]{2,1,0:T(8,128)S(1)}, f32[2,128,128]{2,1,0:T(8,128)}, u32[]{:S(2)}) copy-start(f32[2,128,128]{2,1,0:T(8,128)} %constant.56.clone.twist) | copy-start | bytes 393220
  75.0 59.1 %copy-start.5 = (bf16[256,256]{1,0:T(8,128)(2,1)S(1)}, bf16[256,256]{1,0:T(8,128)(2,1)}, u32[]{:S(2)}) copy-start(bf16[256,256]{1,0:T(8,128)(2,1)} %constant.55.clone.first) | copy-start | bytes 393220

commit v3 on v2

--- a/solution.py
+++ b/solution.py
@@ -43,7 +43,7 @@
 
 
 def row_tables():
-    place = 8 * (4 * np.arange(2)[None, None, :] + np.arange(4)[None, :, None]) + np.arange(8)[:, None, None]
+    place = 8 * (4 * np.arange(2)[None, :, None] + np.arange(4)[None, None, :]) + np.arange(8)[:, None, None]
     angle = 2.0 * np.pi * (np.arange(64)[:, None] * place.reshape(1, 64) % 64) / 64
     cosine, sine = np.cos(angle), np.sin(angle)
     real_part = np.stack([cosine, sine], -1).reshape(64, 128)
@@ -64,9 +64,13 @@
         nodes**2, np.sin(2 * np.pi * nodes) / nodes, 4, domain=[0, 1 / 16]
     ).convert(kind=np.polynomial.Polynomial, domain=[-1, 1], window=[-1, 1])
     cosine = np.polynomial.chebyshev.Chebyshev.fit(
-        nodes**2, np.cos(2 * np.pi * nodes), 5, domain=[0, 1 / 16]
+        nodes**2, np.cos(2 * np.pi * nodes), 4, domain=[0, 1 / 16]
     ).convert(kind=np.polynomial.Polynomial, domain=[-1, 1], window=[-1, 1])
-    return [float(c) for c in square.coef], [float(c) for c in cosine.coef]
+    scale = 2.0**-12
+    return (
+        [float(c) * scale ** (2 * i + 1) for i, c in enumerate(square.coef)],
+        [float(c) * scale ** (2 * i) for i, c in enumerate(cosine.coef)],
+    )
 
 
 SINE, COSINE = sine_polynomials()
@@ -85,9 +89,10 @@
 
 def draw(bits_0, bits_1, eigen):
     uniform = (bits_0.astype(F32) + 0.5) * 2.0**-12
-    radius = jnp.sqrt(jnp.log(uniform) * eigen * (-2.0 / (N * M)))
-    past = (bits_1.astype(F32) - 2047.5) * 2.0**-12
-    h = jnp.abs(past) - 0.25
+    square = jnp.log(uniform) * eigen * (-2.0 / (N * M))
+    radius = square * lax.rsqrt(square)
+    past = bits_1.astype(F32) - 2047.5
+    h = jnp.abs(past) - 1024.0
     square = h * h
     value_re = radius * (h * horner(SINE, square))
     value_im = jnp.where(past > 0, -radius, radius) * horner(COSINE, square)
@@ -131,7 +136,7 @@
     return [second[k % 4][k // 4] for k in range(16)]
 
 
-def front_kernel(noise, eigen, base, turn, out, bits, eig, base_in, turn_in, tables, high, low, arrived):
+def front_kernel(noise, eigen, base, turn, out, bits, eig, base_in, tables, values, arrived):
     step = pl.program_id(0)
 
     def copies():
@@ -140,7 +145,6 @@
             yield pltpu.make_async_copy(noise.at[:, :, columns], bits.at[i], arrived.at[i])
             yield pltpu.make_async_copy(eigen.at[:, columns], eig.at[i], arrived.at[STEPS + i])
         yield pltpu.make_async_copy(base, base_in, arrived.at[2 * STEPS])
-        yield pltpu.make_async_copy(turn, turn_in, arrived.at[2 * STEPS + 1])
 
     moves = list(copies())
 
@@ -149,17 +153,16 @@
             move.start()
 
     def prepare():
-        moves[-2].wait()
         moves[-1].wait()
         for r in range(4):
-            cosine = base_in[0, r] * turn_in[0, r] - base_in[1, r] * turn_in[1, r]
-            sine = base_in[1, r] * turn_in[0, r] + base_in[0, r] * turn_in[1, r]
+            cosine = base_in[0, r] * turn[0, r] - base_in[1, r] * turn[1, r]
+            sine = base_in[1, r] * turn[0, r] + base_in[0, r] * turn[1, r]
             (cosine, cosine_low), (sine, sine_low) = split(cosine), split(sine)
-            for at, c, s in ((0, cosine, sine), (256, cosine_low, sine_low)):
-                tables[r, at : at + 128, :128] = c
-                tables[r, at : at + 128, 128:] = s
-                tables[r, at + 128 : at + 256, :128] = -s
-                tables[r, at + 128 : at + 256, 128:] = c
+            for at, c, s in ((0, cosine, sine), (256, cosine, sine), (512, cosine_low, sine_low)):
+                tables[r, :128, at : at + 128] = c
+                tables[r, :128, at + 128 : at + 256] = s
+                tables[r, 128:, at : at + 128] = -s
+                tables[r, 128:, at + 128 : at + 256] = c
 
     def wait(i):
         moves[2 * i].wait()
@@ -172,17 +175,17 @@
         ]
         for r, value in enumerate(dft_4(*parts)):
             for part in range(2):
-                at = slice(128 * part, 128 * (part + 1))
-                high[r, at, :], low[r, at, :] = split(value[part])
+                high, low = split(value[part])
+                for at, half in ((0, high), (256, low), (512, high)):
+                    values[r, at + 128 * part : at + 128 * (part + 1), :] = half
 
     def multiply():
         for r in range(4):
-            both = dot(tables[r], high[r])
-            both = both[:256] + both[256:] + dot(tables[r, :256, :], low[r])
+            both = dot(tables[r], values[r])
             for a in range(BLOCK // 128):
                 for row in range(0, 256, 8):
                     part, zl, y, b = row // 128, row // 64 % 2, row // 16 % 4, row // 8 % 2
-                    out[a, b, zl, y, part, r] = both[row : row + 8, 128 * a : 128 * (a + 1)]
+                    out[a, b, y, zl, part, r] = both[row : row + 8, 128 * a : 128 * (a + 1)]
 
     @pl.when(step == 0)
     def _():
@@ -208,24 +211,22 @@
     return pl.pallas_call(
         front_kernel,
         grid=(STEPS + 1,),
-        in_specs=[in_hbm] * 4,
+        in_specs=[in_hbm] * 3 + [pl.BlockSpec(memory_space=pltpu.VMEM)],
         out_specs=pl.BlockSpec(
-            (BLOCK // 128, 2, 2, 4, 2, 4, 8, 128), lambda i: (jnp.maximum(i - 1, 0), 0, 0, 0, 0, 0, 0, 0)
+            (BLOCK // 128, 2, 4, 2, 2, 4, 8, 128), lambda i: (jnp.maximum(i - 1, 0), 0, 0, 0, 0, 0, 0, 0)
         ),
-        out_shape=jax.ShapeDtypeStruct((8, 2, 2, 4, 2, 4, 8, 128), F32),
+        out_shape=jax.ShapeDtypeStruct((8, 2, 4, 2, 2, 4, 8, 128), F32),
         scratch_shapes=[
             pltpu.VMEM((STEPS, 2, LOCAL, BLOCK), jnp.int32),
             pltpu.VMEM((STEPS, LOCAL, BLOCK), F32),
             pltpu.VMEM((2, 4, 128, 128), F32),
-            pltpu.VMEM((2, 4, 128, 128), F32),
-            pltpu.VMEM((4, 512, 256), BF16),
-            pltpu.VMEM((4, 256, BLOCK), BF16),
-            pltpu.VMEM((4, 256, BLOCK), BF16),
-            pltpu.SemaphoreType.DMA((2 * STEPS + 2,)),
+            pltpu.VMEM((4, 256, 768), BF16),
+            pltpu.VMEM((4, 768, BLOCK), BF16),
+            pltpu.SemaphoreType.DMA((2 * STEPS + 1,)),
         ],
         compiler_params=pltpu.CompilerParams(vmem_limit_bytes=40 * 2**20),
         cost_estimate=pl.CostEstimate(flops=2 * 10**9, bytes_accessed=12 * 2**20, transcendentals=0),
-    )(noise, eigen, base, turn)
+    )(*(pltpu.with_memory_space_constraint(value, pltpu.HBM) for value in (noise, eigen, base)), turn)
 
 
 IN_VMEM = pl.BlockSpec(memory_space=pltpu.VMEM)
@@ -233,21 +234,22 @@
 
 def middle_kernel(data, out):
     def step(at, carry):
-        y, part = at // 4, at % 4
-        row = pl.ds(pl.multiple_of(8 * part, 8), 8)
-        for zl in range(2):
+        zl, r = at // 4, at % 4
+        for y in range(4):
             values = []
             for e in range(16):
                 core, zh, xl, xh = e >> 3, e >> 2 & 1, e >> 1 & 1, e & 1
-                index = (2 * xh + xl, zh, core, zl, y)
-                values.append((data[*index, 0, row, :], data[*index, 1, row, :]))
+                index = (2 * xh + xl, zh, core, y, zl)
+                values.append((data[*index, 0, r], data[*index, 1, r]))
             for k, value in enumerate(dft_16(values)):
                 core, zh, xl, xh = k & 1, k >> 1 & 1, k >> 2 & 1, k >> 3
-                index = (2 * xh + xl, zh, core, y, zl)
-                out[*index, 0, row, :], out[*index, 1, row, :] = value
+                place = 4 * (2 * xh + xl) + 2 * zh + core
+                row = pl.multiple_of(512 * place + 64 * at, 64)
+                for part in range(2):
+                    out[pl.ds(row + 2 * y + part, 8, stride=8), :] = value[part]
         return carry
 
-    lax.fori_loop(0, 16, step, 0)
+    lax.fori_loop(0, 8, step, 0)
 
 
 def middle(data):
@@ -255,7 +257,7 @@
         middle_kernel,
         in_specs=[IN_VMEM],
         out_specs=IN_VMEM,
-        out_shape=jax.ShapeDtypeStruct((4, 2, 2, 4, 2, 2, 32, 128), F32),
+        out_shape=jax.ShapeDtypeStruct((8192, 128), F32),
         compiler_params=pltpu.CompilerParams(vmem_limit_bytes=32 * 2**20),
         cost_estimate=pl.CostEstimate(flops=10**7, bytes_accessed=8 * 2**20, transcendentals=0),
     )(data)
@@ -263,11 +265,9 @@
 
 def row_kernel(data, first, twist, last, out):
     step = pl.program_id(0)
-    start = 512 * (step // 2) + 4 * (step % 2)
 
     def piece(t):
-        row = start + 8 * (t % 4) + t // 4
-        return jnp.concatenate([data[pl.ds(1024 * a + row, 16, stride=32), :] for a in range(8)], 0)
+        return data[:, step // 2, :, t % 4, 4 * (step % 2) + t // 4].reshape(128, 128)
 
     high, low = split(jnp.concatenate([piece(t) for t in range(16)], 1))
     sums = dot(first[...], jnp.concatenate([high, low], 0))
@@ -282,7 +282,7 @@
         whole = dot(high, last[...])
         whole = (whole[:, :128] + whole[:, 128:] + dot(low, last[:, :128])).T
         for part in range(2):
-            out[part, t // 8, :, t % 8, :] = whole[64 * part : 64 * (part + 1)]
+            out[part, pl.ds(512 * (t // 8) + t % 8, 64, stride=8), :] = whole[64 * part : 64 * (part + 1)]
 
 
 def row_transform(data):
@@ -291,12 +291,12 @@
         row_kernel,
         grid=(4,),
         in_specs=[IN_VMEM] * 4,
-        out_specs=pl.BlockSpec((2, 2, 64, 8, 128), lambda i: (0, i, 0, 0, 0)),
-        out_shape=jax.ShapeDtypeStruct((2, 8, 64, 8, 128), F32),
+        out_specs=pl.BlockSpec((2, 1024, 128), lambda i: (0, i, 0)),
+        out_shape=jax.ShapeDtypeStruct((2, 4096, 128), F32),
         compiler_params=pltpu.CompilerParams(vmem_limit_bytes=48 * 2**20),
         cost_estimate=pl.CostEstimate(flops=3 * 10**9, bytes_accessed=9 * 2**20, transcendentals=0),
-    )(data.reshape(8192, 128), *tables)
-    return result.transpose(0, 1, 3, 2, 4).reshape(2, 64, M)
+    )(data.reshape(8, 2, 2, 4, 8, 8, 128), *tables)
+    return result.reshape(2, 8, 64, 8, 128).transpose(0, 1, 3, 2, 4).reshape(2, 64, M)
 
 
 def on_device(noise, eigen):
@@ -308,11 +308,11 @@
     with jax.named_scope("columns"):
         data = front(noise, eigen, turn)
     with jax.named_scope("first_exchange"):
-        data = lax.all_to_all(data.reshape(32, 4, 2, 32, 128), ("x", "zh", "core", "zl"), 0, 0, tiled=True)
+        data = lax.all_to_all(data.reshape(64, 2, 2, 32, 128), ("x", "zh", "core", "y"), 0, 0, tiled=True)
     with jax.named_scope("middle"):
-        data = middle(data.reshape(4, 2, 2, 2, 4, 2, 32, 128))
+        data = middle(data.reshape(4, 2, 2, 4, 2, 2, 4, 8, 128))
     with jax.named_scope("second_exchange"):
-        data = lax.all_to_all(data.reshape(64, 2, 2, 32, 128), ("x", "zh", "core", "y"), 0, 0, tiled=True)
+        data = lax.all_to_all(data.reshape(32, 256, 128), ("x", "zh", "core", "zl"), 0, 0, tiled=True)
     with jax.named_scope("rows"):
         return row_transform(data)
 

time: 144 us -> 137 us (0.951)
  local copies, waits for them, and re-layouts: 5.03 us -> 0.21 us
  Pallas kernels: 17.2 us -> 15.1 us
    unnamed x12 -> x6, local copies, waits for them, and re-layouts: 4.84 us -> 0.02 us
    all_to_all x1, blocking collectives: 59.1 us -> 63.7 us  [on_device(): lax.all_to_all(data.reshape(64, 2, 2, 32, 128), ('x', 'zh', 'core', 'y'),...]
    all_to_all x1, blocking collectives: 61.3 us -> 57.4 us  [on_device(): lax.all_to_all(data.reshape(32, 256, 128), ('x', 'zh', 'core', 'zl'), 0,...]
    pallas_call x1, Pallas kernels: 8.65 us -> 5.81 us  [row_transform(): pl.pallas_call(row_kernel, grid=(4,), in_specs=[IN_VMEM] * 4, out_specs=p...]
where the time goes in v3:
time: 137 us; the launch traced here: 136 us
  blocking collectives  121 us (88%)
  Pallas kernels  15.1 us (11%)
    all_to_all x1, blocking collectives, on_device(): lax.all_to_all(data.reshape(64, 2, 2, 32, 128), ('x', 'zh', 'core', 'y'),...  63.7 us
    all_to_all x1, blocking collectives, on_device(): lax.all_to_all(data.reshape(32, 256, 128), ('x', 'zh', 'core', 'zl'), 0,...  57.4 us
    pallas_call x1, Pallas kernels, front(): pl.pallas_call(front_kernel, grid=(STEPS + 1,), in_specs=[in_hbm] * 3 + [...  7.92 us
    pallas_call x1, Pallas kernels, row_transform(): pl.pallas_call(row_kernel, grid=(4,), in_specs=[IN_VMEM] * 4, out_specs=p...  5.81 us

profile of v3, /device:TPU:0, one launch (start us, length us, event | category | flops | bytes accessed | tf_op | source)
XLA Modules:
  0.0 136.5 jit_solution(13344625956283854411)
XLA Ops:
  0.1 0.2 broadcast_in_dim.2.turn
  0.3 7.9 %columns.1 = f32[8,2,4,2,2,4,8,128]{7,6,5,4,3,2,1,0:T(8,128)S(1)} custom-call(s32[2,512,1024]{2,1,0:T(8,128)} %noise.1, f32[512,1024]{1,0:T(8,128)} %eigen.1, f32[2,4,128,128]{3,2,1,0:T(8,128)} %constant.54.clone.base, f32[2,4,128,128]{3,2,1,0:T(8,128)S(1)} %broadcast_in_dim.2.turn), custom_call_target="tpu_custom_call" | custom-call | flops 2000000000 | bytes 12582912 | tf_op jit(solution)/shard_map/columns/pallas_call | solution.py:211
  8.2 63.7 %all_to_all.10 = f32[64,2,2,32,128]{4,3,2,1,0:T(8,128)S(1)} all-to-all(f32[64,2,2,32,128]{4,3,2,1,0:T(8,128)S(1)} %bitcast.11), channel_id=1, replica_groups=mesh['x'=4,'zh'=2,'core'=2,'zl'=2,'y'=4] {'x','zh','core','y'}, dimensions={0} | all-to-all | bytes 8388608 | tf_op jit(solution)/shard_map/first_exchange/all_to_all | solution.py:311
  71.9 1.4 middle.1
  73.2 0.0 copy-start
  73.2 0.0 copy-start.1
  73.3 0.0 copy-start.2
  73.3 57.4 %all_to_all.11 = f32[32,256,128]{2,1,0:T(8,128)S(1)} all-to-all(f32[32,256,128]{2,1,0:T(8,128)S(1)} %bitcast.10), channel_id=1, replica_groups=mesh['x'=4,'zh'=2,'core'=2,'zl'=2,'y'=4] {'x','zh','core','zl'}, dimensions={0} | all-to-all | bytes 8388608 | tf_op jit(solution)/shard_map/second_exchange/all_to_all | solution.py:315
  130.7 0.0 copy-done
  130.7 0.0 copy-done.1
  130.7 0.0 copy-done.2
  130.7 5.8 %rows.1 = f32[2,4096,128]{2,1,0:T(8,128)} custom-call(f32[8,2,2,4,8,8,128]{6,5,4,3,2,1,0:T(8,128)S(1)} %bitcast.12, bf16[256,256]{1,0:T(8,128)(2,1)S(1)} %copy-done.2, f32[2,128,128]{2,1,0:T(8,128)S(1)} %copy-done.1, bf16[256,256]{1,0:T(8,128)(2,1)S(1)} %copy-done), custom_call_target="tpu_custom_call" | custom-call | flops 3000000000 | bytes 9437184 | tf_op jit(solution)/shard_map/rows/pallas_call | solution.py:290
  (3 shorter events, 0.1 us)
Async XLA Ops:
  73.2 57.4 %copy-start = (bf16[256,256]{1,0:T(8,128)(2,1)S(1)}, bf16[256,256]{1,0:T(8,128)(2,1)}, u32[]{:S(2)}) copy-start(bf16[256,256]{1,0:T(8,128)(2,1)} %constant.57.clone.last) | copy-start | bytes 393220
  73.2 57.4 %copy-start.1 = (f32[2,128,128]{2,1,0:T(8,128)S(1)}, f32[2,128,128]{2,1,0:T(8,128)}, u32[]{:S(2)}) copy-start(f32[2,128,128]{2,1,0:T(8,128)} %constant.56.clone.twist) | copy-start | bytes 393220
  73.3 57.4 %copy-start.2 = (bf16[256,256]{1,0:T(8,128)(2,1)S(1)}, bf16[256,256]{1,0:T(8,128)(2,1)}, u32[]{:S(2)}) copy-start(bf16[256,256]{1,0:T(8,128)(2,1)} %constant.55.clone.first) | copy-start | bytes 393220

commit v4 on v3

--- a/solution.py
+++ b/solution.py
@@ -15,7 +15,7 @@
 LOCAL = 512
 WIDTH = 1024
 BLOCK = 256
-STEPS = WIDTH // BLOCK
+STEPS = WIDTH // BLOCK // 2
 
 AXES = ("x", "zh", "core", "zl", "y")
 SIZES = (4, 2, 2, 2, 4)
@@ -117,43 +117,74 @@
     return add(even, odd), add(less, turned), sub(even, odd), sub(less, turned)
 
 
-def spin(a, step):
-    if step == 0:
-        return a
-    if step == 4:
-        return turn_back(a)
-    if step % 4 == 2:
-        root = math.sqrt(0.5)
-        a = ((a[0] + a[1]) * root, (a[1] - a[0]) * root)
-        return a if step == 2 else turn_back(a)
-    c, s = math.cos(math.pi * step / 8), math.sin(math.pi * step / 8)
-    return a[0] * c + a[1] * s, a[1] * c - a[0] * s
-
-
-def dft_16(v):
-    first = [dft_4(v[e], v[4 + e], v[8 + e], v[12 + e]) for e in range(4)]
-    second = [dft_4(*(spin(first[e][s], e * s) for e in range(4))) for s in range(4)]
-    return [second[k % 4][k // 4] for k in range(16)]
-
-
-def front_kernel(noise, eigen, base, turn, out, bits, eig, base_in, tables, values, arrived):
+ROOT = math.sqrt(0.5)
+
+
+def dft_8(v):
+    even = dft_4(v[0], v[2], v[4], v[6])
+    odd = dft_4(v[1], v[3], v[5], v[7])
+    spun = [
+        odd[0],
+        ((odd[1][0] + odd[1][1]) * ROOT, (odd[1][1] - odd[1][0]) * ROOT),
+        turn_back(odd[2]),
+        ((odd[3][1] - odd[3][0]) * ROOT, (odd[3][0] + odd[3][1]) * -ROOT),
+    ]
+    return [add(e, o) for e, o in zip(even, spun)] + [sub(e, o) for e, o in zip(even, spun)]
+
+
+def draws(bits, eig, block, values):
+    parts = [
+        draw(bits[block, 0, at, :], bits[block, 1, at, :], eig[block, at, :])
+        for at in (slice(128 * j, 128 * (j + 1)) for j in range(4))
+    ]
+    for r, value in enumerate(dft_4(*parts)):
+        for part in range(2):
+            high, low = split(value[part])
+            for at, half in ((0, high), (256, low), (512, high)):
+                values[r, at + 128 * part : at + 128 * (part + 1), :] = half
+
+
+def multiply(tables, values, out):
+    for r in range(4):
+        both = dot(tables[r], values[r])
+        for a in range(BLOCK // 128):
+            for row in range(0, 256, 8):
+                part, zl, y, t = row // 128, row // 64 % 2, row // 16 % 4, row % 16
+                out[a, y, zl, part, r, t : t + 8] = both[row : row + 8, 128 * a : 128 * (a + 1)]
+
+
+def blocks(step, arrive, bits, eig, tables, values, out):
+    @pl.when(step == 0)
+    def _():
+        arrive(0)
+        draws(bits, eig, 0, values)
+
+    for i in range(1, STEPS):
+        pl.when(step == i)(functools.partial(arrive, i))
+
+    @pl.when(jnp.logical_and(step > 0, step < STEPS))
+    def _():
+        multiply(tables, values, out)
+        draws(bits, eig, step, values)
+
+    pl.when(step == STEPS)(functools.partial(multiply, tables, values, out))
+
+
+def first_half_kernel(noise, eigen, base, turn, out, tables, bits_left, eig_left, bits, eig, base_in, values, arrived):
     step = pl.program_id(0)
-
-    def copies():
-        for i in range(STEPS):
-            columns = slice(BLOCK * i, BLOCK * (i + 1))
-            yield pltpu.make_async_copy(noise.at[:, :, columns], bits.at[i], arrived.at[i])
-            yield pltpu.make_async_copy(eigen.at[:, columns], eig.at[i], arrived.at[STEPS + i])
-        yield pltpu.make_async_copy(base, base_in, arrived.at[2 * STEPS])
-
-    moves = list(copies())
-
-    def start():
+    moves = []
+    for i in range(2 * STEPS):
+        columns = slice(BLOCK * i, BLOCK * (i + 1))
+        to = (bits.at[i], eig.at[i]) if i < STEPS else (bits_left.at[i - STEPS], eig_left.at[i - STEPS])
+        moves.append(pltpu.make_async_copy(noise.at[:, :, columns], to[0], arrived.at[2 * i]))
+        moves.append(pltpu.make_async_copy(eigen.at[:, columns], to[1], arrived.at[2 * i + 1]))
+    moves.insert(2, pltpu.make_async_copy(base, base_in, arrived.at[4 * STEPS]))
+
+    @pl.when(step == 0)
+    def _():
         for move in moves:
             move.start()
-
-    def prepare():
-        moves[-1].wait()
+        moves[2].wait()
         for r in range(4):
             cosine = base_in[0, r] * turn[0, r] - base_in[1, r] * turn[1, r]
             sine = base_in[1, r] * turn[0, r] + base_in[0, r] * turn[1, r]
@@ -164,110 +195,107 @@
                 tables[r, 128:, at : at + 128] = -s
                 tables[r, 128:, at + 128 : at + 256] = c
 
-    def wait(i):
-        moves[2 * i].wait()
-        moves[2 * i + 1].wait()
-
-    def draws():
-        parts = [
-            draw(bits[step, 0, at, :], bits[step, 1, at, :], eig[step, at, :])
-            for at in (slice(128 * j, 128 * (j + 1)) for j in range(4))
-        ]
-        for r, value in enumerate(dft_4(*parts)):
-            for part in range(2):
-                high, low = split(value[part])
-                for at, half in ((0, high), (256, low), (512, high)):
-                    values[r, at + 128 * part : at + 128 * (part + 1), :] = half
-
-    def multiply():
-        for r in range(4):
-            both = dot(tables[r], values[r])
-            for a in range(BLOCK // 128):
-                for row in range(0, 256, 8):
-                    part, zl, y, b = row // 128, row // 64 % 2, row // 16 % 4, row // 8 % 2
-                    out[a, b, y, zl, part, r] = both[row : row + 8, 128 * a : 128 * (a + 1)]
-
-    @pl.when(step == 0)
+    def arrive(i):
+        for move in moves[:2] if i == 0 else moves[2 * i + 1 : 2 * i + 3]:
+            move.wait()
+
+    blocks(step, arrive, bits, eig, tables, values, out)
+
+    @pl.when(step == STEPS)
     def _():
-        start()
-        wait(0)
-        draws()
-        prepare()
-
-    for i in range(1, STEPS):
-        pl.when(step == i)(functools.partial(wait, i))
-
-    @pl.when(jnp.logical_and(step > 0, step < STEPS))
-    def _():
-        multiply()
-        draws()
-
-    pl.when(step == STEPS)(multiply)
-
-
-def front(noise, eigen, turn):
+        for move in moves[2 * STEPS + 1 :]:
+            move.wait()
+
+
+def second_half_kernel(bits, eig, tables, out, values):
+    blocks(pl.program_id(0), lambda i: None, bits, eig, tables, values, out)
+
+
+IN_VMEM = pl.BlockSpec(memory_space=pltpu.VMEM)
+HALF_OUT = pl.BlockSpec((BLOCK // 128, 4, 2, 2, 4, 16, 128), lambda i: (jnp.maximum(i - 1, 0), 0, 0, 0, 0, 0, 0))
+HALF_SHAPE = jax.ShapeDtypeStruct((4, 4, 2, 2, 4, 16, 128), F32)
+VALUES = pltpu.VMEM((4, 768, BLOCK), BF16)
+
+
+def first_half(noise, eigen, turn):
     base = jnp.asarray(column_table())
-    in_hbm = pl.BlockSpec(memory_space=pltpu.HBM)
+    bits, eig = (STEPS, 2, LOCAL, BLOCK), (STEPS, LOCAL, BLOCK)
     return pl.pallas_call(
-        front_kernel,
+        first_half_kernel,
         grid=(STEPS + 1,),
-        in_specs=[in_hbm] * 3 + [pl.BlockSpec(memory_space=pltpu.VMEM)],
-        out_specs=pl.BlockSpec(
-            (BLOCK // 128, 2, 4, 2, 2, 4, 8, 128), lambda i: (jnp.maximum(i - 1, 0), 0, 0, 0, 0, 0, 0, 0)
-        ),
-        out_shape=jax.ShapeDtypeStruct((8, 2, 4, 2, 2, 4, 8, 128), F32),
+        in_specs=[pl.BlockSpec(memory_space=pltpu.HBM)] * 3 + [IN_VMEM],
+        out_specs=[HALF_OUT] + [IN_VMEM] * 3,
+        out_shape=[
+            HALF_SHAPE,
+            jax.ShapeDtypeStruct((4, 256, 768), BF16),
+            jax.ShapeDtypeStruct(bits, jnp.int32),
+            jax.ShapeDtypeStruct(eig, F32),
+        ],
         scratch_shapes=[
-            pltpu.VMEM((STEPS, 2, LOCAL, BLOCK), jnp.int32),
-            pltpu.VMEM((STEPS, LOCAL, BLOCK), F32),
+            pltpu.VMEM(bits, jnp.int32),
+            pltpu.VMEM(eig, F32),
             pltpu.VMEM((2, 4, 128, 128), F32),
-            pltpu.VMEM((4, 256, 768), BF16),
-            pltpu.VMEM((4, 768, BLOCK), BF16),
-            pltpu.SemaphoreType.DMA((2 * STEPS + 1,)),
+            VALUES,
+            pltpu.SemaphoreType.DMA((4 * STEPS + 1,)),
         ],
         compiler_params=pltpu.CompilerParams(vmem_limit_bytes=40 * 2**20),
-        cost_estimate=pl.CostEstimate(flops=2 * 10**9, bytes_accessed=12 * 2**20, transcendentals=0),
+        cost_estimate=pl.CostEstimate(flops=10**9, bytes_accessed=12 * 2**20, transcendentals=0),
     )(*(pltpu.with_memory_space_constraint(value, pltpu.HBM) for value in (noise, eigen, base)), turn)
 
 
-IN_VMEM = pl.BlockSpec(memory_space=pltpu.VMEM)
-
-
-def middle_kernel(data, out):
+def second_half(bits, eig, tables):
+    return pl.pallas_call(
+        second_half_kernel,
+        grid=(STEPS + 1,),
+        in_specs=[IN_VMEM] * 3,
+        out_specs=HALF_OUT,
+        out_shape=HALF_SHAPE,
+        scratch_shapes=[VALUES],
+        compiler_params=pltpu.CompilerParams(vmem_limit_bytes=40 * 2**20),
+        cost_estimate=pl.CostEstimate(flops=10**9, bytes_accessed=8 * 2**20, transcendentals=0),
+    )(bits, eig, tables)
+
+
+def middle_kernel(scalars, data, out):
     def step(at, carry):
         zl, r = at // 4, at % 4
-        for y in range(4):
-            values = []
-            for e in range(16):
-                core, zh, xl, xh = e >> 3, e >> 2 & 1, e >> 1 & 1, e & 1
-                index = (2 * xh + xl, zh, core, y, zl)
-                values.append((data[*index, 0, r], data[*index, 1, r]))
-            for k, value in enumerate(dft_16(values)):
-                core, zh, xl, xh = k & 1, k >> 1 & 1, k >> 2 & 1, k >> 3
-                place = 4 * (2 * xh + xl) + 2 * zh + core
-                row = pl.multiple_of(512 * place + 64 * at, 64)
-                for part in range(2):
-                    out[pl.ds(row + 2 * y + part, 8, stride=8), :] = value[part]
+        for half in range(2):
+            line = slice(8 * half, 8 * half + 8)
+            for y in range(4):
+                values = []
+                for e in range(8):
+                    zh, xl, xh = e >> 2, e >> 1 & 1, e & 1
+                    index = (2 * xh + xl, zh, y, zl)
+                    re, im = data[*index, 0, r, line], data[*index, 1, r, line]
+                    c, s = scalars[2 * e], scalars[2 * e + 1]
+                    values.append((re * c - im * s, re * s + im * c) if e else (re, im))
+                for k, value in enumerate(dft_8(values)):
+                    zh, xl, xh = k & 1, k >> 1 & 1, k >> 2
+                    place = 2 * (2 * xh + xl) + zh
+                    row = pl.multiple_of(1024 * place + 128 * at, 128) + 64 * half
+                    for part in range(2):
+                        out[pl.ds(row + 2 * y + part, 8, stride=8), :] = value[part]
         return carry
 
     lax.fori_loop(0, 8, step, 0)
 
 
-def middle(data):
+def middle(scalars, data):
     return pl.pallas_call(
         middle_kernel,
-        in_specs=[IN_VMEM],
+        in_specs=[pl.BlockSpec(memory_space=pltpu.SMEM), IN_VMEM],
         out_specs=IN_VMEM,
         out_shape=jax.ShapeDtypeStruct((8192, 128), F32),
         compiler_params=pltpu.CompilerParams(vmem_limit_bytes=32 * 2**20),
         cost_estimate=pl.CostEstimate(flops=10**7, bytes_accessed=8 * 2**20, transcendentals=0),
-    )(data)
+    )(scalars, data)
 
 
 def row_kernel(data, first, twist, last, out):
     step = pl.program_id(0)
 
     def piece(t):
-        return data[:, step // 2, :, t % 4, 4 * (step % 2) + t // 4].reshape(128, 128)
+        return data[:, :, t % 4, 4 * step + t // 4].reshape(128, 128)
 
     high, low = split(jnp.concatenate([piece(t) for t in range(16)], 1))
     sums = dot(first[...], jnp.concatenate([high, low], 0))
@@ -295,7 +323,7 @@
         out_shape=jax.ShapeDtypeStruct((2, 4096, 128), F32),
         compiler_params=pltpu.CompilerParams(vmem_limit_bytes=48 * 2**20),
         cost_estimate=pl.CostEstimate(flops=3 * 10**9, bytes_accessed=9 * 2**20, transcendentals=0),
-    )(data.reshape(8, 2, 2, 4, 8, 8, 128), *tables)
+    )(data.reshape(8, 2, 4, 16, 8, 128), *tables)
     return result.reshape(2, 8, 64, 8, 128).transpose(0, 1, 3, 2, 4).reshape(2, 64, M)
 
 
@@ -305,14 +333,23 @@
     row = 4 * jnp.arange(128, dtype=jnp.int32)[None, :] + jnp.arange(4, dtype=jnp.int32)[:, None]
     angle = (anchor * row).astype(F32) * (2.0 * math.pi / N)
     turn = jnp.broadcast_to(jnp.stack([jnp.cos(angle), jnp.sin(angle)])[..., None], (2, 4, 128, 128))
+    angle = (core * jnp.arange(8, dtype=jnp.int32)).astype(F32) * (-2.0 * math.pi / 16)
+    scalars = jnp.stack([jnp.cos(angle), jnp.sin(angle)], 1).reshape(16)
+    sign = (1 - 2 * core).astype(F32)
+    swap = lambda value: lax.ppermute(value, "core", [(0, 1), (1, 0)])
     with jax.named_scope("columns"):
-        data = front(noise, eigen, turn)
+        data, tables, bits, eig = first_half(noise, eigen, turn)
+        other = swap(data)
+        data_2 = second_half(bits, eig, tables)
+        other_2 = swap(data_2)
+    with jax.named_scope("cores"):
+        data = jnp.concatenate([data * sign + other, data_2 * sign + other_2])
     with jax.named_scope("first_exchange"):
-        data = lax.all_to_all(data.reshape(64, 2, 2, 32, 128), ("x", "zh", "core", "y"), 0, 0, tiled=True)
+        data = lax.all_to_all(data.reshape(32, 256, 128), ("x", "zh", "y"), 0, 0, tiled=True)
     with jax.named_scope("middle"):
-        data = middle(data.reshape(4, 2, 2, 4, 2, 2, 4, 8, 128))
+        data = middle(scalars, data.reshape(4, 2, 4, 2, 2, 4, 16, 128))
     with jax.named_scope("second_exchange"):
-        data = lax.all_to_all(data.reshape(32, 256, 128), ("x", "zh", "core", "zl"), 0, 0, tiled=True)
+        data = lax.all_to_all(data.reshape(16, 512, 128), ("x", "zh", "zl"), 0, 0, tiled=True)
     with jax.named_scope("rows"):
         return row_transform(data)
 

time: 137 us -> 160 us (1.17)
  waiting for transfers between devices: 0 us -> 68.3 us
  blocking collectives: 121 us -> 54.8 us
  starting transfers between devices: 0 us -> 11.4 us
  other arithmetic: 0.06 us -> 7.11 us
  Pallas kernels: 15.1 us -> 17.6 us
    all_to_all x2 -> x1, blocking collectives: 121 us -> 54.8 us  [on_device(): lax.all_to_all(data.reshape(16, 512, 128), ('x', 'zh', 'zl'), 0, 0, tiled...]
    all_to_all x0 -> x1, waiting for transfers between devices: none -> 62.5 us  [on_device(): lax.all_to_all(data.reshape(32, 256, 128), ('x', 'zh', 'y'), 0, 0, tiled=...]
    all_to_all x0 -> x1, starting transfers between devices: none -> 10.8 us  [on_device(): lax.all_to_all(data.reshape(32, 256, 128), ('x', 'zh', 'y'), 0, 0, tiled=...]
    ppermute x0 -> x2, waiting for transfers between devices: none -> 5.84 us  [on_device(): swap = lambda value: lax.ppermute(value, 'core', [(0, 1), (1, 0)])]
    add x0 -> x2, other arithmetic: none -> 4.67 us  [on_device(): data = jnp.concatenate([data * sign + other, data_2 * sign + other_2])]
    pallas_call x2 -> x3, Pallas kernels: 9.28 us -> 11.8 us  [the longest x1 5.7 us: first_half(): pl.pallas_call(first_half_kernel, grid=(STEPS + 1,), in_specs=[pl.BlockSp...]
    concatenate x0 -> x1, other arithmetic: none -> 2.32 us  [on_device(): data = jnp.concatenate([data * sign + other, data_2 * sign + other_2])]
  transfers between devices with their start and end apart: 0 -> 3, of which waited for: 0 -> 2; matrix products, arithmetic and copies ran while one was open for 0% -> 1% of each run, Pallas kernels for 0% -> 0%
where the time goes in v4:
time: 160 us
  waiting for transfers between devices  68.3 us (43%)
  blocking collectives  54.8 us (34%)
  Pallas kernels  17.6 us (11%)
  starting transfers between devices  11.4 us (7%)
  other arithmetic  7.11 us (4%)
    all_to_all x1, waiting for transfers between devices, on_device(): lax.all_to_all(data.reshape(32, 256, 128), ('x', 'zh', 'y'), 0, 0, tiled=...  62.5 us
    all_to_all x1, blocking collectives, on_device(): lax.all_to_all(data.reshape(16, 512, 128), ('x', 'zh', 'zl'), 0, 0, tiled...  54.8 us
    all_to_all x1, starting transfers between devices, on_device(): lax.all_to_all(data.reshape(32, 256, 128), ('x', 'zh', 'y'), 0, 0, tiled=...  10.8 us
    ppermute x2, waiting for transfers between devices, on_device(): swap = lambda value: lax.ppermute(value, 'core', [(0, 1), (1, 0)])  5.84 us
    pallas_call x1, Pallas kernels, row_transform(): pl.pallas_call(row_kernel, grid=(4,), in_specs=[IN_VMEM] * 4, out_specs=p...  5.77 us
    pallas_call x1, Pallas kernels, first_half(): pl.pallas_call(first_half_kernel, grid=(STEPS + 1,), in_specs=[pl.BlockSp...  5.7 us
    add x2, other arithmetic, on_device(): data = jnp.concatenate([data * sign + other, data_2 * sign + other_2])  4.67 us
    pallas_call x1, Pallas kernels, middle(): pl.pallas_call(middle_kernel, in_specs=[pl.BlockSpec(memory_space=pltpu.S...  3.37 us
  transfers between devices with their start and end apart: 3, of which 2 were waited for; matrix products, arithmetic and copies ran while one was open for 1% of the time, Pallas kernels for 0%

profile of v4, /device:TPU:0, one launch (start us, length us, event | category | flops | bytes accessed | tf_op | source)
XLA Modules:
  0.0 159.8 jit_solution(13928854518626811278)
XLA Ops:
  0.1 0.2 broadcast_in_dim.2.turn
  0.3 5.7 %columns.2 = (f32[4,4,2,2,4,16,128]{6,5,4,3,2,1,0:T(8,128)}, bf16[4,256,768]{2,1,0:T(8,128)(2,1)S(1)}, s32[2,2,512,256]{3,2,1,0:T(8,128)S(1)}, f32[2,512,256]{2,1,0:T(8,128)S(1)}) custom-call(s32[2,512,1024]{2,1,0:T(8,128)} %noise.1, f32[512,1024]{1,0:T(8,128)} %eigen.1, f32[2,4,128,128]{3,2,1,0:T(8,128)} %constant.57.clone.base, ...), custom_call_target="tpu_custom_call" | custom-call | flops 1000000000 | bytes 12582912 | tf_op jit(solution)/shard_map/columns/pallas_call | solution.py:223
  6.0 2.8 %columns.3 = f32[4,4,2,2,4,16,128]{6,5,4,3,2,1,0:T(8,128)S(1)} custom-call(s32[2,2,512,256]{3,2,1,0:T(8,128)S(1)} %get-tuple-element.10.bits, f32[2,512,256]{2,1,0:T(8,128)S(1)} %get-tuple-element.11.eig, bf16[4,256,768]{2,1,0:T(8,128)(2,1)S(1)} %get-tuple-element.12.tables), custom_call_target="tpu_custom_call" | custom-call | flops 1000000000 | bytes 8388608 | tf_op jit(solution)/shard_map/columns/pallas_call | solution.py:247
  8.8 0.1 collective-permute-start.1
  8.8 0.5 collective-permute-start
  9.3 5.8 %collective-permute-done.1 = f32[4,4,2,2,4,16,128]{6,5,4,3,2,1,0:T(8,128)} collective-permute-done((f32[4,4,2,2,4,16,128]{6,5,4,3,2,1,0:T(8,128)S(1)}, f32[4,4,2,2,4,16,128]{6,5,4,3,2,1,0:T(8,128)}, u32[]{:S(2)}, u32[]{:S(2)}) %collective-permute-start.1) | collective-permute-done | bytes 2097184 | tf_op jit(solution)/shard_map/columns/ppermute | solution.py:339
  15.2 2.0 %multiply_add_fusion = f32[4,4,2,2,4,16,128]{6,5,4,3,2,1,0:T(8,128)S(1)} fusion(f32[4,4,2,2,4,16,128]{6,5,4,3,2,1,0:T(8,128)} %collective-permute-done.1, f32[4,4,2,2,4,16,128]{6,5,4,3,2,1,0:T(8,128)S(1)} %columns.3, f32[]{:T(128)S(6)} %convert_element_type.33), kind=kLoop, calls=%fused_computation.1 | loop fusion | flops 1048576 | bytes 6291460 | tf_op jit(solution)/shard_map/cores/add | solution.py:346
  17.2 0.0 collective-permute-done
  17.2 2.7 %multiply_add_fusion.1 = f32[4,4,2,2,4,16,128]{6,5,4,3,2,1,0:T(8,128)S(1)} fusion(f32[4,4,2,2,4,16,128]{6,5,4,3,2,1,0:T(8,128)} %collective-permute-done, f32[4,4,2,2,4,16,128]{6,5,4,3,2,1,0:T(8,128)} %get-tuple-element.9, f32[]{:T(128)S(6)} %convert_element_type.33), kind=kLoop, calls=%fused_computation.2 | loop fusion | flops 1048576 | bytes 6291460 | tf_op jit(solution)/shard_map/cores/add | solution.py:346
  19.9 2.3 %pad_maximum_fusion = f32[8,4,2,2,4,16,128]{6,5,4,3,2,1,0:T(8,128)} fusion(f32[4,4,2,2,4,16,128]{6,5,4,3,2,1,0:T(8,128)S(1)} %multiply_add_fusion, f32[4,4,2,2,4,16,128]{6,5,4,3,2,1,0:T(8,128)S(1)} %multiply_add_fusion.1), kind=kLoop, calls=%fused_computation | loop fusion | flops 1048576 | bytes 8388608 | tf_op jit(solution)/shard_map/cores/concatenate | solution.py:346
  22.2 10.8 %all-to-all-start = ((f32[32,256,128]{2,1,0:T(8,128)}), f32[32,256,128]{2,1,0:T(8,128)}, u32[]{:S(2)}, u32[]{:S(2)}) async-start(f32[32,256,128]{2,1,0:T(8,128)} %bitcast.11), calls=%async_computation | async-start | bytes 8388608 | tf_op jit(solution)/shard_map/first_exchange/all_to_all | solution.py:348
  33.1 0.1 copy.7
  33.2 0.1 reshape.116.scalars
  33.3 62.5 %all-to-all-done = f32[32,256,128]{2,1,0:T(8,128)} async-done(((f32[32,256,128]{2,1,0:T(8,128)}), f32[32,256,128]{2,1,0:T(8,128)}, u32[]{:S(2)}, u32[]{:S(2)}) %all-to-all-start) | async-done | bytes 4194336 | tf_op jit(solution)/shard_map/first_exchange/all_to_all | solution.py:348
  95.7 3.4 %middle.1 = f32[8192,128]{1,0:T(8,128)S(1)} custom-call(f32[16]{0:T(128)S(1)} %reshape.116.scalars, f32[4,2,4,2,2,4,16,128]{7,6,5,4,3,2,1,0:T(8,128)} %bitcast.1.data), custom_call_target="tpu_custom_call" | custom-call | flops 10000000 | bytes 8388608 | tf_op jit(solution)/shard_map/middle/pallas_call | solution.py:284
  99.1 0.0 copy-start
  99.1 0.0 copy-start.1
  99.1 0.0 copy-start.2
  99.1 54.8 %all_to_all.10 = f32[16,512,128]{2,1,0:T(8,128)S(1)} all-to-all(f32[16,512,128]{2,1,0:T(8,128)S(1)} %bitcast.9), channel_id=1, replica_groups=mesh['x'=4,'zh'=2,'core'=2,'zl'=2,'y'=4] {'x','zh','zl'}, dimensions={0} | all-to-all | bytes 8388608 | tf_op jit(solution)/shard_map/second_exchange/all_to_all | solution.py:352
  154.0 0.0 copy-done
  154.0 0.0 copy-done.1
  154.0 0.0 copy-done.2
  154.0 5.8 %rows.1 = f32[2,4096,128]{2,1,0:T(8,128)} custom-call(f32[8,2,4,16,8,128]{5,4,3,2,1,0:T(8,128)S(1)} %bitcast.10, bf16[256,256]{1,0:T(8,128)(2,1)S(1)} %copy-done.2, f32[2,128,128]{2,1,0:T(8,128)S(1)} %copy-done.1, bf16[256,256]{1,0:T(8,128)(2,1)S(1)} %copy-done), custom_call_target="tpu_custom_call" | custom-call | flops 3000000000 | bytes 9437184 | tf_op jit(solution)/shard_map/rows/pallas_call | solution.py:318
  (5 shorter events, 0.1 us)
Async XLA Ops:
  8.8 6.4 %collective-permute-start.1 = (f32[4,4,2,2,4,16,128]{6,5,4,3,2,1,0:T(8,128)S(1)}, f32[4,4,2,2,4,16,128]{6,5,4,3,2,1,0:T(8,128)}, u32[]{:S(2)}, u32[]{:S(2)}) collective-permute-start(f32[4,4,2,2,4,16,128]{6,5,4,3,2,1,0:T(8,128)S(1)} %columns.3), channel_id=1, source_target_pairs={{0,8},{8,0},{1,9},{9,1},{2,10},{10,2},{3,11},{11,3},{4,12},{12,4},... | collective-permute-start | bytes 6291464 | tf_op jit(solution)/shard_map/columns/ppermute | solution.py:339
  8.8 8.4 %collective-permute-start = (f32[4,4,2,2,4,16,128]{6,5,4,3,2,1,0:T(8,128)}, f32[4,4,2,2,4,16,128]{6,5,4,3,2,1,0:T(8,128)}, u32[]{:S(2)}, u32[]{:S(2)}) collective-permute-start(f32[4,4,2,2,4,16,128]{6,5,4,3,2,1,0:T(8,128)} %get-tuple-element.9), channel_id=1, source_target_pairs={{0,8},{8,0},{1,9},{9,1},{2,10},{10,2},{3,11},{11,3},{4,12},{12,4},... | collective-permute-start | bytes 6291464 | tf_op jit(solution)/shard_map/columns/ppermute | solution.py:339
  22.2 73.5 %all-to-all-start = ((f32[32,256,128]{2,1,0:T(8,128)}), f32[32,256,128]{2,1,0:T(8,128)}, u32[]{:S(2)}, u32[]{:S(2)}) async-start(f32[32,256,128]{2,1,0:T(8,128)} %bitcast.11), calls=%async_computation | async-start | bytes 8388608 | tf_op jit(solution)/shard_map/first_exchange/all_to_all | solution.py:348
  99.1 54.9 %copy-start = (bf16[256,256]{1,0:T(8,128)(2,1)S(1)}, bf16[256,256]{1,0:T(8,128)(2,1)}, u32[]{:S(2)}) copy-start(bf16[256,256]{1,0:T(8,128)(2,1)} %constant.60.clone.last) | copy-start | bytes 393220
  99.1 54.9 %copy-start.1 = (f32[2,128,128]{2,1,0:T(8,128)S(1)}, f32[2,128,128]{2,1,0:T(8,128)}, u32[]{:S(2)}) copy-start(f32[2,128,128]{2,1,0:T(8,128)} %constant.59.clone.twist) | copy-start | bytes 393220
  99.1 54.9 %copy-start.2 = (bf16[256,256]{1,0:T(8,128)(2,1)S(1)}, bf16[256,256]{1,0:T(8,128)(2,1)}, u32[]{:S(2)}) copy-start(bf16[256,256]{1,0:T(8,128)(2,1)} %constant.58.clone.first) | copy-start | bytes 393220

commit v5 on v4

--- a/solution.py
+++ b/solution.py
@@ -238,7 +238,7 @@
             VALUES,
             pltpu.SemaphoreType.DMA((4 * STEPS + 1,)),
         ],
-        compiler_params=pltpu.CompilerParams(vmem_limit_bytes=40 * 2**20),
+        compiler_params=pltpu.CompilerParams(vmem_limit_bytes=16 * 2**20),
         cost_estimate=pl.CostEstimate(flops=10**9, bytes_accessed=12 * 2**20, transcendentals=0),
     )(*(pltpu.with_memory_space_constraint(value, pltpu.HBM) for value in (noise, eigen, base)), turn)
 
@@ -251,9 +251,33 @@
         out_specs=HALF_OUT,
         out_shape=HALF_SHAPE,
         scratch_shapes=[VALUES],
-        compiler_params=pltpu.CompilerParams(vmem_limit_bytes=40 * 2**20),
-        cost_estimate=pl.CostEstimate(flops=10**9, bytes_accessed=8 * 2**20, transcendentals=0),
+        compiler_params=pltpu.CompilerParams(vmem_limit_bytes=10 * 2**20),
+        cost_estimate=pl.CostEstimate(flops=2 * 10**10, bytes_accessed=8 * 2**20, transcendentals=0),
     )(bits, eig, tables)
+
+
+def cores_kernel(half, sign, mine, other, *refs):
+    out = refs[-1]
+
+    def step(i, carry):
+        at = pl.ds(pl.multiple_of(128 * i, 128), 128)
+        out[half, at, :] = mine[at, :] * sign[0] + other[at, :]
+        return carry
+
+    lax.fori_loop(0, 32, step, 0)
+
+
+def add_cores(half, result, sign, mine, other):
+    operands = [sign, mine.reshape(4096, 128), other.reshape(4096, 128)]
+    return pl.pallas_call(
+        functools.partial(cores_kernel, half),
+        in_specs=[pl.BlockSpec(memory_space=pltpu.SMEM)] + [IN_VMEM] * (2 + half),
+        out_specs=IN_VMEM,
+        out_shape=jax.ShapeDtypeStruct((2, 4096, 128), F32),
+        input_output_aliases={3: 0} if half else {},
+        compiler_params=pltpu.CompilerParams(vmem_limit_bytes=8 * 2**20),
+        cost_estimate=pl.CostEstimate(flops=10**6, bytes_accessed=6 * 2**20, transcendentals=0),
+    )(*operands, *([result] * half))
 
 
 def middle_kernel(scalars, data, out):
@@ -286,7 +310,7 @@
         in_specs=[pl.BlockSpec(memory_space=pltpu.SMEM), IN_VMEM],
         out_specs=IN_VMEM,
         out_shape=jax.ShapeDtypeStruct((8192, 128), F32),
-        compiler_params=pltpu.CompilerParams(vmem_limit_bytes=32 * 2**20),
+        compiler_params=pltpu.CompilerParams(vmem_limit_bytes=6 * 2**20),
         cost_estimate=pl.CostEstimate(flops=10**7, bytes_accessed=8 * 2**20, transcendentals=0),
     )(scalars, data)
 
@@ -321,7 +345,7 @@
         in_specs=[IN_VMEM] * 4,
         out_specs=pl.BlockSpec((2, 1024, 128), lambda i: (0, i, 0)),
         out_shape=jax.ShapeDtypeStruct((2, 4096, 128), F32),
-        compiler_params=pltpu.CompilerParams(vmem_limit_bytes=48 * 2**20),
+        compiler_params=pltpu.CompilerParams(vmem_limit_bytes=16 * 2**20),
         cost_estimate=pl.CostEstimate(flops=3 * 10**9, bytes_accessed=9 * 2**20, transcendentals=0),
     )(data.reshape(8, 2, 4, 16, 8, 128), *tables)
     return result.reshape(2, 8, 64, 8, 128).transpose(0, 1, 3, 2, 4).reshape(2, 64, M)
@@ -335,7 +359,7 @@
     turn = jnp.broadcast_to(jnp.stack([jnp.cos(angle), jnp.sin(angle)])[..., None], (2, 4, 128, 128))
     angle = (core * jnp.arange(8, dtype=jnp.int32)).astype(F32) * (-2.0 * math.pi / 16)
     scalars = jnp.stack([jnp.cos(angle), jnp.sin(angle)], 1).reshape(16)
-    sign = (1 - 2 * core).astype(F32)
+    sign = (1 - 2 * core).astype(F32).reshape(1)
     swap = lambda value: lax.ppermute(value, "core", [(0, 1), (1, 0)])
     with jax.named_scope("columns"):
         data, tables, bits, eig = first_half(noise, eigen, turn)
@@ -343,8 +367,10 @@
         data_2 = second_half(bits, eig, tables)
         other_2 = swap(data_2)
     with jax.named_scope("cores"):
-        data = jnp.concatenate([data * sign + other, data_2 * sign + other_2])
+        data = add_cores(0, None, sign, data, other)
+        data = add_cores(1, data, sign, data_2, other_2)
     with jax.named_scope("first_exchange"):
+        data, scalars = lax.optimization_barrier((data, scalars))
         data = lax.all_to_all(data.reshape(32, 256, 128), ("x", "zh", "y"), 0, 0, tiled=True)
     with jax.named_scope("middle"):
         data = middle(scalars, data.reshape(4, 2, 4, 2, 2, 4, 16, 128))

time: 160 us -> 142 us (0.89)
  waiting for transfers between devices: 68.3 us -> 1.18 us
  blocking collectives: 54.8 us -> 119 us
  starting transfers between devices: 11.4 us -> 0.64 us
  other arithmetic: 7.11 us -> 0.11 us
  Pallas kernels: 17.6 us -> 20.4 us
    all_to_all x1 -> x0, waiting for transfers between devices: 62.5 us -> none  [on_device(): lax.all_to_all(data.reshape(32, 256, 128), ('x', 'zh', 'y'), 0, 0, tiled=...]
    all_to_all x0 -> x1, blocking collectives: none -> 62.4 us  [on_device(): lax.all_to_all(data.reshape(32, 256, 128), ('x', 'zh', 'y'), 0, 0, tiled=...]
    all_to_all x1 -> x0, starting transfers between devices: 10.8 us -> none  [on_device(): lax.all_to_all(data.reshape(32, 256, 128), ('x', 'zh', 'y'), 0, 0, tiled=...]
    add x2 -> x0, other arithmetic: 4.67 us -> none  [on_device(): data = jnp.concatenate([data * sign + other, data_2 * sign + other_2])]
    ppermute x2, waiting for transfers between devices: 5.84 us -> 1.18 us  [on_device(): swap = lambda value: lax.ppermute(value, 'core', [(0, 1), (1, 0)])]
    pallas_call x0 -> x2, Pallas kernels: none -> 4.44 us  [add_cores(): pl.pallas_call(functools.partial(cores_kernel, half), in_specs=[pl.BlockS...]
    concatenate x1 -> x0, other arithmetic: 2.32 us -> none  [on_device(): data = jnp.concatenate([data * sign + other, data_2 * sign + other_2])]
    pallas_call x1, Pallas kernels: 3.37 us -> 1.72 us  [middle(): pl.pallas_call(middle_kernel, in_specs=[pl.BlockSpec(memory_space=pltpu.S...]
  transfers between devices with their start and end apart: 3 -> 2, of which waited for: 2 -> 2; matrix products, arithmetic and copies ran while one was open for 1% -> 0% of each run, Pallas kernels for 0% -> 4%
where the time goes in v5:
time: 142 us; the launch traced here: 141 us
  blocking collectives  119 us (84%)
  Pallas kernels  20.4 us (14%)
    all_to_all x1, blocking collectives, on_device(): lax.all_to_all(data.reshape(32, 256, 128), ('x', 'zh', 'y'), 0, 0, tiled=...  62.4 us
    all_to_all x1, blocking collectives, on_device(): lax.all_to_all(data.reshape(16, 512, 128), ('x', 'zh', 'zl'), 0, 0, tiled...  56.2 us
    pallas_call x1, Pallas kernels, row_transform(): pl.pallas_call(row_kernel, grid=(4,), in_specs=[IN_VMEM] * 4, out_specs=p...  5.77 us
    pallas_call x1, Pallas kernels, first_half(): pl.pallas_call(first_half_kernel, grid=(STEPS + 1,), in_specs=[pl.BlockSp...  5.7 us
    pallas_call x2, Pallas kernels, add_cores(): pl.pallas_call(functools.partial(cores_kernel, half), in_specs=[pl.BlockS...  4.44 us
  transfers between devices with their start and end apart: 2, of which 2 were waited for; matrix products, arithmetic and copies ran while one was open for 0% of the time, Pallas kernels for 4%

profile of v5, /device:TPU:0, one launch (start us, length us, event | category | flops | bytes accessed | tf_op | source)
XLA Modules:
  0.0 141.4 jit_solution(18288737943127516663)
XLA Ops:
  0.1 0.2 broadcast_in_dim.2.turn
  0.3 5.7 %columns.2 = (f32[4,4,2,2,4,16,128]{6,5,4,3,2,1,0:T(8,128)}, bf16[4,256,768]{2,1,0:T(8,128)(2,1)S(1)}, s32[2,2,512,256]{3,2,1,0:T(8,128)S(1)}, f32[2,512,256]{2,1,0:T(8,128)S(1)}) custom-call(s32[2,512,1024]{2,1,0:T(8,128)} %noise.1, f32[512,1024]{1,0:T(8,128)} %eigen.1, f32[2,4,128,128]{3,2,1,0:T(8,128)} %constant.57.clone.base, ...), custom_call_target="tpu_custom_call" | custom-call | flops 1000000000 | bytes 12582912 | tf_op jit(solution)/shard_map/columns/pallas_call | solution.py:223
  6.0 0.1 collective-permute-start.1
  6.1 2.8 %columns.3 = f32[4,4,2,2,4,16,128]{6,5,4,3,2,1,0:T(8,128)S(1)} custom-call(s32[2,2,512,256]{3,2,1,0:T(8,128)S(1)} %get-tuple-element.11.bits, f32[2,512,256]{2,1,0:T(8,128)S(1)} %get-tuple-element.12.eig, bf16[4,256,768]{2,1,0:T(8,128)(2,1)S(1)} %get-tuple-element.13.tables), custom_call_target="tpu_custom_call" | custom-call | flops 20000000000 | bytes 8388608 | tf_op jit(solution)/shard_map/columns/pallas_call | solution.py:247
  8.8 0.6 collective-permute-start
  9.5 0.1 copy.8
  9.5 0.1 reshape.136.scalars
  9.6 0.9 collective-permute-done.1
  10.6 2.5 %cores.2.refs_0_ = f32[2,4096,128]{2,1,0:T(8,128)S(1)} custom-call(f32[1]{0:T(128)} %bitcast.sign, f32[4096,128]{1,0:T(8,128)} %bitcast.3.mine, f32[4096,128]{1,0:T(8,128)} %bitcast.4.other), custom_call_target="tpu_custom_call" | custom-call | flops 1000000 | bytes 6291456 | tf_op jit(solution)/shard_map/cores/pallas_call | solution.py:272
  13.1 0.2 collective-permute-done
  13.3 1.9 %cores.3 = f32[2,4096,128]{2,1,0:T(8,128)S(1)} custom-call(f32[1]{0:T(128)} %bitcast.sign, f32[4096,128]{1,0:T(8,128)S(1)} %bitcast.18, f32[4096,128]{1,0:T(8,128)} %bitcast.2.other, f32[2,4096,128]{2,1,0:T(8,128)S(1)} %cores.2.refs_0_), custom_call_target="tpu_custom_call", output_to_operand_aliasing={{}: (3, {})} | custom-call | flops 1000000 | bytes 6291456 | tf_op jit(solution)/shard_map/cores/pallas_call | solution.py:272
  15.3 62.4 %all_to_all.10 = f32[32,256,128]{2,1,0:T(8,128)S(1)} all-to-all(f32[32,256,128]{2,1,0:T(8,128)S(1)} %bitcast.14), channel_id=1, replica_groups=mesh['x'=4,'zh'=2,'core'=2,'zl'=2,'y'=4] {'x','zh','y'}, dimensions={0} | all-to-all | bytes 8388608 | tf_op jit(solution)/shard_map/first_exchange/all_to_all | solution.py:374
  77.6 1.7 %middle.1 = f32[8192,128]{1,0:T(8,128)S(1)} custom-call(f32[16]{0:T(128)S(1)} %reshape.136.scalars, f32[4,2,4,2,2,4,16,128]{7,6,5,4,3,2,1,0:T(8,128)S(1)} %bitcast.15), custom_call_target="tpu_custom_call" | custom-call | flops 10000000 | bytes 8388608 | tf_op jit(solution)/shard_map/middle/pallas_call | solution.py:308
  79.4 0.0 copy-start
  79.4 0.0 copy-start.1
  79.4 0.0 copy-start.2
  79.4 56.2 %all_to_all.11 = f32[16,512,128]{2,1,0:T(8,128)S(1)} all-to-all(f32[16,512,128]{2,1,0:T(8,128)S(1)} %bitcast.16), channel_id=1, replica_groups=mesh['x'=4,'zh'=2,'core'=2,'zl'=2,'y'=4] {'x','zh','zl'}, dimensions={0} | all-to-all | bytes 8388608 | tf_op jit(solution)/shard_map/second_exchange/all_to_all | solution.py:378
  135.6 0.0 copy-done
  135.6 0.0 copy-done.1
  135.6 0.0 copy-done.2
  135.6 5.8 %rows.1 = f32[2,4096,128]{2,1,0:T(8,128)} custom-call(f32[8,2,4,16,8,128]{5,4,3,2,1,0:T(8,128)S(1)} %bitcast.17, bf16[256,256]{1,0:T(8,128)(2,1)S(1)} %copy-done.2, f32[2,128,128]{2,1,0:T(8,128)S(1)} %copy-done.1, bf16[256,256]{1,0:T(8,128)(2,1)S(1)} %copy-done), custom_call_target="tpu_custom_call" | custom-call | flops 3000000000 | bytes 9437184 | tf_op jit(solution)/shard_map/rows/pallas_call | solution.py:342
  (5 shorter events, 0.1 us)
Async XLA Ops:
  6.0 4.6 %collective-permute-start.1 = (f32[4,4,2,2,4,16,128]{6,5,4,3,2,1,0:T(8,128)}, f32[4,4,2,2,4,16,128]{6,5,4,3,2,1,0:T(8,128)}, u32[]{:S(2)}, u32[]{:S(2)}) collective-permute-start(f32[4,4,2,2,4,16,128]{6,5,4,3,2,1,0:T(8,128)} %get-tuple-element.14), channel_id=1, source_target_pairs={{0,8},{8,0},{1,9},{9,1},{2,10},{10,2},{3,11},{11,3},{4,12},{12,4},... | collective-permute-start | bytes 6291464 | tf_op jit(solution)/shard_map/columns/ppermute | solution.py:363
  8.8 4.5 %collective-permute-start = (f32[4,4,2,2,4,16,128]{6,5,4,3,2,1,0:T(8,128)S(1)}, f32[4,4,2,2,4,16,128]{6,5,4,3,2,1,0:T(8,128)}, u32[]{:S(2)}, u32[]{:S(2)}) collective-permute-start(f32[4,4,2,2,4,16,128]{6,5,4,3,2,1,0:T(8,128)S(1)} %columns.3), channel_id=1, source_target_pairs={{0,8},{8,0},{1,9},{9,1},{2,10},{10,2},{3,11},{11,3},{4,12},{12,4},... | collective-permute-start | bytes 6291464 | tf_op jit(solution)/shard_map/columns/ppermute | solution.py:363
  79.4 56.2 %copy-start = (bf16[256,256]{1,0:T(8,128)(2,1)S(1)}, bf16[256,256]{1,0:T(8,128)(2,1)}, u32[]{:S(2)}) copy-start(bf16[256,256]{1,0:T(8,128)(2,1)} %constant.60.clone.last) | copy-start | bytes 393220
  79.4 56.2 %copy-start.1 = (f32[2,128,128]{2,1,0:T(8,128)S(1)}, f32[2,128,128]{2,1,0:T(8,128)}, u32[]{:S(2)}) copy-start(f32[2,128,128]{2,1,0:T(8,128)} %constant.59.clone.twist) | copy-start | bytes 393220
  79.4 56.2 %copy-start.2 = (bf16[256,256]{1,0:T(8,128)(2,1)S(1)}, bf16[256,256]{1,0:T(8,128)(2,1)}, u32[]{:S(2)}) copy-start(bf16[256,256]{1,0:T(8,128)(2,1)} %constant.58.clone.first) | copy-start | bytes 393220

commit v6 on v3

--- a/solution.py
+++ b/solution.py
@@ -43,7 +43,8 @@
 
 
 def row_tables():
-    place = 8 * (4 * np.arange(2)[None, :, None] + np.arange(4)[None, None, :]) + np.arange(8)[:, None, None]
+    place = 8 * (4 * np.arange(2)[None, :, None] + np.arange(4)[None, None, :])
+    place = place + np.array([0, 2, 4, 6, 1, 3, 5, 7])[:, None, None]
     angle = 2.0 * np.pi * (np.arange(64)[:, None] * place.reshape(1, 64) % 64) / 64
     cosine, sine = np.cos(angle), np.sin(angle)
     real_part = np.stack([cosine, sine], -1).reshape(64, 128)
@@ -136,120 +137,100 @@
     return [second[k % 4][k // 4] for k in range(16)]
 
 
-def front_kernel(noise, eigen, base, turn, out, bits, eig, base_in, tables, values, arrived):
-    step = pl.program_id(0)
-
-    def copies():
-        for i in range(STEPS):
-            columns = slice(BLOCK * i, BLOCK * (i + 1))
-            yield pltpu.make_async_copy(noise.at[:, :, columns], bits.at[i], arrived.at[i])
-            yield pltpu.make_async_copy(eigen.at[:, columns], eig.at[i], arrived.at[STEPS + i])
-        yield pltpu.make_async_copy(base, base_in, arrived.at[2 * STEPS])
-
-    moves = list(copies())
-
-    def start():
-        for move in moves:
-            move.start()
-
-    def prepare():
-        moves[-1].wait()
-        for r in range(4):
-            cosine = base_in[0, r] * turn[0, r] - base_in[1, r] * turn[1, r]
-            sine = base_in[1, r] * turn[0, r] + base_in[0, r] * turn[1, r]
-            (cosine, cosine_low), (sine, sine_low) = split(cosine), split(sine)
-            for at, c, s in ((0, cosine, sine), (256, cosine, sine), (512, cosine_low, sine_low)):
-                tables[r, :128, at : at + 128] = c
-                tables[r, :128, at + 128 : at + 256] = s
-                tables[r, 128:, at : at + 128] = -s
-                tables[r, 128:, at + 128 : at + 256] = c
-
-    def wait(i):
-        moves[2 * i].wait()
-        moves[2 * i + 1].wait()
-
-    def draws():
+IN_VMEM = pl.BlockSpec(memory_space=pltpu.VMEM)
+
+
+def front_kernel(noise, eigen, base, turn, out, bits, eig, base_in, drawn, tables, values, arrived):
+    moves = [pltpu.make_async_copy(base, base_in, arrived.at[12])]
+    for g in range(4):
+        rows = slice(128 * g, 128 * (g + 1))
+        for part in range(2):
+            moves.append(pltpu.make_async_copy(noise.at[part, rows], bits.at[part, rows], arrived.at[3 * g + part]))
+        moves.append(pltpu.make_async_copy(eigen.at[rows], eig.at[rows], arrived.at[3 * g + 2]))
+    for move in moves:
+        move.start()
+
+    moves[0].wait()
+    for r in range(4):
+        cosine = base_in[0, r] * turn[0, r] - base_in[1, r] * turn[1, r]
+        sine = base_in[1, r] * turn[0, r] + base_in[0, r] * turn[1, r]
+        (cosine, cosine_low), (sine, sine_low) = split(cosine), split(sine)
+        for at, c, s in ((0, cosine, sine), (256, cosine, sine), (512, cosine_low, sine_low)):
+            tables[r, :128, at : at + 128] = c
+            tables[r, :128, at + 128 : at + 256] = s
+            tables[r, 128:, at : at + 128] = -s
+            tables[r, 128:, at + 128 : at + 256] = c
+
+    for g in range(3):
+        for move in moves[3 * g + 1 : 3 * g + 4]:
+            move.wait()
+
+        def draws(i, carry):
+            rows = pl.ds(pl.multiple_of(128 * g + 16 * i, 16), 16)
+            drawn[0, rows, :], drawn[1, rows, :] = draw(bits[0, rows, :], bits[1, rows, :], eig[rows, :])
+            return carry
+
+        lax.fori_loop(0, 8, draws, 0)
+
+    for move in moves[10:]:
+        move.wait()
+    for i in range(STEPS):
+        columns = slice(BLOCK * i, BLOCK * (i + 1))
         parts = [
-            draw(bits[step, 0, at, :], bits[step, 1, at, :], eig[step, at, :])
-            for at in (slice(128 * j, 128 * (j + 1)) for j in range(4))
+            (drawn[0, 128 * j : 128 * (j + 1), columns], drawn[1, 128 * j : 128 * (j + 1), columns]) for j in range(3)
         ]
+        parts.append(draw(bits[0, 384:, columns], bits[1, 384:, columns], eig[384:, columns]))
         for r, value in enumerate(dft_4(*parts)):
             for part in range(2):
                 high, low = split(value[part])
                 for at, half in ((0, high), (256, low), (512, high)):
-                    values[r, at + 128 * part : at + 128 * (part + 1), :] = half
-
-    def multiply():
+                    values[i, r, at + 128 * part : at + 128 * (part + 1), :] = half
         for r in range(4):
-            both = dot(tables[r], values[r])
+            both = dot(tables[r], values[i, r])
             for a in range(BLOCK // 128):
                 for row in range(0, 256, 8):
                     part, zl, y, b = row // 128, row // 64 % 2, row // 16 % 4, row // 8 % 2
-                    out[a, b, y, zl, part, r] = both[row : row + 8, 128 * a : 128 * (a + 1)]
-
-    @pl.when(step == 0)
-    def _():
-        start()
-        wait(0)
-        draws()
-        prepare()
-
-    for i in range(1, STEPS):
-        pl.when(step == i)(functools.partial(wait, i))
-
-    @pl.when(jnp.logical_and(step > 0, step < STEPS))
-    def _():
-        multiply()
-        draws()
-
-    pl.when(step == STEPS)(multiply)
+                    out[i, b, a, y, zl, part, r] = both[row : row + 8, 128 * a : 128 * (a + 1)]
 
 
 def front(noise, eigen, turn):
     base = jnp.asarray(column_table())
-    in_hbm = pl.BlockSpec(memory_space=pltpu.HBM)
     return pl.pallas_call(
         front_kernel,
-        grid=(STEPS + 1,),
-        in_specs=[in_hbm] * 3 + [pl.BlockSpec(memory_space=pltpu.VMEM)],
-        out_specs=pl.BlockSpec(
-            (BLOCK // 128, 2, 4, 2, 2, 4, 8, 128), lambda i: (jnp.maximum(i - 1, 0), 0, 0, 0, 0, 0, 0, 0)
-        ),
-        out_shape=jax.ShapeDtypeStruct((8, 2, 4, 2, 2, 4, 8, 128), F32),
+        in_specs=[pl.BlockSpec(memory_space=pltpu.HBM)] * 3 + [IN_VMEM],
+        out_specs=IN_VMEM,
+        out_shape=jax.ShapeDtypeStruct((4, 2, 2, 4, 2, 2, 4, 8, 128), F32),
         scratch_shapes=[
-            pltpu.VMEM((STEPS, 2, LOCAL, BLOCK), jnp.int32),
-            pltpu.VMEM((STEPS, LOCAL, BLOCK), F32),
+            pltpu.VMEM((2, LOCAL, WIDTH), jnp.int32),
+            pltpu.VMEM((LOCAL, WIDTH), F32),
             pltpu.VMEM((2, 4, 128, 128), F32),
+            pltpu.VMEM((2, 384, WIDTH), F32),
             pltpu.VMEM((4, 256, 768), BF16),
-            pltpu.VMEM((4, 768, BLOCK), BF16),
-            pltpu.SemaphoreType.DMA((2 * STEPS + 1,)),
+            pltpu.VMEM((STEPS, 4, 768, BLOCK), BF16),
+            pltpu.SemaphoreType.DMA((13,)),
         ],
-        compiler_params=pltpu.CompilerParams(vmem_limit_bytes=40 * 2**20),
+        compiler_params=pltpu.CompilerParams(vmem_limit_bytes=32 * 2**20),
         cost_estimate=pl.CostEstimate(flops=2 * 10**9, bytes_accessed=12 * 2**20, transcendentals=0),
     )(*(pltpu.with_memory_space_constraint(value, pltpu.HBM) for value in (noise, eigen, base)), turn)
 
 
-IN_VMEM = pl.BlockSpec(memory_space=pltpu.VMEM)
-
-
 def middle_kernel(data, out):
     def step(at, carry):
-        zl, r = at // 4, at % 4
-        for y in range(4):
-            values = []
+        for y, zl in ((y, zl) for y in range(4) for zl in range(2)):
+            r, values = at, []
             for e in range(16):
                 core, zh, xl, xh = e >> 3, e >> 2 & 1, e >> 1 & 1, e & 1
-                index = (2 * xh + xl, zh, core, y, zl)
+                index = (2 * xh + xl, core, zh, y, zl)
                 values.append((data[*index, 0, r], data[*index, 1, r]))
             for k, value in enumerate(dft_16(values)):
                 core, zh, xl, xh = k & 1, k >> 1 & 1, k >> 2 & 1, k >> 3
-                place = 4 * (2 * xh + xl) + 2 * zh + core
-                row = pl.multiple_of(512 * place + 64 * at, 64)
+                place = 4 * zh + 2 * xh + xl
+                row = pl.multiple_of(1024 * place + 512 * zl + 256 * core + 64 * r, 64)
                 for part in range(2):
                     out[pl.ds(row + 2 * y + part, 8, stride=8), :] = value[part]
         return carry
 
-    lax.fori_loop(0, 8, step, 0)
+    lax.fori_loop(0, 4, step, 0)
 
 
 def middle(data):
@@ -263,26 +244,31 @@
     )(data)
 
 
+GROUP = 16
+
+
 def row_kernel(data, first, twist, last, out):
     step = pl.program_id(0)
 
     def piece(t):
-        return data[:, step // 2, :, t % 4, 4 * (step % 2) + t // 4].reshape(128, 128)
-
-    high, low = split(jnp.concatenate([piece(t) for t in range(16)], 1))
-    sums = dot(first[...], jnp.concatenate([high, low], 0))
-    sums = sums[:128] + sums[128:]
-    for t in range(16):
-        re, im = sums[:64, 128 * t : 128 * (t + 1)], sums[64:, 128 * t : 128 * (t + 1)]
-        both = []
-        for v in range(2):
-            c, s = twist[0, 64 * v : 64 * (v + 1), :], twist[1, 64 * v : 64 * (v + 1), :]
-            both.append(jnp.concatenate([re * c - im * s, re * s + im * c], 1))
-        high, low = split(jnp.concatenate(both, 0))
-        whole = dot(high, last[...])
-        whole = (whole[:, :128] + whole[:, 128:] + dot(low, last[:, :128])).T
-        for part in range(2):
-            out[part, pl.ds(512 * (t // 8) + t % 8, 64, stride=8), :] = whole[64 * part : 64 * (part + 1)]
+        return data[:, :, step // 2, t % 4, 4 * (step % 2) + t // 4].reshape(128, 128)
+
+    for group in range(0, 16, GROUP):
+        high, low = split(jnp.concatenate([piece(t) for t in range(group, group + GROUP)], 1))
+        sums = dot(first[...], jnp.concatenate([high, low], 0))
+        sums = sums[:128] + sums[128:]
+        for t in range(group, group + GROUP):
+            at = slice(128 * (t - group), 128 * (t - group + 1))
+            re, im = sums[:64, at], sums[64:, at]
+            both = []
+            for v in range(2):
+                c, s = twist[0, 64 * v : 64 * (v + 1), :], twist[1, 64 * v : 64 * (v + 1), :]
+                both.append(jnp.concatenate([re * c - im * s, re * s + im * c], 1))
+            high, low = split(jnp.concatenate(both, 0))
+            whole = dot(high, last[...])
+            whole = (whole[:, :128] + whole[:, 128:] + dot(low, last[:, :128])).T
+            for part in range(2):
+                out[part, pl.ds(512 * (t // 8) + t % 8, 64, stride=8), :] = whole[64 * part : 64 * (part + 1)]
 
 
 def row_transform(data):
@@ -293,7 +279,7 @@
         in_specs=[IN_VMEM] * 4,
         out_specs=pl.BlockSpec((2, 1024, 128), lambda i: (0, i, 0)),
         out_shape=jax.ShapeDtypeStruct((2, 4096, 128), F32),
-        compiler_params=pltpu.CompilerParams(vmem_limit_bytes=48 * 2**20),
+        compiler_params=pltpu.CompilerParams(vmem_limit_bytes=16 * 2**20),
         cost_estimate=pl.CostEstimate(flops=3 * 10**9, bytes_accessed=9 * 2**20, transcendentals=0),
     )(data.reshape(8, 2, 2, 4, 8, 8, 128), *tables)
     return result.reshape(2, 8, 64, 8, 128).transpose(0, 1, 3, 2, 4).reshape(2, 64, M)
@@ -308,11 +294,11 @@
     with jax.named_scope("columns"):
         data = front(noise, eigen, turn)
     with jax.named_scope("first_exchange"):
-        data = lax.all_to_all(data.reshape(64, 2, 2, 32, 128), ("x", "zh", "core", "y"), 0, 0, tiled=True)
+        data = lax.all_to_all(data.reshape(64, 2, 2, 32, 128), ("x", "core", "zh", "y"), 0, 0, tiled=True)
     with jax.named_scope("middle"):
         data = middle(data.reshape(4, 2, 2, 4, 2, 2, 4, 8, 128))
     with jax.named_scope("second_exchange"):
-        data = lax.all_to_all(data.reshape(32, 256, 128), ("x", "zh", "core", "zl"), 0, 0, tiled=True)
+        data = lax.all_to_all(data.reshape(32, 256, 128), ("zh", "x", "zl", "core"), 0, 0, tiled=True)
     with jax.named_scope("rows"):
         return row_transform(data)
 

time: 137 us -> 134 us (0.978)
  Pallas kernels: 15.1 us -> 13.5 us
    pallas_call x1, Pallas kernels: 7.92 us -> 6.4 us  [front(): pl.pallas_call(front_kernel, in_specs=[pl.BlockSpec(memory_space=pltpu.HB...]
    all_to_all x2, blocking collectives: 121 us -> 120 us  [the longest x1 62.3 us: on_device(): lax.all_to_all(data.reshape(64, 2, 2, 32, 128), ('x', 'core', 'zh', 'y'),...]
where the time goes in v6:
time: 134 us; the launch traced here: 133 us
  blocking collectives  120 us (90%)
  Pallas kernels  13.5 us (10%)
    all_to_all x1, blocking collectives, on_device(): lax.all_to_all(data.reshape(64, 2, 2, 32, 128), ('x', 'core', 'zh', 'y'),...  62.3 us
    all_to_all x1, blocking collectives, on_device(): lax.all_to_all(data.reshape(32, 256, 128), ('zh', 'x', 'zl', 'core'), 0,...  57.3 us
    pallas_call x1, Pallas kernels, front(): pl.pallas_call(front_kernel, in_specs=[pl.BlockSpec(memory_space=pltpu.HB...  6.4 us
    pallas_call x1, Pallas kernels, row_transform(): pl.pallas_call(row_kernel, grid=(4,), in_specs=[IN_VMEM] * 4, out_specs=p...  5.8 us

profile of v6, /device:TPU:0, one launch (start us, length us, event | category | flops | bytes accessed | tf_op | source)
XLA Modules:
  0.0 133.5 jit_solution(11440632346315136864)
XLA Ops:
  0.1 0.2 broadcast_in_dim.2.turn
  0.3 6.4 %columns.1 = f32[4,2,2,4,2,2,4,8,128]{8,7,6,5,4,3,2,1,0:T(8,128)S(1)} custom-call(s32[2,512,1024]{2,1,0:T(8,128)} %noise.1, f32[512,1024]{1,0:T(8,128)} %eigen.1, f32[2,4,128,128]{3,2,1,0:T(8,128)} %constant.54.clone.base, f32[2,4,128,128]{3,2,1,0:T(8,128)S(1)} %broadcast_in_dim.2.turn), custom_call_target="tpu_custom_call" | custom-call | flops 2000000000 | bytes 12582912 | tf_op jit(solution)/shard_map/columns/pallas_call | solution.py:198
  6.7 62.3 %all_to_all.10 = f32[64,2,2,32,128]{4,3,2,1,0:T(8,128)S(1)} all-to-all(f32[64,2,2,32,128]{4,3,2,1,0:T(8,128)S(1)} %bitcast.11), channel_id=1, replica_groups=mesh['x'=4,'zh'=2,'core'=2,'zl'=2,'y'=4] {'x','core','zh','y'}, dimensions={0} | all-to-all | bytes 8388608 | tf_op jit(solution)/shard_map/first_exchange/all_to_all | solution.py:297
  69.0 1.3 middle.1
  70.3 0.0 copy-start
  70.3 0.0 copy-start.1
  70.3 0.0 copy-start.2
  70.3 57.3 %all_to_all.11 = f32[32,256,128]{2,1,0:T(8,128)S(1)} all-to-all(f32[32,256,128]{2,1,0:T(8,128)S(1)} %bitcast.10), channel_id=1, replica_groups=mesh['x'=4,'zh'=2,'core'=2,'zl'=2,'y'=4] {'zh','x','zl','core'}, dimensions={0} | all-to-all | bytes 8388608 | tf_op jit(solution)/shard_map/second_exchange/all_to_all | solution.py:301
  127.7 0.0 copy-done
  127.7 0.0 copy-done.1
  127.7 0.0 copy-done.2
  127.7 5.8 %rows.1 = f32[2,4096,128]{2,1,0:T(8,128)} custom-call(f32[8,2,2,4,8,8,128]{6,5,4,3,2,1,0:T(8,128)S(1)} %bitcast.12, bf16[256,256]{1,0:T(8,128)(2,1)S(1)} %copy-done.2, f32[2,128,128]{2,1,0:T(8,128)S(1)} %copy-done.1, bf16[256,256]{1,0:T(8,128)(2,1)S(1)} %copy-done), custom_call_target="tpu_custom_call" | custom-call | flops 3000000000 | bytes 9437184 | tf_op jit(solution)/shard_map/rows/pallas_call | solution.py:276
  (3 shorter events, 0.1 us)
Async XLA Ops:
  70.3 57.4 %copy-start = (bf16[256,256]{1,0:T(8,128)(2,1)S(1)}, bf16[256,256]{1,0:T(8,128)(2,1)}, u32[]{:S(2)}) copy-start(bf16[256,256]{1,0:T(8,128)(2,1)} %constant.57.clone.last) | copy-start | bytes 393220
  70.3 57.3 %copy-start.1 = (f32[2,128,128]{2,1,0:T(8,128)S(1)}, f32[2,128,128]{2,1,0:T(8,128)}, u32[]{:S(2)}) copy-start(f32[2,128,128]{2,1,0:T(8,128)} %constant.56.clone.twist) | copy-start | bytes 393220
  70.3 57.3 %copy-start.2 = (bf16[256,256]{1,0:T(8,128)(2,1)S(1)}, bf16[256,256]{1,0:T(8,128)(2,1)}, u32[]{:S(2)}) copy-start(bf16[256,256]{1,0:T(8,128)(2,1)} %constant.55.clone.first) | copy-start | bytes 393220

commit v7 on v6

--- a/solution.py
+++ b/solution.py
@@ -36,10 +36,12 @@
     return high, low
 
 
-def column_table():
-    row = 4 * np.arange(128)[None, :, None] + np.arange(4)[:, None, None]
-    angle = 2.0 * np.pi * (row * np.arange(128) % LOCAL) / LOCAL
-    return np.stack([np.cos(angle), np.sin(angle)]).astype(np.float32)
+def column_tables():
+    e, r, m, j = np.ix_(np.arange(16), np.arange(4), np.arange(128), np.arange(128))
+    angle = 2.0 * np.pi * ((4 * m + r) * (16 * j + e) % N) / N
+    cosine, sine = np.cos(angle), np.sin(angle)
+    table = np.concatenate([np.concatenate([cosine, sine], -1), np.concatenate([-sine, cosine], -1)], -2)
+    return np.concatenate(halves(table), -1)
 
 
 def row_tables():
@@ -140,78 +142,81 @@
 IN_VMEM = pl.BlockSpec(memory_space=pltpu.VMEM)
 
 
-def front_kernel(noise, eigen, base, turn, out, bits, eig, base_in, drawn, tables, values, arrived):
-    moves = [pltpu.make_async_copy(base, base_in, arrived.at[12])]
-    for g in range(4):
-        rows = slice(128 * g, 128 * (g + 1))
+def front_kernel(noise, eigen, all_tables, out, bits, eig, drawn, tables, values, arrived):
+    moves = []
+    for g in range(8):
+        rows = slice(64 * g, 64 * (g + 1))
         for part in range(2):
             moves.append(pltpu.make_async_copy(noise.at[part, rows], bits.at[part, rows], arrived.at[3 * g + part]))
         moves.append(pltpu.make_async_copy(eigen.at[rows], eig.at[rows], arrived.at[3 * g + 2]))
+    x, zh, core = (lax.axis_index(name) for name in AXES[:3])
+    digit = 8 * core + 4 * zh + 2 * (x % 2) + x // 2
+    moves.append(pltpu.make_async_copy(all_tables.at[digit], tables, arrived.at[24]))
     for move in moves:
         move.start()
 
-    moves[0].wait()
-    for r in range(4):
-        cosine = base_in[0, r] * turn[0, r] - base_in[1, r] * turn[1, r]
-        sine = base_in[1, r] * turn[0, r] + base_in[0, r] * turn[1, r]
-        (cosine, cosine_low), (sine, sine_low) = split(cosine), split(sine)
-        for at, c, s in ((0, cosine, sine), (256, cosine, sine), (512, cosine_low, sine_low)):
-            tables[r, :128, at : at + 128] = c
-            tables[r, :128, at + 128 : at + 256] = s
-            tables[r, 128:, at : at + 128] = -s
-            tables[r, 128:, at + 128 : at + 256] = c
-
-    for g in range(3):
-        for move in moves[3 * g + 1 : 3 * g + 4]:
+    for g in range(4):
+        for move in moves[3 * g : 3 * g + 3]:
             move.wait()
 
         def draws(i, carry):
-            rows = pl.ds(pl.multiple_of(128 * g + 16 * i, 16), 16)
+            rows = pl.ds(pl.multiple_of(64 * g + 32 * i, 32), 32)
             drawn[0, rows, :], drawn[1, rows, :] = draw(bits[0, rows, :], bits[1, rows, :], eig[rows, :])
             return carry
 
-        lax.fori_loop(0, 8, draws, 0)
-
-    for move in moves[10:]:
+        lax.fori_loop(0, 2, draws, 0)
+
+    for move in moves[12:]:
         move.wait()
-    for i in range(STEPS):
+
+    def prepare(i):
         columns = slice(BLOCK * i, BLOCK * (i + 1))
         parts = [
-            (drawn[0, 128 * j : 128 * (j + 1), columns], drawn[1, 128 * j : 128 * (j + 1), columns]) for j in range(3)
+            (drawn[0, 128 * j : 128 * (j + 1), columns], drawn[1, 128 * j : 128 * (j + 1), columns]) for j in range(2)
         ]
-        parts.append(draw(bits[0, 384:, columns], bits[1, 384:, columns], eig[384:, columns]))
+        for j in range(2, 4):
+            at = slice(128 * j, 128 * (j + 1))
+            parts.append(draw(bits[0, at, columns], bits[1, at, columns], eig[at, columns]))
         for r, value in enumerate(dft_4(*parts)):
             for part in range(2):
                 high, low = split(value[part])
-                for at, half in ((0, high), (256, low), (512, high)):
+                for at, half in ((0, high), (256, low)):
                     values[i, r, at + 128 * part : at + 128 * (part + 1), :] = half
+
+    def multiply(i):
         for r in range(4):
-            both = dot(tables[r], values[i, r])
+            table, value = tables[r, :, :256], values[i, r, :256, :]
+            both = dot(table, values[i, r, :256, :]) + dot(table, values[i, r, 256:, :]) + dot(tables[r, :, 256:], value)
             for a in range(BLOCK // 128):
                 for row in range(0, 256, 8):
                     part, zl, y, b = row // 128, row // 64 % 2, row // 16 % 4, row // 8 % 2
                     out[i, b, a, y, zl, part, r] = both[row : row + 8, 128 * a : 128 * (a + 1)]
 
-
-def front(noise, eigen, turn):
-    base = jnp.asarray(column_table())
+    prepare(0)
+    for i in range(STEPS):
+        if i + 1 < STEPS:
+            prepare(i + 1)
+        multiply(i)
+
+
+def front(noise, eigen):
+    operands = (noise, eigen, jnp.asarray(column_tables()))
     return pl.pallas_call(
         front_kernel,
-        in_specs=[pl.BlockSpec(memory_space=pltpu.HBM)] * 3 + [IN_VMEM],
+        in_specs=[pl.BlockSpec(memory_space=pltpu.HBM)] * 3,
         out_specs=IN_VMEM,
         out_shape=jax.ShapeDtypeStruct((4, 2, 2, 4, 2, 2, 4, 8, 128), F32),
         scratch_shapes=[
             pltpu.VMEM((2, LOCAL, WIDTH), jnp.int32),
             pltpu.VMEM((LOCAL, WIDTH), F32),
-            pltpu.VMEM((2, 4, 128, 128), F32),
-            pltpu.VMEM((2, 384, WIDTH), F32),
-            pltpu.VMEM((4, 256, 768), BF16),
-            pltpu.VMEM((STEPS, 4, 768, BLOCK), BF16),
-            pltpu.SemaphoreType.DMA((13,)),
+            pltpu.VMEM((2, 256, WIDTH), F32),
+            pltpu.VMEM((4, 256, 512), BF16),
+            pltpu.VMEM((STEPS, 4, 512, BLOCK), BF16),
+            pltpu.SemaphoreType.DMA((25,)),
         ],
         compiler_params=pltpu.CompilerParams(vmem_limit_bytes=32 * 2**20),
         cost_estimate=pl.CostEstimate(flops=2 * 10**9, bytes_accessed=12 * 2**20, transcendentals=0),
-    )(*(pltpu.with_memory_space_constraint(value, pltpu.HBM) for value in (noise, eigen, base)), turn)
+    )(*(pltpu.with_memory_space_constraint(value, pltpu.HBM) for value in operands))
 
 
 def middle_kernel(data, out):
@@ -286,13 +291,8 @@
 
 
 def on_device(noise, eigen):
-    x, zh, core = (lax.axis_index(name) for name in AXES[:3])
-    anchor = 8 * core + 4 * zh + 2 * (x % 2) + x // 2
-    row = 4 * jnp.arange(128, dtype=jnp.int32)[None, :] + jnp.arange(4, dtype=jnp.int32)[:, None]
-    angle = (anchor * row).astype(F32) * (2.0 * math.pi / N)
-    turn = jnp.broadcast_to(jnp.stack([jnp.cos(angle), jnp.sin(angle)])[..., None], (2, 4, 128, 128))
     with jax.named_scope("columns"):
-        data = front(noise, eigen, turn)
+        data = front(noise, eigen)
     with jax.named_scope("first_exchange"):
         data = lax.all_to_all(data.reshape(64, 2, 2, 32, 128), ("x", "core", "zh", "y"), 0, 0, tiled=True)
     with jax.named_scope("middle"):

time: 134 us -> 134 us (level)
  no operation moved by 1% of the time
where the time goes in v7:
time: 134 us; the launch traced here: 133 us
  blocking collectives  120 us (90%)
  Pallas kernels  13.7 us (10%)
    all_to_all x1, blocking collectives, on_device(): lax.all_to_all(data.reshape(64, 2, 2, 32, 128), ('x', 'core', 'zh', 'y'),...  62.3 us
    all_to_all x1, blocking collectives, on_device(): lax.all_to_all(data.reshape(32, 256, 128), ('zh', 'x', 'zl', 'core'), 0,...  57.3 us
    pallas_call x1, Pallas kernels, front(): pl.pallas_call(front_kernel, in_specs=[pl.BlockSpec(memory_space=pltpu.HB...  6.57 us
    pallas_call x1, Pallas kernels, row_transform(): pl.pallas_call(row_kernel, grid=(4,), in_specs=[IN_VMEM] * 4, out_specs=p...  5.81 us

profile of v7, /device:TPU:0, one launch (start us, length us, event | category | flops | bytes accessed | tf_op | source)
XLA Modules:
  0.0 133.4 jit_solution(12883458369961437949)
XLA Ops:
  0.0 6.6 %columns.1 = f32[4,2,2,4,2,2,4,8,128]{8,7,6,5,4,3,2,1,0:T(8,128)S(1)} custom-call(s32[2,512,1024]{2,1,0:T(8,128)} %noise.1, f32[512,1024]{1,0:T(8,128)} %eigen.1, bf16[16,4,256,512]{3,2,1,0:T(8,128)(2,1)} %constant.8.clone.all_tables), custom_call_target="tpu_custom_call" | custom-call | flops 2000000000 | bytes 12582912 | tf_op jit(solution)/shard_map/columns/pallas_call | solution.py:204
  6.6 62.3 %all_to_all.10 = f32[64,2,2,32,128]{4,3,2,1,0:T(8,128)S(1)} all-to-all(f32[64,2,2,32,128]{4,3,2,1,0:T(8,128)S(1)} %bitcast.11), channel_id=1, replica_groups=mesh['x'=4,'zh'=2,'core'=2,'zl'=2,'y'=4] {'x','core','zh','y'}, dimensions={0} | all-to-all | bytes 8388608 | tf_op jit(solution)/shard_map/first_exchange/all_to_all | solution.py:297
  68.9 1.3 middle.1
  70.2 0.0 copy-start
  70.2 0.0 copy-start.1
  70.2 0.0 copy-start.2
  70.2 57.3 %all_to_all.11 = f32[32,256,128]{2,1,0:T(8,128)S(1)} all-to-all(f32[32,256,128]{2,1,0:T(8,128)S(1)} %bitcast.10), channel_id=1, replica_groups=mesh['x'=4,'zh'=2,'core'=2,'zl'=2,'y'=4] {'zh','x','zl','core'}, dimensions={0} | all-to-all | bytes 8388608 | tf_op jit(solution)/shard_map/second_exchange/all_to_all | solution.py:301
  127.6 0.0 copy-done
  127.6 0.0 copy-done.1
  127.6 0.0 copy-done.2
  127.6 5.8 %rows.1 = f32[2,4096,128]{2,1,0:T(8,128)} custom-call(f32[8,2,2,4,8,8,128]{6,5,4,3,2,1,0:T(8,128)S(1)} %bitcast.12, bf16[256,256]{1,0:T(8,128)(2,1)S(1)} %copy-done.2, f32[2,128,128]{2,1,0:T(8,128)S(1)} %copy-done.1, bf16[256,256]{1,0:T(8,128)(2,1)S(1)} %copy-done), custom_call_target="tpu_custom_call" | custom-call | flops 3000000000 | bytes 9437184 | tf_op jit(solution)/shard_map/rows/pallas_call | solution.py:281
Async XLA Ops:
  70.2 57.4 %copy-start = (bf16[256,256]{1,0:T(8,128)(2,1)S(1)}, bf16[256,256]{1,0:T(8,128)(2,1)}, u32[]{:S(2)}) copy-start(bf16[256,256]{1,0:T(8,128)(2,1)} %constant.11.clone.last) | copy-start | bytes 393220
  70.2 57.4 %copy-start.1 = (f32[2,128,128]{2,1,0:T(8,128)S(1)}, f32[2,128,128]{2,1,0:T(8,128)}, u32[]{:S(2)}) copy-start(f32[2,128,128]{2,1,0:T(8,128)} %constant.10.clone.twist) | copy-start | bytes 393220
  70.2 57.4 %copy-start.2 = (bf16[256,256]{1,0:T(8,128)(2,1)S(1)}, bf16[256,256]{1,0:T(8,128)(2,1)}, u32[]{:S(2)}) copy-start(bf16[256,256]{1,0:T(8,128)(2,1)} %constant.9.clone.first) | copy-start | bytes 393220

commit v8 on v7

--- a/solution.py
+++ b/solution.py
@@ -249,21 +249,17 @@
     )(data)
 
 
-GROUP = 16
-
-
-def row_kernel(data, first, twist, last, out):
-    step = pl.program_id(0)
-
-    def piece(t):
-        return data[:, :, step // 2, t % 4, 4 * (step % 2) + t // 4].reshape(128, 128)
-
-    for group in range(0, 16, GROUP):
-        high, low = split(jnp.concatenate([piece(t) for t in range(group, group + GROUP)], 1))
+def row_kernel(data, first, twist, last, out, done, sent):
+    moves = []
+    for step in range(4):
+        pieces = []
+        for t in range(16):
+            pieces.append(data[:, :, step // 2, t % 4, 4 * (step % 2) + t // 4].reshape(128, 128))
+        high, low = split(jnp.concatenate(pieces, 1))
         sums = dot(first[...], jnp.concatenate([high, low], 0))
         sums = sums[:128] + sums[128:]
-        for t in range(group, group + GROUP):
-            at = slice(128 * (t - group), 128 * (t - group + 1))
+        for t in range(16):
+            at = slice(128 * t, 128 * (t + 1))
             re, im = sums[:64, at], sums[64:, at]
             both = []
             for v in range(2):
@@ -273,18 +269,31 @@
             whole = dot(high, last[...])
             whole = (whole[:, :128] + whole[:, 128:] + dot(low, last[:, :128])).T
             for part in range(2):
-                out[part, pl.ds(512 * (t // 8) + t % 8, 64, stride=8), :] = whole[64 * part : 64 * (part + 1)]
+                rows = pl.ds(512 * (t // 8) + t % 8, 64, stride=8)
+                done[step, part, rows, :] = whole[64 * part : 64 * (part + 1)]
+            if t % 8 == 7:
+                tile = t // 8
+                for part in range(2):
+                    move = pltpu.make_async_copy(
+                        done.at[step, part, pl.ds(512 * tile, 512)],
+                        out.at[part, pl.ds(1024 * step + 512 * tile, 512)],
+                        sent.at[4 * step + 2 * tile + part],
+                    )
+                    move.start()
+                    moves.append(move)
+    for move in moves:
+        move.wait()
 
 
 def row_transform(data):
     tables = [jnp.asarray(table) for table in row_tables()]
     result = pl.pallas_call(
         row_kernel,
-        grid=(4,),
         in_specs=[IN_VMEM] * 4,
-        out_specs=pl.BlockSpec((2, 1024, 128), lambda i: (0, i, 0)),
+        out_specs=pl.BlockSpec(memory_space=pltpu.HBM),
         out_shape=jax.ShapeDtypeStruct((2, 4096, 128), F32),
-        compiler_params=pltpu.CompilerParams(vmem_limit_bytes=16 * 2**20),
+        scratch_shapes=[pltpu.VMEM((4, 2, 1024, 128), F32), pltpu.SemaphoreType.DMA((16,))],
+        compiler_params=pltpu.CompilerParams(vmem_limit_bytes=20 * 2**20),
         cost_estimate=pl.CostEstimate(flops=3 * 10**9, bytes_accessed=9 * 2**20, transcendentals=0),
     )(data.reshape(8, 2, 2, 4, 8, 8, 128), *tables)
     return result.reshape(2, 8, 64, 8, 128).transpose(0, 1, 3, 2, 4).reshape(2, 64, M)

time: 134 us -> 134 us (level)
  no operation moved by 1% of the time
where the time goes in v8:
time: 134 us; the launch traced here: 133 us
  blocking collectives  120 us (90%)
  Pallas kernels  13.7 us (10%)
    all_to_all x1, blocking collectives, on_device(): lax.all_to_all(data.reshape(64, 2, 2, 32, 128), ('x', 'core', 'zh', 'y'),...  62.3 us
    all_to_all x1, blocking collectives, on_device(): lax.all_to_all(data.reshape(32, 256, 128), ('zh', 'x', 'zl', 'core'), 0,...  57.3 us
    pallas_call x1, Pallas kernels, front(): pl.pallas_call(front_kernel, in_specs=[pl.BlockSpec(memory_space=pltpu.HB...  6.57 us
    pallas_call x1, Pallas kernels, row_transform(): pl.pallas_call(row_kernel, in_specs=[IN_VMEM] * 4, out_specs=pl.BlockSpec...  5.78 us

profile of v8, /device:TPU:0, one launch (start us, length us, event | category | flops | bytes accessed | tf_op | source)
XLA Modules:
  0.0 133.4 jit_solution(9459416548281134648)
XLA Ops:
  0.0 6.6 %columns.1 = f32[4,2,2,4,2,2,4,8,128]{8,7,6,5,4,3,2,1,0:T(8,128)S(1)} custom-call(s32[2,512,1024]{2,1,0:T(8,128)} %noise.1, f32[512,1024]{1,0:T(8,128)} %eigen.1, bf16[16,4,256,512]{3,2,1,0:T(8,128)(2,1)} %constant.8.clone.all_tables), custom_call_target="tpu_custom_call" | custom-call | flops 2000000000 | bytes 12582912 | tf_op jit(solution)/shard_map/columns/pallas_call | solution.py:204
  6.6 62.3 %all_to_all.10 = f32[64,2,2,32,128]{4,3,2,1,0:T(8,128)S(1)} all-to-all(f32[64,2,2,32,128]{4,3,2,1,0:T(8,128)S(1)} %bitcast.11), channel_id=1, replica_groups=mesh['x'=4,'zh'=2,'core'=2,'zl'=2,'y'=4] {'x','core','zh','y'}, dimensions={0} | all-to-all | bytes 8388608 | tf_op jit(solution)/shard_map/first_exchange/all_to_all | solution.py:306
  68.9 1.3 middle.1
  70.2 0.0 copy-start
  70.2 0.0 copy-start.1
  70.2 0.0 copy-start.2
  70.2 57.3 %all_to_all.11 = f32[32,256,128]{2,1,0:T(8,128)S(1)} all-to-all(f32[32,256,128]{2,1,0:T(8,128)S(1)} %bitcast.10), channel_id=1, replica_groups=mesh['x'=4,'zh'=2,'core'=2,'zl'=2,'y'=4] {'zh','x','zl','core'}, dimensions={0} | all-to-all | bytes 8388608 | tf_op jit(solution)/shard_map/second_exchange/all_to_all | solution.py:310
  127.6 0.0 copy-done
  127.6 0.0 copy-done.1
  127.6 0.0 copy-done.2
  127.6 5.8 %rows.1 = f32[2,4096,128]{2,1,0:T(8,128)} custom-call(f32[8,2,2,4,8,8,128]{6,5,4,3,2,1,0:T(8,128)S(1)} %bitcast.12, bf16[256,256]{1,0:T(8,128)(2,1)S(1)} %copy-done.2, f32[2,128,128]{2,1,0:T(8,128)S(1)} %copy-done.1, bf16[256,256]{1,0:T(8,128)(2,1)S(1)} %copy-done), custom_call_target="tpu_custom_call" | custom-call | flops 3000000000 | bytes 9437184 | tf_op jit(solution)/shard_map/rows/pallas_call | solution.py:290
Async XLA Ops:
  70.2 57.4 %copy-start = (bf16[256,256]{1,0:T(8,128)(2,1)S(1)}, bf16[256,256]{1,0:T(8,128)(2,1)}, u32[]{:S(2)}) copy-start(bf16[256,256]{1,0:T(8,128)(2,1)} %constant.11.clone.last) | copy-start | bytes 393220
  70.2 57.4 %copy-start.1 = (f32[2,128,128]{2,1,0:T(8,128)S(1)}, f32[2,128,128]{2,1,0:T(8,128)}, u32[]{:S(2)}) copy-start(f32[2,128,128]{2,1,0:T(8,128)} %constant.10.clone.twist) | copy-start | bytes 393220
  70.2 57.4 %copy-start.2 = (bf16[256,256]{1,0:T(8,128)(2,1)S(1)}, bf16[256,256]{1,0:T(8,128)(2,1)}, u32[]{:S(2)}) copy-start(bf16[256,256]{1,0:T(8,128)(2,1)} %constant.9.clone.first) | copy-start | bytes 393220

commit v9 on v8

--- a/solution.py
+++ b/solution.py
@@ -16,6 +16,8 @@
 WIDTH = 1024
 BLOCK = 256
 STEPS = WIDTH // BLOCK
+PIECES = (32, 32, 64, 64, 64, 64, 64, 64, 64)
+EARLY = 448
 
 AXES = ("x", "zh", "core", "zl", "y")
 SIZES = (4, 2, 2, 2, 4)
@@ -143,40 +145,44 @@
 
 
 def front_kernel(noise, eigen, all_tables, out, bits, eig, drawn, tables, values, arrived):
-    moves = []
-    for g in range(8):
-        rows = slice(64 * g, 64 * (g + 1))
+    moves, first = [], 0
+    for g, count in enumerate(PIECES):
+        rows = slice(first, first + count)
         for part in range(2):
             moves.append(pltpu.make_async_copy(noise.at[part, rows], bits.at[part, rows], arrived.at[3 * g + part]))
         moves.append(pltpu.make_async_copy(eigen.at[rows], eig.at[rows], arrived.at[3 * g + 2]))
+        first += count
     x, zh, core = (lax.axis_index(name) for name in AXES[:3])
     digit = 8 * core + 4 * zh + 2 * (x % 2) + x // 2
-    moves.append(pltpu.make_async_copy(all_tables.at[digit], tables, arrived.at[24]))
+    moves.append(pltpu.make_async_copy(all_tables.at[digit], tables, arrived.at[3 * len(PIECES)]))
     for move in moves:
         move.start()
 
-    for g in range(4):
+    first = 0
+    for g, count in enumerate(PIECES):
         for move in moves[3 * g : 3 * g + 3]:
             move.wait()
-
-        def draws(i, carry):
-            rows = pl.ds(pl.multiple_of(64 * g + 32 * i, 32), 32)
-            drawn[0, rows, :], drawn[1, rows, :] = draw(bits[0, rows, :], bits[1, rows, :], eig[rows, :])
-            return carry
-
-        lax.fori_loop(0, 2, draws, 0)
-
-    for move in moves[12:]:
-        move.wait()
+        if first < EARLY:
+
+            def draws(i, carry, first=first):
+                rows = pl.ds(pl.multiple_of(first + 32 * i, 32), 32)
+                drawn[0, rows, :], drawn[1, rows, :] = draw(bits[0, rows, :], bits[1, rows, :], eig[rows, :])
+                return carry
+
+            lax.fori_loop(0, count // 32, draws, 0)
+        first += count
+    moves[-1].wait()
 
     def prepare(i):
         columns = slice(BLOCK * i, BLOCK * (i + 1))
-        parts = [
-            (drawn[0, 128 * j : 128 * (j + 1), columns], drawn[1, 128 * j : 128 * (j + 1), columns]) for j in range(2)
-        ]
-        for j in range(2, 4):
-            at = slice(128 * j, 128 * (j + 1))
-            parts.append(draw(bits[0, at, columns], bits[1, at, columns], eig[at, columns]))
+        parts = []
+        for j in range(4):
+            known = min(max(EARLY - 128 * j, 0), 128)
+            old, new = slice(128 * j, 128 * j + known), slice(128 * j + known, 128 * (j + 1))
+            part = [(drawn[0, old, columns], drawn[1, old, columns])] if known else []
+            if known < 128:
+                part.append(draw(bits[0, new, columns], bits[1, new, columns], eig[new, columns]))
+            parts.append(part[0] if len(part) == 1 else tuple(jnp.concatenate(both, 0) for both in zip(*part)))
         for r, value in enumerate(dft_4(*parts)):
             for part in range(2):
                 high, low = split(value[part])
@@ -209,10 +215,10 @@
         scratch_shapes=[
             pltpu.VMEM((2, LOCAL, WIDTH), jnp.int32),
             pltpu.VMEM((LOCAL, WIDTH), F32),
-            pltpu.VMEM((2, 256, WIDTH), F32),
+            pltpu.VMEM((2, EARLY, WIDTH), F32),
             pltpu.VMEM((4, 256, 512), BF16),
             pltpu.VMEM((STEPS, 4, 512, BLOCK), BF16),
-            pltpu.SemaphoreType.DMA((25,)),
+            pltpu.SemaphoreType.DMA((3 * len(PIECES) + 1,)),
         ],
         compiler_params=pltpu.CompilerParams(vmem_limit_bytes=32 * 2**20),
         cost_estimate=pl.CostEstimate(flops=2 * 10**9, bytes_accessed=12 * 2**20, transcendentals=0),

time: 134 us -> 134 us (level)
  no operation moved by 1% of the time
where the time goes in v9:
time: 134 us; the launch traced here: 133 us
  blocking collectives  120 us (90%)
  Pallas kernels  13.2 us (10%)
    all_to_all x1, blocking collectives, on_device(): lax.all_to_all(data.reshape(64, 2, 2, 32, 128), ('x', 'core', 'zh', 'y'),...  62.3 us
    all_to_all x1, blocking collectives, on_device(): lax.all_to_all(data.reshape(32, 256, 128), ('zh', 'x', 'zl', 'core'), 0,...  57.3 us
    pallas_call x1, Pallas kernels, front(): pl.pallas_call(front_kernel, in_specs=[pl.BlockSpec(memory_space=pltpu.HB...  6.1 us
    pallas_call x1, Pallas kernels, row_transform(): pl.pallas_call(row_kernel, in_specs=[IN_VMEM] * 4, out_specs=pl.BlockSpec...  5.77 us

profile of v9, /device:TPU:0, one launch (start us, length us, event | category | flops | bytes accessed | tf_op | source)
XLA Modules:
  0.0 132.9 jit_solution(6985065161129843422)
XLA Ops:
  0.0 6.1 %columns.1 = f32[4,2,2,4,2,2,4,8,128]{8,7,6,5,4,3,2,1,0:T(8,128)S(1)} custom-call(s32[2,512,1024]{2,1,0:T(8,128)} %noise.1, f32[512,1024]{1,0:T(8,128)} %eigen.1, bf16[16,4,256,512]{3,2,1,0:T(8,128)(2,1)} %constant.8.clone.all_tables), custom_call_target="tpu_custom_call" | custom-call | flops 2000000000 | bytes 12582912 | tf_op jit(solution)/shard_map/columns/pallas_call | solution.py:210
  6.1 62.3 %all_to_all.10 = f32[64,2,2,32,128]{4,3,2,1,0:T(8,128)S(1)} all-to-all(f32[64,2,2,32,128]{4,3,2,1,0:T(8,128)S(1)} %bitcast.11), channel_id=1, replica_groups=mesh['x'=4,'zh'=2,'core'=2,'zl'=2,'y'=4] {'x','core','zh','y'}, dimensions={0} | all-to-all | bytes 8388608 | tf_op jit(solution)/shard_map/first_exchange/all_to_all | solution.py:312
  68.4 1.3 middle.1
  69.7 0.0 copy-start
  69.7 0.0 copy-start.1
  69.8 0.0 copy-start.2
  69.8 57.3 %all_to_all.11 = f32[32,256,128]{2,1,0:T(8,128)S(1)} all-to-all(f32[32,256,128]{2,1,0:T(8,128)S(1)} %bitcast.10), channel_id=1, replica_groups=mesh['x'=4,'zh'=2,'core'=2,'zl'=2,'y'=4] {'zh','x','zl','core'}, dimensions={0} | all-to-all | bytes 8388608 | tf_op jit(solution)/shard_map/second_exchange/all_to_all | solution.py:316
  127.1 0.0 copy-done
  127.1 0.0 copy-done.1
  127.1 0.0 copy-done.2
  127.1 5.8 %rows.1 = f32[2,4096,128]{2,1,0:T(8,128)} custom-call(f32[8,2,2,4,8,8,128]{6,5,4,3,2,1,0:T(8,128)S(1)} %bitcast.12, bf16[256,256]{1,0:T(8,128)(2,1)S(1)} %copy-done.2, f32[2,128,128]{2,1,0:T(8,128)S(1)} %copy-done.1, bf16[256,256]{1,0:T(8,128)(2,1)S(1)} %copy-done), custom_call_target="tpu_custom_call" | custom-call | flops 3000000000 | bytes 9437184 | tf_op jit(solution)/shard_map/rows/pallas_call | solution.py:296
Async XLA Ops:
  69.7 57.4 %copy-start = (bf16[256,256]{1,0:T(8,128)(2,1)S(1)}, bf16[256,256]{1,0:T(8,128)(2,1)}, u32[]{:S(2)}) copy-start(bf16[256,256]{1,0:T(8,128)(2,1)} %constant.11.clone.last) | copy-start | bytes 393220
  69.7 57.4 %copy-start.1 = (f32[2,128,128]{2,1,0:T(8,128)S(1)}, f32[2,128,128]{2,1,0:T(8,128)}, u32[]{:S(2)}) copy-start(f32[2,128,128]{2,1,0:T(8,128)} %constant.10.clone.twist) | copy-start | bytes 393220
  69.8 57.4 %copy-start.2 = (bf16[256,256]{1,0:T(8,128)(2,1)S(1)}, bf16[256,256]{1,0:T(8,128)(2,1)}, u32[]{:S(2)}) copy-start(bf16[256,256]{1,0:T(8,128)(2,1)} %constant.9.clone.first) | copy-start | bytes 393220

commit v10 on v9

--- a/solution.py
+++ b/solution.py
@@ -55,12 +55,16 @@
     imag_part = np.stack([-sine, cosine], -1).reshape(64, 128)
     high, low = halves(np.concatenate([real_part, imag_part], 0))
     first = np.concatenate([np.concatenate([high, high], 1), np.concatenate([low, np.zeros_like(low)], 1)], 0)
-    angle = 2.0 * np.pi * (np.outer(np.arange(128), np.arange(128)) % M) / M
+    angle = 2.0 * np.pi * np.outer(np.arange(64), np.arange(128)) / M
     twist = np.stack([np.cos(angle), -np.sin(angle)]).astype(np.float32)
-    angle = 2.0 * np.pi * (np.outer(np.arange(128), np.arange(64)) % 64) / 64
-    cosine, sine = np.cos(angle), np.sin(angle)
-    last = np.concatenate([np.concatenate([cosine, -sine], 1), np.concatenate([sine, cosine], 1)], 0)
-    return first, twist, np.concatenate(halves(last), 1)
+    last = []
+    for order in ([0, 1], [1, 0]):
+        k = 2 * np.arange(64)[None, :] + np.array(order)[:, None]
+        angle = 2.0 * np.pi * (np.outer(np.arange(128), k.reshape(128)) % 128) / 128
+        cosine, sine = np.cos(angle), np.sin(angle)
+        table = np.concatenate([np.concatenate([cosine, -sine], 1), np.concatenate([sine, cosine], 1)], 0)
+        last.append(np.stack(halves(table)))
+    return first, twist, np.stack(last)
 
 
 def sine_polynomials():
@@ -255,40 +259,56 @@
     )(data)
 
 
+ROWS = 32
+TOGETHER = 8
+
+
 def row_kernel(data, first, twist, last, out, done, sent):
-    moves = []
-    for step in range(4):
+    def move(step, tile, part):
+        row = pl.multiple_of(64 * ROWS * step + 512 * tile, 512)
+        return pltpu.make_async_copy(
+            done.at[part, pl.ds(row, 512)], out.at[part, pl.ds(row, 512)], sent.at[ROWS // 4 * step + 2 * tile + part]
+        )
+
+    left = lax.broadcasted_iota(jnp.int32, (64, 128), 1) < 64
+
+    def run(step, carry):
         pieces = []
-        for t in range(16):
-            pieces.append(data[:, :, step // 2, t % 4, 4 * (step % 2) + t // 4].reshape(128, 128))
+        for t in range(ROWS):
+            pieces.append(data[:, :, ROWS * step // 32, t % 4, ROWS * step % 32 // 4 + t // 4].reshape(128, 128))
         high, low = split(jnp.concatenate(pieces, 1))
         sums = dot(first[...], jnp.concatenate([high, low], 0))
         sums = sums[:128] + sums[128:]
-        for t in range(16):
-            at = slice(128 * t, 128 * (t + 1))
-            re, im = sums[:64, at], sums[64:, at]
-            both = []
-            for v in range(2):
-                c, s = twist[0, 64 * v : 64 * (v + 1), :], twist[1, 64 * v : 64 * (v + 1), :]
-                both.append(jnp.concatenate([re * c - im * s, re * s + im * c], 1))
-            high, low = split(jnp.concatenate(both, 0))
-            whole = dot(high, last[...])
-            whole = (whole[:, :128] + whole[:, 128:] + dot(low, last[:, :128])).T
+        for group in range(0, ROWS, TOGETHER):
+            sides = []
+            for side in range(2):
+                turned = []
+                for t in range(group + side, group + TOGETHER, 2):
+                    at = slice(128 * t, 128 * (t + 1))
+                    re, im = sums[:64, at], sums[64:, at]
+                    turned.append(jnp.concatenate([re * twist[0] - im * twist[1], re * twist[1] + im * twist[0]], 1))
+                high, low = split(jnp.concatenate(turned, 0))
+                table = last[side, 0]
+                sides.append(dot(high, table) + dot(low, table) + dot(high, last[side, 1]))
+            for t in range(group, group + TOGETHER, 2):
+                at = slice(32 * (t - group), 32 * (t - group) + 64)
+                for part in range(2):
+                    lanes = slice(128 * part, 128 * (part + 1))
+                    even, odd = sides[0][at, lanes], sides[1][at, lanes]
+                    whole = jnp.concatenate([jnp.where(left, even, odd), jnp.where(left, odd, even)], 0).T
+                    row = pl.multiple_of(64 * ROWS * step, 64 * ROWS) + 512 * (t // 8) + t % 8
+                    done[part, pl.ds(row, 64, stride=8), :] = jnp.where(left, whole[:64], whole[64:])
+                    done[part, pl.ds(row + 1, 64, stride=8), :] = jnp.where(left, whole[64:], whole[:64])
+                if t % 8 == 6:
+                    for part in range(2):
+                        move(step, t // 8, part).start()
+        return carry
+
+    lax.fori_loop(0, 64 // ROWS, run, 0)
+    for step in range(64 // ROWS):
+        for tile in range(ROWS // 8):
             for part in range(2):
-                rows = pl.ds(512 * (t // 8) + t % 8, 64, stride=8)
-                done[step, part, rows, :] = whole[64 * part : 64 * (part + 1)]
-            if t % 8 == 7:
-                tile = t // 8
-                for part in range(2):
-                    move = pltpu.make_async_copy(
-                        done.at[step, part, pl.ds(512 * tile, 512)],
-                        out.at[part, pl.ds(1024 * step + 512 * tile, 512)],
-                        sent.at[4 * step + 2 * tile + part],
-                    )
-                    move.start()
-                    moves.append(move)
-    for move in moves:
-        move.wait()
+                move(step, tile, part).wait()
 
 
 def row_transform(data):
@@ -298,7 +318,7 @@
         in_specs=[IN_VMEM] * 4,
         out_specs=pl.BlockSpec(memory_space=pltpu.HBM),
         out_shape=jax.ShapeDtypeStruct((2, 4096, 128), F32),
-        scratch_shapes=[pltpu.VMEM((4, 2, 1024, 128), F32), pltpu.SemaphoreType.DMA((16,))],
+        scratch_shapes=[pltpu.VMEM((2, 4096, 128), F32), pltpu.SemaphoreType.DMA((16,))],
         compiler_params=pltpu.CompilerParams(vmem_limit_bytes=20 * 2**20),
         cost_estimate=pl.CostEstimate(flops=3 * 10**9, bytes_accessed=9 * 2**20, transcendentals=0),
     )(data.reshape(8, 2, 2, 4, 8, 8, 128), *tables)

time: 134 us -> 133 us (level)
  no operation moved by 1% of the time
where the time goes in v10:
time: 133 us; the launch traced here: 132 us
  blocking collectives  120 us (90%)
  Pallas kernels  12.3 us (9%)
    all_to_all x1, blocking collectives, on_device(): lax.all_to_all(data.reshape(64, 2, 2, 32, 128), ('x', 'core', 'zh', 'y'),...  62.3 us
    all_to_all x1, blocking collectives, on_device(): lax.all_to_all(data.reshape(32, 256, 128), ('zh', 'x', 'zl', 'core'), 0,...  57.3 us
    pallas_call x1, Pallas kernels, front(): pl.pallas_call(front_kernel, in_specs=[pl.BlockSpec(memory_space=pltpu.HB...  6.1 us
    pallas_call x1, Pallas kernels, row_transform(): pl.pallas_call(row_kernel, in_specs=[IN_VMEM] * 4, out_specs=pl.BlockSpec...  4.84 us

profile of v10, /device:TPU:0, one launch (start us, length us, event | category | flops | bytes accessed | tf_op | source)
XLA Modules:
  0.0 131.9 jit_solution(4970783230708734129)
XLA Ops:
  0.0 6.1 %columns.1 = f32[4,2,2,4,2,2,4,8,128]{8,7,6,5,4,3,2,1,0:T(8,128)S(1)} custom-call(s32[2,512,1024]{2,1,0:T(8,128)} %noise.1, f32[512,1024]{1,0:T(8,128)} %eigen.1, bf16[16,4,256,512]{3,2,1,0:T(8,128)(2,1)} %constant.8.clone.all_tables), custom_call_target="tpu_custom_call" | custom-call | flops 2000000000 | bytes 12582912 | tf_op jit(solution)/shard_map/columns/pallas_call | solution.py:214
  6.1 62.3 %all_to_all.10 = f32[64,2,2,32,128]{4,3,2,1,0:T(8,128)S(1)} all-to-all(f32[64,2,2,32,128]{4,3,2,1,0:T(8,128)S(1)} %bitcast.11), channel_id=1, replica_groups=mesh['x'=4,'zh'=2,'core'=2,'zl'=2,'y'=4] {'x','core','zh','y'}, dimensions={0} | all-to-all | bytes 8388608 | tf_op jit(solution)/shard_map/first_exchange/all_to_all | solution.py:332
  68.4 1.3 middle.1
  69.7 0.0 copy-start
  69.7 0.0 copy-start.1
  69.8 0.0 copy-start.2
  69.8 57.3 %all_to_all.11 = f32[32,256,128]{2,1,0:T(8,128)S(1)} all-to-all(f32[32,256,128]{2,1,0:T(8,128)S(1)} %bitcast.10), channel_id=1, replica_groups=mesh['x'=4,'zh'=2,'core'=2,'zl'=2,'y'=4] {'zh','x','zl','core'}, dimensions={0} | all-to-all | bytes 8388608 | tf_op jit(solution)/shard_map/second_exchange/all_to_all | solution.py:336
  127.1 0.0 copy-done
  127.1 0.0 copy-done.1
  127.1 0.0 copy-done.2
  127.1 4.8 %rows.1 = f32[2,4096,128]{2,1,0:T(8,128)} custom-call(f32[8,2,2,4,8,8,128]{6,5,4,3,2,1,0:T(8,128)S(1)} %bitcast.12, bf16[256,256]{1,0:T(8,128)(2,1)S(1)} %copy-done.1, f32[2,64,128]{2,1,0:T(8,128)S(1)} %copy-done.2, bf16[2,2,256,256]{3,2,1,0:T(8,128)(2,1)S(1)} %copy-done), custom_call_target="tpu_custom_call" | custom-call | flops 3000000000 | bytes 9437184 | tf_op jit(solution)/shard_map/rows/pallas_call | solution.py:316
Async XLA Ops:
  69.7 57.4 %copy-start = (bf16[2,2,256,256]{3,2,1,0:T(8,128)(2,1)S(1)}, bf16[2,2,256,256]{3,2,1,0:T(8,128)(2,1)}, u32[]{:S(2)}) copy-start(bf16[2,2,256,256]{3,2,1,0:T(8,128)(2,1)} %constant.11.clone.last) | copy-start | bytes 1572868
  69.7 57.4 %copy-start.1 = (bf16[256,256]{1,0:T(8,128)(2,1)S(1)}, bf16[256,256]{1,0:T(8,128)(2,1)}, u32[]{:S(2)}) copy-start(bf16[256,256]{1,0:T(8,128)(2,1)} %constant.9.clone.first) | copy-start | bytes 393220
  69.8 57.4 %copy-start.2 = (f32[2,64,128]{2,1,0:T(8,128)S(1)}, f32[2,64,128]{2,1,0:T(8,128)}, u32[]{:S(2)}) copy-start(f32[2,64,128]{2,1,0:T(8,128)} %constant.10.clone.twist) | copy-start | bytes 196612

commit v11 on v10

--- a/solution.py
+++ b/solution.py
@@ -195,8 +195,9 @@
 
     def multiply(i):
         for r in range(4):
-            table, value = tables[r, :, :256], values[i, r, :256, :]
-            both = dot(table, values[i, r, :256, :]) + dot(table, values[i, r, 256:, :]) + dot(tables[r, :, 256:], value)
+            table = jnp.concatenate([tables[r, :, :256], tables[r, :, 256:]], 0)
+            both = dot(table, values[i, r, :256, :])
+            both = both[:256] + both[256:] + dot(tables[r, :, :256], values[i, r, 256:, :])
             for a in range(BLOCK // 128):
                 for row in range(0, 256, 8):
                     part, zl, y, b = row // 128, row // 64 % 2, row // 16 % 4, row // 8 % 2

time: 133 us -> 133 us (level)
  no operation moved by 1% of the time
where the time goes in v11:
time: 133 us; the launch traced here: 132 us
  blocking collectives  120 us (90%)
  Pallas kernels  12.2 us (9%)
    all_to_all x1, blocking collectives, on_device(): lax.all_to_all(data.reshape(64, 2, 2, 32, 128), ('x', 'core', 'zh', 'y'),...  62.3 us
    all_to_all x1, blocking collectives, on_device(): lax.all_to_all(data.reshape(32, 256, 128), ('zh', 'x', 'zl', 'core'), 0,...  57.3 us
    pallas_call x1, Pallas kernels, front(): pl.pallas_call(front_kernel, in_specs=[pl.BlockSpec(memory_space=pltpu.HB...  6.04 us
    pallas_call x1, Pallas kernels, row_transform(): pl.pallas_call(row_kernel, in_specs=[IN_VMEM] * 4, out_specs=pl.BlockSpec...  4.86 us

profile of v11, /device:TPU:0, one launch (start us, length us, event | category | flops | bytes accessed | tf_op | source)
XLA Modules:
  0.0 131.9 jit_solution(17267203705736694023)
XLA Ops:
  0.0 6.0 %columns.1 = f32[4,2,2,4,2,2,4,8,128]{8,7,6,5,4,3,2,1,0:T(8,128)S(1)} custom-call(s32[2,512,1024]{2,1,0:T(8,128)} %noise.1, f32[512,1024]{1,0:T(8,128)} %eigen.1, bf16[16,4,256,512]{3,2,1,0:T(8,128)(2,1)} %constant.8.clone.all_tables), custom_call_target="tpu_custom_call" | custom-call | flops 2000000000 | bytes 12582912 | tf_op jit(solution)/shard_map/columns/pallas_call | solution.py:215
  6.0 62.3 %all_to_all.10 = f32[64,2,2,32,128]{4,3,2,1,0:T(8,128)S(1)} all-to-all(f32[64,2,2,32,128]{4,3,2,1,0:T(8,128)S(1)} %bitcast.11), channel_id=1, replica_groups=mesh['x'=4,'zh'=2,'core'=2,'zl'=2,'y'=4] {'x','core','zh','y'}, dimensions={0} | all-to-all | bytes 8388608 | tf_op jit(solution)/shard_map/first_exchange/all_to_all | solution.py:333
  68.3 1.3 middle.1
  69.7 0.0 copy-start
  69.7 0.0 copy-start.1
  69.7 0.0 copy-start.2
  69.7 57.3 %all_to_all.11 = f32[32,256,128]{2,1,0:T(8,128)S(1)} all-to-all(f32[32,256,128]{2,1,0:T(8,128)S(1)} %bitcast.10), channel_id=1, replica_groups=mesh['x'=4,'zh'=2,'core'=2,'zl'=2,'y'=4] {'zh','x','zl','core'}, dimensions={0} | all-to-all | bytes 8388608 | tf_op jit(solution)/shard_map/second_exchange/all_to_all | solution.py:337
  127.0 0.0 copy-done
  127.0 0.0 copy-done.1
  127.0 0.0 copy-done.2
  127.0 4.9 %rows.1 = f32[2,4096,128]{2,1,0:T(8,128)} custom-call(f32[8,2,2,4,8,8,128]{6,5,4,3,2,1,0:T(8,128)S(1)} %bitcast.12, bf16[256,256]{1,0:T(8,128)(2,1)S(1)} %copy-done.1, f32[2,64,128]{2,1,0:T(8,128)S(1)} %copy-done.2, bf16[2,2,256,256]{3,2,1,0:T(8,128)(2,1)S(1)} %copy-done), custom_call_target="tpu_custom_call" | custom-call | flops 3000000000 | bytes 9437184 | tf_op jit(solution)/shard_map/rows/pallas_call | solution.py:317
Async XLA Ops:
  69.7 57.4 %copy-start = (bf16[2,2,256,256]{3,2,1,0:T(8,128)(2,1)S(1)}, bf16[2,2,256,256]{3,2,1,0:T(8,128)(2,1)}, u32[]{:S(2)}) copy-start(bf16[2,2,256,256]{3,2,1,0:T(8,128)(2,1)} %constant.11.clone.last) | copy-start | bytes 1572868
  69.7 57.4 %copy-start.1 = (bf16[256,256]{1,0:T(8,128)(2,1)S(1)}, bf16[256,256]{1,0:T(8,128)(2,1)}, u32[]{:S(2)}) copy-start(bf16[256,256]{1,0:T(8,128)(2,1)} %constant.9.clone.first) | copy-start | bytes 393220
  69.7 57.4 %copy-start.2 = (f32[2,64,128]{2,1,0:T(8,128)S(1)}, f32[2,64,128]{2,1,0:T(8,128)}, u32[]{:S(2)}) copy-start(f32[2,64,128]{2,1,0:T(8,128)} %constant.10.clone.twist) | copy-start | bytes 196612

commit v12 on v11

--- a/solution.py
+++ b/solution.py
@@ -47,8 +47,8 @@
 
 
 def row_tables():
-    place = 8 * (4 * np.arange(2)[None, :, None] + np.arange(4)[None, None, :])
-    place = place + np.array([0, 2, 4, 6, 1, 3, 5, 7])[:, None, None]
+    zh, zl, x, y = np.ix_(np.arange(2), np.arange(2), np.arange(4), np.arange(4))
+    place = 8 * (4 * zl + y) + 2 * x + zh
     angle = 2.0 * np.pi * (np.arange(64)[:, None] * place.reshape(1, 64) % 64) / 64
     cosine, sine = np.cos(angle), np.sin(angle)
     real_part = np.stack([cosine, sine], -1).reshape(64, 128)
@@ -240,8 +240,8 @@
                 values.append((data[*index, 0, r], data[*index, 1, r]))
             for k, value in enumerate(dft_16(values)):
                 core, zh, xl, xh = k & 1, k >> 1 & 1, k >> 2 & 1, k >> 3
-                place = 4 * zh + 2 * xh + xl
-                row = pl.multiple_of(1024 * place + 512 * zl + 256 * core + 64 * r, 64)
+                place = 8 * zh + 4 * zl + 2 * xh + xl
+                row = pl.multiple_of(512 * place + 256 * core + 64 * r, 64)
                 for part in range(2):
                     out[pl.ds(row + 2 * y + part, 8, stride=8), :] = value[part]
         return carry
@@ -276,7 +276,7 @@
     def run(step, carry):
         pieces = []
         for t in range(ROWS):
-            pieces.append(data[:, :, ROWS * step // 32, t % 4, ROWS * step % 32 // 4 + t // 4].reshape(128, 128))
+            pieces.append(data[:, ROWS * step // 32, t % 4, ROWS * step % 32 // 4 + t // 4].reshape(128, 128))
         high, low = split(jnp.concatenate(pieces, 1))
         sums = dot(first[...], jnp.concatenate([high, low], 0))
         sums = sums[:128] + sums[128:]
@@ -322,7 +322,7 @@
         scratch_shapes=[pltpu.VMEM((2, 4096, 128), F32), pltpu.SemaphoreType.DMA((16,))],
         compiler_params=pltpu.CompilerParams(vmem_limit_bytes=20 * 2**20),
         cost_estimate=pl.CostEstimate(flops=3 * 10**9, bytes_accessed=9 * 2**20, transcendentals=0),
-    )(data.reshape(8, 2, 2, 4, 8, 8, 128), *tables)
+    )(data.reshape(16, 2, 4, 8, 8, 128), *tables)
     return result.reshape(2, 8, 64, 8, 128).transpose(0, 1, 3, 2, 4).reshape(2, 64, M)
 
 
@@ -334,7 +334,7 @@
     with jax.named_scope("middle"):
         data = middle(data.reshape(4, 2, 2, 4, 2, 2, 4, 8, 128))
     with jax.named_scope("second_exchange"):
-        data = lax.all_to_all(data.reshape(32, 256, 128), ("zh", "x", "zl", "core"), 0, 0, tiled=True)
+        data = lax.all_to_all(data.reshape(32, 256, 128), ("zh", "zl", "x", "core"), 0, 0, tiled=True)
     with jax.named_scope("rows"):
         return row_transform(data)
 

time: 133 us -> 132 us (level)
  blocking collectives: 120 us -> 118 us
where the time goes in v12:
time: 132 us; the launch traced here: 131 us
  blocking collectives  118 us (89%)
  Pallas kernels  12.2 us (9%)
    all_to_all x1, blocking collectives, on_device(): lax.all_to_all(data.reshape(64, 2, 2, 32, 128), ('x', 'core', 'zh', 'y'),...  62.3 us
    all_to_all x1, blocking collectives, on_device(): lax.all_to_all(data.reshape(32, 256, 128), ('zh', 'zl', 'x', 'core'), 0,...  56.2 us
    pallas_call x1, Pallas kernels, front(): pl.pallas_call(front_kernel, in_specs=[pl.BlockSpec(memory_space=pltpu.HB...  6.04 us
    pallas_call x1, Pallas kernels, row_transform(): pl.pallas_call(row_kernel, in_specs=[IN_VMEM] * 4, out_specs=pl.BlockSpec...  4.86 us

profile of v12, /device:TPU:0, one launch (start us, length us, event | category | flops | bytes accessed | tf_op | source)
XLA Modules:
  0.0 130.7 jit_solution(6265825828886729146)
XLA Ops:
  0.0 6.0 %columns.1 = f32[4,2,2,4,2,2,4,8,128]{8,7,6,5,4,3,2,1,0:T(8,128)S(1)} custom-call(s32[2,512,1024]{2,1,0:T(8,128)} %noise.1, f32[512,1024]{1,0:T(8,128)} %eigen.1, bf16[16,4,256,512]{3,2,1,0:T(8,128)(2,1)} %constant.8.clone.all_tables), custom_call_target="tpu_custom_call" | custom-call | flops 2000000000 | bytes 12582912 | tf_op jit(solution)/shard_map/columns/pallas_call | solution.py:215
  6.0 62.3 %all_to_all.10 = f32[64,2,2,32,128]{4,3,2,1,0:T(8,128)S(1)} all-to-all(f32[64,2,2,32,128]{4,3,2,1,0:T(8,128)S(1)} %bitcast.11), channel_id=1, replica_groups=mesh['x'=4,'zh'=2,'core'=2,'zl'=2,'y'=4] {'x','core','zh','y'}, dimensions={0} | all-to-all | bytes 8388608 | tf_op jit(solution)/shard_map/first_exchange/all_to_all | solution.py:333
  68.3 1.3 middle.1
  69.7 0.0 copy-start
  69.7 0.0 copy-start.1
  69.7 0.0 copy-start.2
  69.7 56.2 %all_to_all.11 = f32[32,256,128]{2,1,0:T(8,128)S(1)} all-to-all(f32[32,256,128]{2,1,0:T(8,128)S(1)} %bitcast.10), channel_id=1, replica_groups=mesh['x'=4,'zh'=2,'core'=2,'zl'=2,'y'=4] {'zh','zl','x','core'}, dimensions={0} | all-to-all | bytes 8388608 | tf_op jit(solution)/shard_map/second_exchange/all_to_all | solution.py:337
  125.9 0.0 copy-done
  125.9 0.0 copy-done.1
  125.9 0.0 copy-done.2
  125.9 4.9 %rows.1 = f32[2,4096,128]{2,1,0:T(8,128)} custom-call(f32[16,2,4,8,8,128]{5,4,3,2,1,0:T(8,128)S(1)} %bitcast.12, bf16[256,256]{1,0:T(8,128)(2,1)S(1)} %copy-done.1, f32[2,64,128]{2,1,0:T(8,128)S(1)} %copy-done.2, bf16[2,2,256,256]{3,2,1,0:T(8,128)(2,1)S(1)} %copy-done), custom_call_target="tpu_custom_call" | custom-call | flops 3000000000 | bytes 9437184 | tf_op jit(solution)/shard_map/rows/pallas_call | solution.py:317
Async XLA Ops:
  69.7 56.2 %copy-start = (bf16[2,2,256,256]{3,2,1,0:T(8,128)(2,1)S(1)}, bf16[2,2,256,256]{3,2,1,0:T(8,128)(2,1)}, u32[]{:S(2)}) copy-start(bf16[2,2,256,256]{3,2,1,0:T(8,128)(2,1)} %constant.11.clone.last) | copy-start | bytes 1572868
  69.7 56.2 %copy-start.1 = (bf16[256,256]{1,0:T(8,128)(2,1)S(1)}, bf16[256,256]{1,0:T(8,128)(2,1)}, u32[]{:S(2)}) copy-start(bf16[256,256]{1,0:T(8,128)(2,1)} %constant.9.clone.first) | copy-start | bytes 393220
  69.7 56.2 %copy-start.2 = (f32[2,64,128]{2,1,0:T(8,128)S(1)}, f32[2,64,128]{2,1,0:T(8,128)}, u32[]{:S(2)}) copy-start(f32[2,64,128]{2,1,0:T(8,128)} %constant.10.clone.twist) | copy-start | bytes 196612

commit v13 on v12

--- a/solution.py
+++ b/solution.py
@@ -175,7 +175,6 @@
 
             lax.fori_loop(0, count // 32, draws, 0)
         first += count
-    moves[-1].wait()
 
     def prepare(i):
         columns = slice(BLOCK * i, BLOCK * (i + 1))
@@ -204,6 +203,7 @@
                     out[i, b, a, y, zl, part, r] = both[row : row + 8, 128 * a : 128 * (a + 1)]
 
     prepare(0)
+    moves[-1].wait()
     for i in range(STEPS):
         if i + 1 < STEPS:
             prepare(i + 1)

time: 132 us -> 132 us (level)
  no operation moved by 1% of the time
where the time goes in v13:
time: 132 us; the launch traced here: 131 us
  blocking collectives  118 us (89%)
  Pallas kernels  12.4 us (9%)
    all_to_all x1, blocking collectives, on_device(): lax.all_to_all(data.reshape(64, 2, 2, 32, 128), ('x', 'core', 'zh', 'y'),...  62.3 us
    all_to_all x1, blocking collectives, on_device(): lax.all_to_all(data.reshape(32, 256, 128), ('zh', 'zl', 'x', 'core'), 0,...  56.2 us
    pallas_call x1, Pallas kernels, front(): pl.pallas_call(front_kernel, in_specs=[pl.BlockSpec(memory_space=pltpu.HB...  6.24 us
    pallas_call x1, Pallas kernels, row_transform(): pl.pallas_call(row_kernel, in_specs=[IN_VMEM] * 4, out_specs=pl.BlockSpec...  4.84 us

profile of v13, /device:TPU:0, one launch (start us, length us, event | category | flops | bytes accessed | tf_op | source)
XLA Modules:
  0.0 130.9 jit_solution(16318502778499169386)
XLA Ops:
  0.0 6.2 %columns.1 = f32[4,2,2,4,2,2,4,8,128]{8,7,6,5,4,3,2,1,0:T(8,128)S(1)} custom-call(s32[2,512,1024]{2,1,0:T(8,128)} %noise.1, f32[512,1024]{1,0:T(8,128)} %eigen.1, bf16[16,4,256,512]{3,2,1,0:T(8,128)(2,1)} %constant.8.clone.all_tables), custom_call_target="tpu_custom_call" | custom-call | flops 2000000000 | bytes 12582912 | tf_op jit(solution)/shard_map/columns/pallas_call | solution.py:215
  6.2 62.3 %all_to_all.10 = f32[64,2,2,32,128]{4,3,2,1,0:T(8,128)S(1)} all-to-all(f32[64,2,2,32,128]{4,3,2,1,0:T(8,128)S(1)} %bitcast.11), channel_id=1, replica_groups=mesh['x'=4,'zh'=2,'core'=2,'zl'=2,'y'=4] {'x','core','zh','y'}, dimensions={0} | all-to-all | bytes 8388608 | tf_op jit(solution)/shard_map/first_exchange/all_to_all | solution.py:333
  68.6 1.3 middle.1
  69.9 0.0 copy-start
  69.9 0.0 copy-start.1
  69.9 0.0 copy-start.2
  69.9 56.2 %all_to_all.11 = f32[32,256,128]{2,1,0:T(8,128)S(1)} all-to-all(f32[32,256,128]{2,1,0:T(8,128)S(1)} %bitcast.10), channel_id=1, replica_groups=mesh['x'=4,'zh'=2,'core'=2,'zl'=2,'y'=4] {'zh','zl','x','core'}, dimensions={0} | all-to-all | bytes 8388608 | tf_op jit(solution)/shard_map/second_exchange/all_to_all | solution.py:337
  126.1 0.0 copy-done
  126.1 0.0 copy-done.1
  126.1 0.0 copy-done.2
  126.1 4.8 %rows.1 = f32[2,4096,128]{2,1,0:T(8,128)} custom-call(f32[16,2,4,8,8,128]{5,4,3,2,1,0:T(8,128)S(1)} %bitcast.12, bf16[256,256]{1,0:T(8,128)(2,1)S(1)} %copy-done.1, f32[2,64,128]{2,1,0:T(8,128)S(1)} %copy-done.2, bf16[2,2,256,256]{3,2,1,0:T(8,128)(2,1)S(1)} %copy-done), custom_call_target="tpu_custom_call" | custom-call | flops 3000000000 | bytes 9437184 | tf_op jit(solution)/shard_map/rows/pallas_call | solution.py:317
Async XLA Ops:
  69.9 56.2 %copy-start = (bf16[2,2,256,256]{3,2,1,0:T(8,128)(2,1)S(1)}, bf16[2,2,256,256]{3,2,1,0:T(8,128)(2,1)}, u32[]{:S(2)}) copy-start(bf16[2,2,256,256]{3,2,1,0:T(8,128)(2,1)} %constant.11.clone.last) | copy-start | bytes 1572868
  69.9 56.2 %copy-start.1 = (bf16[256,256]{1,0:T(8,128)(2,1)S(1)}, bf16[256,256]{1,0:T(8,128)(2,1)}, u32[]{:S(2)}) copy-start(bf16[256,256]{1,0:T(8,128)(2,1)} %constant.9.clone.first) | copy-start | bytes 393220
  69.9 56.2 %copy-start.2 = (f32[2,64,128]{2,1,0:T(8,128)S(1)}, f32[2,64,128]{2,1,0:T(8,128)}, u32[]{:S(2)}) copy-start(f32[2,64,128]{2,1,0:T(8,128)} %constant.10.clone.twist) | copy-start | bytes 196612
